TPU v7x, 32 devices: a whole 2x2x4 slice. The times are simulated.
32 devices in a mesh: seg: 8 (over y, x, core), head: 4 (over z).
Axes of the slice: x: 2, y: 2, z: 4, core: 2. Of those that a mesh axis runs over, the one named last changes fastest.
Arguments:
- queries: bfloat16 [4096, 4096], P('seg', 'head'), may hold values from -6 to 6
- key_tokens: bfloat16 [4096, 4096], P('seg', 'head'), may hold values from -0.52734375 to 0.52734375
- values: bfloat16 [4096, 4096], P('seg', 'head'), may hold values from -6 to 6
- upstream: bfloat16 [4096, 4096], P('seg', 'head'), may hold values from -6 to 6
- norm_gain: float32 [4096], P('head'), may hold values from 0.1 to 1.9
- decay_rate: float32 [32], P('head'), may hold values from 1.2207031e-05 to 0.00390625
- block_length: int32 [8], replicated, may hold values from 1 to 512, 3072 in all
- parent: int32 [8], replicated, may hold values from -1 to 6, as said below
Outputs:
- attention_out: bfloat16 [4096, 4096], P('seg', 'head')
- query_grad: bfloat16 [4096, 4096], P('seg', 'head')
- key_grad: bfloat16 [4096, 4096], P('seg', 'head')
- value_grad: bfloat16 [4096, 4096], P('seg', 'head')
Inputs may be any that keep to these rules, and one draw needn't show every extreme that they name: parent[0] is -1; every other block's parent is -1 or an earlier block, and block 7 always continues block 6.
All inputs are finite; a program needn't handle non-finite values.
Results may differ from a plain program's by a relative error of at most 0.012.
Values sent between devices are 32-bit elements; how exact they have to be, the bound alone decides.
No kernel may reach another device: no remote copies, remote signals or barrier semaphores. Data moves between devices by JAX's collectives and lax.ppermute only.
A program may use at most 64 MiB of HBM per device.

v0:
```python
import functools

import jax
import jax.numpy as jnp
from jax import lax
from jax.experimental import pallas as pl
from jax.experimental.pallas import tpu as pltpu
from jax.sharding import PartitionSpec as P

norm_eps = 1e-05
f32 = jnp.float32
bf16 = jnp.bfloat16
VMEM_LIMIT = 40 * 1024 * 1024

SMEM_SPEC = pl.BlockSpec(memory_space=pltpu.SMEM)
VMEM_SPEC = pl.BlockSpec(memory_space=pltpu.VMEM)


def nn(a, b):
    return lax.dot_general(a, b, (((1,), (0,)), ((), ())), preferred_element_type=f32)


def nt(a, b):
    return lax.dot_general(a, b, (((1,), (1,)), ((), ())), preferred_element_type=f32)


def tn(a, b):
    return lax.dot_general(a, b, (((0,), (0,)), ((), ())), preferred_element_type=f32)


def row_index(rows, columns):
    return lax.broadcasted_iota(jnp.int32, (rows, columns), 0)


def key_scale(rows, size, length, rate):
    slot = row_index(rows, size)
    remaining = jnp.maximum(length - 1 - slot, 0).astype(f32)
    return jnp.where(slot < length, jnp.exp(-rate * remaining), 0.0)


def query_scale(rows, size, rate):
    return jnp.exp(-rate * (row_index(rows, size) + 1).astype(f32))


def masked_rows(array, length):
    return jnp.where(row_index(*array.shape) < length, array, jnp.zeros_like(array))


def column(row):
    count = row.shape[1]
    return jnp.broadcast_to(row, (count, count)).T


def write_pieces(whole, outs, chip):
    piece = outs[0].shape[0]
    for offset, out in enumerate(outs):
        at = pl.multiple_of((chip ^ offset) * piece, piece)
        out[...] = whole[pl.ds(at, piece), :]


def read_pieces(pieces, whole, chip):
    piece = pieces[0].shape[0]
    for offset, part in enumerate(pieces):
        at = pl.multiple_of((chip ^ offset) * piece, piece)
        whole[pl.ds(at, piece), :] = part[...]


def state_kernel(chips, length_ref, rate_ref, key_ref, value_ref, *rest):
    outs, whole = rest[:chips], rest[chips]
    own = lax.axis_index("seg")
    step = pl.program_id(0)
    rows, wide = key_ref.shape
    size = whole.shape[1]
    length = length_ref[own]
    here = wide // size
    scaled = []
    for at in range(here):
        scale = key_scale(rows, size, length, rate_ref[step * here + at])
        part = value_ref[:, at * size:(at + 1) * size].astype(f32) * scale
        scaled.append(part.astype(bf16))
    both = tn(key_ref[...], jnp.concatenate(scaled, axis=1))
    for at in range(here):
        span = slice(at * size, (at + 1) * size)
        begin = pl.multiple_of(step * wide + at * size, size)
        whole[pl.ds(begin, size), :] = both[span, span]

    @pl.when(step == pl.num_programs(0) - 1)
    def finish():
        write_pieces(whole, outs, own // 2)


def decay_tile(tile, rate, distance, transposed):
    u = lax.broadcasted_iota(jnp.int32, (tile, tile), 1 if transposed else 0)
    w = lax.broadcasted_iota(jnp.int32, (tile, tile), 0 if transposed else 1)
    spacing = u - w + distance
    decay = jnp.exp(-rate * jnp.maximum(spacing, 0).astype(f32))
    return jnp.where(spacing >= 0, decay, 0.0) if distance < tile else decay


def local_kernel(size, tile, length_ref, rate_ref, query_ref, key_ref, value_ref, out_ref):
    own = lax.axis_index("seg")
    step = pl.program_id(0)
    rows, wide = query_ref.shape
    here = wide // size
    length = length_ref[own]
    count = rows // tile
    for at in range(here):
        span = slice(at * size, (at + 1) * size)
        rate = rate_ref[step * here + at]
        query = masked_rows(query_ref[:, span], length)
        decays = [decay_tile(tile, rate, tile * gap, False) for gap in range(count)]
        for i in range(count):
            total = None
            for j in range(i + 1):
                w_span = slice(j * tile, (j + 1) * tile)
                scores = nt(query[i * tile:(i + 1) * tile], key_ref[w_span, span])
                weighted = (scores * decays[i - j]).astype(bf16)
                part = nn(weighted, value_ref[w_span, span])
                total = part if total is None else total + part
            out_ref[i * tile:(i + 1) * tile, span] = total


def tree_distances(length_ref, parent_ref, table, count):
    def clear(at, carry):
        table[at] = jnp.int32(-1)
        return carry

    lax.fori_loop(0, count * count, clear, 0)

    def one(block, carry):
        def up(at):
            node, distance = at
            table[block * count + node] = distance
            return parent_ref[node], distance + length_ref[node]

        lax.while_loop(lambda at: at[0] >= 0, up, (parent_ref[block], jnp.int32(0)))
        return carry

    lax.fori_loop(0, count, one, 0)


def mix_kernel(chips, size, backward, length_ref, parent_ref, rate_ref, *rest):
    mine, other, outs, table = rest[:chips], rest[chips:2 * chips], rest[2 * chips:3 * chips], rest[3 * chips]
    own = lax.axis_index("seg")
    chip, core = own // 2, own % 2
    count = 2 * chips
    tree_distances(length_ref, parent_ref, table, count)
    piece = mine[0].shape[0]
    part = min(piece, size)
    for at in range(piece // part):
        head = (chip * piece + at * part) // size
        rate = rate_ref[head]
        span = slice(at * part, (at + 1) * part)
        totals = [jnp.zeros((part, size), f32) for _ in range(chips)]
        for offset in range(chips):
            for sibling, sources in ((0, mine), (1, other)):
                source = (chip ^ offset) * 2 + (core ^ sibling)
                data = sources[offset][span, :]
                for target in range(chips):
                    wanted = (chip ^ target) * 2 + core
                    place = source * count + wanted if backward else wanted * count + source
                    distance = table[place]
                    level = jnp.full((8, size), -rate * distance.astype(f32), f32)
                    weight = jnp.exp(level) * (distance >= 0).astype(f32)
                    weight = jnp.concatenate([weight] * (part // 8), axis=0)
                    totals[target] = totals[target] + weight * data
        for target in range(chips):
            outs[target][span, :] = totals[target]


def attend_kernel(chips, length_ref, rate_ref, query_ref, upstream_ref, local_ref, gain_ref, *rest):
    pieces, attended_ref, sums_ref, whole = rest[:chips], rest[chips], rest[chips + 1], rest[chips + 2]
    own = lax.axis_index("seg")
    rows, wide = query_ref.shape
    size = whole.shape[1]
    length = length_ref[own]
    read_pieces(pieces, whole, own // 2)
    squares = jnp.zeros((rows, size), f32)
    inners = jnp.zeros((rows, size), f32)
    for head in range(wide // size):
        span = slice(head * size, (head + 1) * size)
        query = masked_rows(query_ref[:, span], length)
        carried = whole[span, :].astype(bf16)
        scale = query_scale(rows, size, rate_ref[head])
        attended = local_ref[:, span] + scale * nn(query, carried)
        attended_ref[:, span] = attended
        scaled = upstream_ref[:, span].astype(f32) * gain_ref[:, span]
        squares = squares + attended * attended
        inners = inners + scaled * attended
    groups = rows // size
    for at in range(groups):
        span = slice(at * size, (at + 1) * size)
        sums_ref[at:at + 1, :] = jnp.sum(squares[span].T, axis=0, keepdims=True)
        sums_ref[groups + at:groups + at + 1, :] = jnp.sum(inners[span].T, axis=0, keepdims=True)


def norm_columns(sum_refs, width, inverse_ref, factor_ref):
    total = sum_refs[0][...]
    for ref in sum_refs[1:]:
        total = total + ref[...]
    groups = total.shape[0] // 2
    size = total.shape[1]
    inverse = lax.rsqrt(total[:groups] / width + norm_eps)
    factor = inverse * inverse * inverse * total[groups:] / width
    for at in range(groups):
        span = slice(at * size, (at + 1) * size)
        inverse_ref[span, :] = column(inverse[at:at + 1])
        factor_ref[span, :] = column(factor[at:at + 1])


def state_grad_kernel(chips, sums, width, length_ref, rate_ref, query_ref, upstream_ref, attended_ref, gain_ref, *rest):
    sum_refs, outs = rest[:sums], rest[sums:sums + chips]
    inverse_ref, factor_ref, whole = rest[sums + chips:]
    own = lax.axis_index("seg")
    rows, wide = query_ref.shape
    size = whole.shape[1]
    length = length_ref[own]
    norm_columns(sum_refs, width, inverse_ref, factor_ref)
    inverse = inverse_ref[...]
    factor = factor_ref[...]
    heads = wide // size
    group = min(2, heads)
    for first in range(0, heads, group):
        parts = []
        for head in range(first, first + group):
            span = slice(head * size, (head + 1) * size)
            scaled = upstream_ref[:, span].astype(f32) * gain_ref[:, span]
            grad = inverse * scaled - factor * attended_ref[:, span]
            parts.append((grad * query_scale(rows, size, rate_ref[head])).astype(bf16))
        span = slice(first * size, (first + group) * size)
        query = masked_rows(query_ref[:, span], length)
        both = tn(query, jnp.concatenate(parts, axis=1))
        for at in range(group):
            inner = slice(at * size, (at + 1) * size)
            whole[(first + at) * size:(first + at + 1) * size, :] = both[inner, inner]
    write_pieces(whole, outs, own // 2)


def backward_kernel(chips, sums, width, tile, first, filled, length_ref, rate_ref, query_ref, key_ref, value_ref, upstream_ref, attended_ref, gain_ref, *rest):
    sum_refs, pieces = rest[:sums], rest[sums:sums + chips]
    outs = rest[sums + chips + filled:]
    out_ref, query_grad_ref, key_grad_ref, value_grad_ref, inverse_ref, factor_ref, whole = outs
    own = lax.axis_index("seg")
    step = pl.program_id(0)
    rows, wide = query_ref.shape
    size = whole.shape[1]
    here = wide // size
    length = length_ref[own]
    count = rows // tile

    @pl.when(step == 0)
    def begin():
        norm_columns(sum_refs, width, inverse_ref, factor_ref)
        read_pieces(pieces, whole, own // 2)

    for at in range(here):
        span = slice(at * size, (at + 1) * size)
        head = (first + step) * here + at
        rate = rate_ref[head]
        query = masked_rows(query_ref[:, span], length)
        key = key_ref[:, span]
        value = value_ref[:, span]
        gain = gain_ref[:, span]
        inverse = inverse_ref[...]
        attended = attended_ref[:, span]
        out_ref[:, span] = (attended * inverse * gain).astype(bf16)
        scaled = upstream_ref[:, span].astype(f32) * gain
        grad = (inverse * scaled - factor_ref[...] * attended).astype(bf16)
        carried = whole[pl.ds(pl.multiple_of(head * size, size), size), :].astype(bf16)
        query_grad = nt(grad, carried) * query_scale(rows, size, rate)
        decays = [decay_tile(tile, rate, tile * gap, True) for gap in range(count)]
        local_query = [None] * count
        for j in range(count):
            w_span = slice(j * tile, (j + 1) * tile)
            key_total = value_total = None
            for i in range(j, count):
                u_span = slice(i * tile, (i + 1) * tile)
                decay = decays[i - j]
                weighted = (nt(key[w_span], query[u_span]) * decay).astype(bf16)
                weighted_grad = nt(value[w_span], grad[u_span]).astype(bf16).astype(f32)
                score_grad = (weighted_grad * decay).astype(bf16)
                value_part = nn(weighted, grad[u_span])
                key_part = nn(score_grad, query[u_span])
                query_part = tn(score_grad, key[w_span])
                value_total = value_part if value_total is None else value_total + value_part
                key_total = key_part if key_total is None else key_total + key_part
                local_query[i] = query_part if local_query[i] is None else local_query[i] + query_part
            key_grad_ref[w_span, span] = key_total.astype(bf16)
            value_grad_ref[w_span, span] = value_total.astype(bf16)
        query_grad = query_grad + jnp.concatenate(local_query, axis=0)
        query_grad_ref[:, span] = masked_rows(query_grad, length).astype(bf16)


def finish_kernel(chips, length_ref, rate_ref, key_ref, value_ref, key_local_ref, value_local_ref, *rest):
    pieces, key_grad_ref, value_grad_ref, whole = rest[:chips], rest[chips], rest[chips + 1], rest[chips + 2]
    own = lax.axis_index("seg")
    rows, wide = key_ref.shape
    size = whole.shape[1]
    length = length_ref[own]
    read_pieces(pieces, whole, own // 2)
    for head in range(wide // size):
        span = slice(head * size, (head + 1) * size)
        scale = key_scale(rows, size, length, rate_ref[head])
        state_grad = whole[span, :].astype(bf16)
        key_part = scale * nt(value_ref[:, span], state_grad)
        value_part = scale * nn(key_ref[:, span], state_grad)
        key_grad_ref[:, span] = (key_local_ref[:, span].astype(f32) + key_part).astype(bf16)
        value_grad_ref[:, span] = (value_local_ref[:, span].astype(f32) + value_part).astype(bf16)


def params():
    return pltpu.CompilerParams(vmem_limit_bytes=VMEM_LIMIT)


def shape(dims, dtype):
    return jax.ShapeDtypeStruct(dims, dtype)


def exchange(pieces, count):
    moved = [pieces[0]]
    for offset in range(1, len(pieces)):
        pairs = [(at, at ^ (2 * offset)) for at in range(count)]
        moved.append(lax.ppermute(pieces[offset], "seg", pairs))
    return moved


def swap_cores(pieces, count):
    pairs = [(at, at ^ 1) for at in range(count)]
    return [lax.ppermute(piece, "seg", pairs) for piece in pieces]


def head_sums(sums, count):
    if count <= 4:
        return [sums] + [lax.ppermute(sums, "head", [(at, at ^ step) for at in range(count)]) for step in range(1, count)]
    step = 1
    while step < count:
        sums = sums + lax.ppermute(sums, "head", [(at, at ^ step) for at in range(count)])
        step *= 2
    return [sums]


def local(seg_count, head_count, queries, key_tokens, values, upstream, norm_gain, decay_rate, block_length, parent):
    rows, wide = queries.shape
    heads = decay_rate.shape[0]
    size = wide // heads
    width = wide * head_count
    chips = seg_count // 2
    piece = wide // chips
    group = min(2, heads) * size
    steps = wide // group
    tile = min(256, rows)
    gain = norm_gain[None, :]
    piece_shapes = [shape((piece, size), f32)] * chips
    piece_specs = [VMEM_SPEC] * chips
    whole = pltpu.VMEM((wide, size), f32)

    def column_spec(first=0):
        return pl.BlockSpec((rows, group), lambda step: (0, first + step))

    states = pl.pallas_call(
        functools.partial(state_kernel, chips),
        grid=(steps,),
        out_shape=piece_shapes,
        in_specs=[SMEM_SPEC] * 2 + [column_spec()] * 2,
        out_specs=[pl.BlockSpec((piece, size), lambda step: (0, 0))] * chips,
        scratch_shapes=[whole],
        compiler_params=params(),
        name="block_state",
    )(block_length, decay_rate, key_tokens, values)

    local_out = pl.pallas_call(
        functools.partial(local_kernel, size, tile),
        grid=(steps,),
        out_shape=shape((rows, wide), f32),
        in_specs=[SMEM_SPEC] * 2 + [column_spec()] * 3,
        out_specs=column_spec(),
        compiler_params=params(),
        cost_estimate=pl.CostEstimate(flops=3 * rows * rows * wide, bytes_accessed=10 * rows * wide, transcendentals=rows * rows * heads),
        name="local_attention",
    )(block_length, decay_rate, queries, key_tokens, values)

    def mix(pieces, backward):
        mine = exchange(pieces, seg_count)
        other = swap_cores(mine, seg_count)
        mixed = pl.pallas_call(
            functools.partial(mix_kernel, chips, size, backward),
            out_shape=piece_shapes,
            in_specs=[SMEM_SPEC] * 3 + piece_specs * 2,
            out_specs=piece_specs,
            scratch_shapes=[pltpu.SMEM((seg_count * seg_count,), jnp.int32)],
            compiler_params=params(),
            name="mix_backward" if backward else "mix_forward",
        )(block_length, parent, decay_rate, *mine, *other)
        return exchange(mixed, seg_count)

    carried = mix(states, False)

    attended, sums = pl.pallas_call(
        functools.partial(attend_kernel, chips),
        out_shape=[shape((rows, wide), f32), shape((2 * rows // size, size), f32)],
        in_specs=[SMEM_SPEC] * 2 + [VMEM_SPEC] * (4 + chips),
        out_specs=[VMEM_SPEC] * 2,
        scratch_shapes=[whole],
        compiler_params=params(),
        name="attend",
    )(block_length, decay_rate, queries, upstream, local_out, gain, *carried)

    sum_parts = head_sums(sums, head_count)
    columns = pltpu.VMEM((rows, size), f32)

    state_grads = pl.pallas_call(
        functools.partial(state_grad_kernel, chips, len(sum_parts), width),
        out_shape=piece_shapes,
        in_specs=[SMEM_SPEC] * 2 + [VMEM_SPEC] * (4 + len(sum_parts)),
        out_specs=piece_specs,
        scratch_shapes=[columns, columns, whole],
        compiler_params=params(),
        name="state_grad",
    )(block_length, decay_rate, queries, upstream, attended, gain, *sum_parts)

    def backward(first, amount, filled):
        names = len(sum_parts) + chips
        gain_spec = pl.BlockSpec((1, group), lambda step: (0, first + step))
        at = 2 + 6 + names
        return pl.pallas_call(
            functools.partial(backward_kernel, chips, len(sum_parts), width, tile, first, len(filled)),
            grid=(amount,),
            out_shape=[shape((rows, wide), bf16)] * 4,
            in_specs=[SMEM_SPEC] * 2
            + [column_spec(first)] * 5
            + [gain_spec]
            + [VMEM_SPEC] * names
            + [pl.BlockSpec(memory_space=pl.ANY)] * len(filled),
            out_specs=[column_spec(first)] * 4,
            scratch_shapes=[columns, columns, whole],
            input_output_aliases={at + i: i for i in range(len(filled))},
            compiler_params=params(),
            cost_estimate=pl.CostEstimate(
                flops=8 * rows * rows * group * amount, bytes_accessed=16 * rows * group * amount, transcendentals=rows * rows * amount
            ),
            name="local_backward",
        )(block_length, decay_rate, queries, key_tokens, values, upstream, attended, gain, *sum_parts, *carried, *filled)

    half = steps // 2
    grads = backward(0, steps - half, [])
    if half:
        grads = backward(steps - half, half, grads)
    attention_out, query_grad, key_local, value_local = grads

    state_sums = mix(state_grads, True)

    key_grad, value_grad = pl.pallas_call(
        functools.partial(finish_kernel, chips),
        out_shape=[shape((rows, wide), bf16)] * 2,
        in_specs=[SMEM_SPEC] * 2 + [VMEM_SPEC] * (4 + chips),
        out_specs=[VMEM_SPEC] * 2,
        scratch_shapes=[whole],
        compiler_params=params(),
        name="finish",
    )(block_length, decay_rate, key_tokens, values, key_local, value_local, *state_sums)
    return attention_out, query_grad, key_grad, value_grad


def solution(mesh):
    sizes = dict(mesh.shape)
    tokens = P("seg", "head")
    return jax.shard_map(
        functools.partial(local, sizes["seg"], sizes["head"]),
        mesh=mesh,
        in_specs=(tokens, tokens, tokens, tokens, P("head"), P("head"), P(), P()),
        out_specs=(tokens, tokens, tokens, tokens),
        check_vma=False,
    )
```

profile of v0, /device:TPU:0, one launch (start us, length us, event | category | flops | bytes accessed | tf_op | source)
XLA Modules:
  0.0 74.1 jit_solution(9658677380737438766)
XLA Ops:
  0.6 0.0 copy-start
  0.6 1.2 %copy-done = bf16[512,1024]{1,0:T(8,128)(2,1)S(1)} copy-done((bf16[512,1024]{1,0:T(8,128)(2,1)S(1)}, bf16[512,1024]{1,0:T(8,128)(2,1)}, u32[]{:S(2)}) %copy-start) | copy-done | bytes 1048600
  1.9 1.2 %copy-done.2 = bf16[512,1024]{1,0:T(8,128)(2,1)S(1)} copy-done((bf16[512,1024]{1,0:T(8,128)(2,1)S(1)}, bf16[512,1024]{1,0:T(8,128)(2,1)}, u32[]{:S(2)}) %copy-start.2) | copy-done | bytes 1048600
  3.1 0.7 copy-done.7
  3.7 0.7 copy-done.8
  4.4 2.4 %block_state.1 = (f32[256,128]{1,0:T(8,128)S(1)}, f32[256,128]{1,0:T(8,128)S(1)}, f32[256,128]{1,0:T(8,128)S(1)}, f32[256,128]{1,0:T(8,128)S(1)}) custom-call(s32[8]{0:T(128)S(1)} %copy-done.7, f32[8]{0:T(128)S(1)} %copy-done.8, bf16[512,1024]{1,0:T(8,128)(2,1)S(1)} %copy-done, bf16[512,1024]{1,0:T(8,128)(2,1)S(1)} %copy-done.2), custom_call_target="tpu_custom_call" | custom-call | tf_op jit(solution)/shard_map/block_state/pallas_call | solution.py:360
  6.8 3.0 %collective-permute-start = (f32[256,128]{1,0:T(8,128)S(1)}, f32[256,128]{1,0:T(8,128)S(1)}, u32[]{:S(2)}, u32[]{:S(2)}) collective-permute-start(f32[256,128]{1,0:T(8,128)S(1)} %get-tuple-element.33), channel_id=1, source_target_pairs={{0,8},{4,12},{8,0},{12,4},{16,24},{20,28},{24,16},{28,20},{1,9},{5... | collective-permute-start | bytes 393224 | tf_op jit(solution)/shard_map/ppermute | solution.py:323
  9.8 1.5 %collective-permute-start.1 = (f32[256,128]{1,0:T(8,128)S(1)}, f32[256,128]{1,0:T(8,128)S(1)}, u32[]{:S(2)}, u32[]{:S(2)}) collective-permute-start(f32[256,128]{1,0:T(8,128)S(1)} %get-tuple-element.34), channel_id=1, source_target_pairs={{0,16},{4,20},{8,24},{12,28},{16,0},{20,4},{24,8},{28,12},{1,17},{... | collective-permute-start | bytes 393224 | tf_op jit(solution)/shard_map/ppermute | solution.py:323
  11.3 0.0 collective-permute-start.2
  11.3 0.0 collective-permute-start.3
  11.3 2.4 %collective-permute-done.rest_1_ = f32[256,128]{1,0:T(8,128)S(1)} collective-permute-done((f32[256,128]{1,0:T(8,128)S(1)}, f32[256,128]{1,0:T(8,128)S(1)}, u32[]{:S(2)}, u32[]{:S(2)}) %collective-permute-start) | collective-permute-done | bytes 131104 | tf_op jit(solution)/shard_map/ppermute | solution.py:323
  13.7 0.0 collective-permute-start.4
  13.7 3.9 %collective-permute-done.1.rest_2_ = f32[256,128]{1,0:T(8,128)S(1)} collective-permute-done((f32[256,128]{1,0:T(8,128)S(1)}, f32[256,128]{1,0:T(8,128)S(1)}, u32[]{:S(2)}, u32[]{:S(2)}) %collective-permute-start.1) | collective-permute-done | bytes 131104 | tf_op jit(solution)/shard_map/ppermute | solution.py:323
  17.6 0.0 collective-permute-start.5
  17.6 0.0 collective-permute-done.2.rest_3_
  17.6 0.5 collective-permute-start.6
  18.1 0.0 collective-permute-done.3.rest_4_
  18.1 0.0 collective-permute-done.4.rest_5_
  18.1 0.8 %collective-permute-done.5.rest_6_ = f32[256,128]{1,0:T(8,128)S(1)} collective-permute-done((f32[256,128]{1,0:T(8,128)S(1)}, f32[256,128]{1,0:T(8,128)S(1)}, u32[]{:S(2)}, u32[]{:S(2)}) %collective-permute-start.5) | collective-permute-done | bytes 131104 | tf_op jit(solution)/shard_map/ppermute | solution.py:329
  18.9 0.2 collective-permute-done.6.rest_7_
  19.1 0.7 copy-done.9
  19.8 1.6 %mix_forward.1 = (f32[256,128]{1,0:T(8,128)S(1)}, f32[256,128]{1,0:T(8,128)S(1)}, f32[256,128]{1,0:T(8,128)S(1)}, f32[256,128]{1,0:T(8,128)S(1)}) custom-call(s32[8]{0:T(128)S(1)} %copy-done.7, s32[8]{0:T(128)S(1)} %copy-done.9, f32[8]{0:T(128)S(1)} %copy-done.8, f32[256,128]{1,0:T(8,128)S(1)} %get-tuple-element.32.rest_0_, ...), custom_call_target="tpu_custom_call" | custom-call | tf_op jit(solution)/shard_map/mix_forward/pallas_call | solution.py:385
  21.4 1.1 %collective-permute-start.7 = (f32[256,128]{1,0:T(8,128)S(1)}, f32[256,128]{1,0:T(8,128)S(1)}, u32[]{:S(2)}, u32[]{:S(2)}) collective-permute-start(f32[256,128]{1,0:T(8,128)S(1)} %get-tuple-element.37), channel_id=1, source_target_pairs={{0,8},{4,12},{8,0},{12,4},{16,24},{20,28},{24,16},{28,20},{1,9},{5... | collective-permute-start | bytes 393224 | tf_op jit(solution)/shard_map/ppermute | solution.py:323
  22.5 1.0 %collective-permute-start.8 = (f32[256,128]{1,0:T(8,128)S(1)}, f32[256,128]{1,0:T(8,128)S(1)}, u32[]{:S(2)}, u32[]{:S(2)}) collective-permute-start(f32[256,128]{1,0:T(8,128)S(1)} %get-tuple-element.38), channel_id=1, source_target_pairs={{0,16},{4,20},{8,24},{12,28},{16,0},{20,4},{24,8},{28,12},{1,17},{... | collective-permute-start | bytes 393224 | tf_op jit(solution)/shard_map/ppermute | solution.py:323
  23.5 1.4 %collective-permute-start.9 = (f32[256,128]{1,0:T(8,128)S(1)}, f32[256,128]{1,0:T(8,128)S(1)}, u32[]{:S(2)}, u32[]{:S(2)}) collective-permute-start(f32[256,128]{1,0:T(8,128)S(1)} %get-tuple-element.39), channel_id=1, source_target_pairs={{0,24},{4,28},{8,16},{12,20},{16,8},{20,12},{24,0},{28,4},{1,25},{... | collective-permute-start | bytes 393224 | tf_op jit(solution)/shard_map/ppermute | solution.py:323
  25.0 0.0 copy-done.1
  25.0 0.0 copy-done.4
  25.0 4.6 %local_attention.1.local_ref = f32[512,1024]{1,0:T(8,128)S(1)} custom-call(s32[8]{0:T(128)S(1)} %copy-done.7, f32[8]{0:T(128)S(1)} %copy-done.8, bf16[512,1024]{1,0:T(8,128)(2,1)S(1)} %copy-done.4, bf16[512,1024]{1,0:T(8,128)(2,1)S(1)} %copy-done.1, bf16[512,1024]{1,0:T(8,128)(2,1)S(1)} %copy-done.3), custom_call_target="tpu_custom_call" | custom-call | flops 805306368 | bytes 5242880 | tf_op jit(solution)/shard_map/local_attention/pallas_call | solution.py:371
  29.5 0.0 collective-permute-done.7.rest_1_.rest_5_
  29.6 0.0 collective-permute-done.8.rest_2_.rest_6_
  29.6 1.4 %collective-permute-done.9.rest_3_.rest_7_ = f32[256,128]{1,0:T(8,128)S(1)} collective-permute-done((f32[256,128]{1,0:T(8,128)S(1)}, f32[256,128]{1,0:T(8,128)S(1)}, u32[]{:S(2)}, u32[]{:S(2)}) %collective-permute-start.9) | collective-permute-done | bytes 131104 | tf_op jit(solution)/shard_map/ppermute | solution.py:323
  31.0 1.8 %attend.1 = (f32[512,1024]{1,0:T(8,128)S(1)}, f32[8,128]{1,0:T(8,128)S(1)}) custom-call(s32[8]{0:T(128)S(1)} %copy-done.7, f32[8]{0:T(128)S(1)} %copy-done.8, bf16[512,1024]{1,0:T(8,128)(2,1)S(1)} %copy-done.4, bf16[512,1024]{1,0:T(8,128)(2,1)S(1)} %copy-done.5, f32[512,1024]{1,0:T(8,128)S(1)} %local_attention.1.local_ref, f32[1,1024]{1,0:T(1,128)S(1)} %bitcast.1, ...), custom_call_target="tpu_custom_call" | custom-call | tf_op jit(solution)/shard_map/attend/pallas_call | solution.py:398
  32.8 1.6 %collective-permute-start.10 = (f32[8,128]{1,0:T(8,128)S(1)}, f32[8,128]{1,0:T(8,128)S(1)}, u32[]{:S(2)}, u32[]{:S(2)}) collective-permute-start(f32[8,128]{1,0:T(8,128)S(1)} %get-tuple-element.41.rest_0_), channel_id=1, source_target_pairs={{0,1},{1,0},{2,3},{3,2},{4,5},{5,4},{6,7},{7,6},{8,9},{9,8},{10,11... | collective-permute-start | bytes 12296 | tf_op jit(solution)/shard_map/ppermute | solution.py:334
  34.4 2.6 %collective-permute-start.11 = (f32[8,128]{1,0:T(8,128)S(1)}, f32[8,128]{1,0:T(8,128)S(1)}, u32[]{:S(2)}, u32[]{:S(2)}) collective-permute-start(f32[8,128]{1,0:T(8,128)S(1)} %get-tuple-element.41.rest_0_), channel_id=1, source_target_pairs={{0,2},{1,3},{2,0},{3,1},{4,6},{5,7},{6,4},{7,5},{8,10},{9,11},{10,... | collective-permute-start | bytes 12296 | tf_op jit(solution)/shard_map/ppermute | solution.py:334
  37.0 0.2 collective-permute-start.12
  37.2 0.0 collective-permute-done.10.rest_1_
  37.2 1.7 %collective-permute-done.11.rest_2_ = f32[8,128]{1,0:T(8,128)S(1)} collective-permute-done((f32[8,128]{1,0:T(8,128)S(1)}, f32[8,128]{1,0:T(8,128)S(1)}, u32[]{:S(2)}, u32[]{:S(2)}) %collective-permute-start.11) | collective-permute-done | bytes 4128 | tf_op jit(solution)/shard_map/ppermute | solution.py:334
  38.9 3.5 %collective-permute-done.12.rest_3_ = f32[8,128]{1,0:T(8,128)S(1)} collective-permute-done((f32[8,128]{1,0:T(8,128)S(1)}, f32[8,128]{1,0:T(8,128)S(1)}, u32[]{:S(2)}, u32[]{:S(2)}) %collective-permute-start.12) | collective-permute-done | bytes 4128 | tf_op jit(solution)/shard_map/ppermute | solution.py:334
  42.4 1.8 %state_grad.1 = (f32[256,128]{1,0:T(8,128)S(1)}, f32[256,128]{1,0:T(8,128)S(1)}, f32[256,128]{1,0:T(8,128)S(1)}, f32[256,128]{1,0:T(8,128)S(1)}) custom-call(s32[8]{0:T(128)S(1)} %copy-done.7, f32[8]{0:T(128)S(1)} %copy-done.8, bf16[512,1024]{1,0:T(8,128)(2,1)S(1)} %copy-done.4, bf16[512,1024]{1,0:T(8,128)(2,1)S(1)} %copy-done.5, ...), custom_call_target="tpu_custom_call" | custom-call | tf_op jit(solution)/shard_map/state_grad/pallas_call | solution.py:411
  44.2 0.9 %collective-permute-start.13 = (f32[256,128]{1,0:T(8,128)S(1)}, f32[256,128]{1,0:T(8,128)S(1)}, u32[]{:S(2)}, u32[]{:S(2)}) collective-permute-start(f32[256,128]{1,0:T(8,128)S(1)} %get-tuple-element.51), channel_id=1, source_target_pairs={{0,8},{4,12},{8,0},{12,4},{16,24},{20,28},{24,16},{28,20},{1,9},{5... | collective-permute-start | bytes 393224 | tf_op jit(solution)/shard_map/ppermute | solution.py:323
  45.1 1.5 %collective-permute-start.14 = (f32[256,128]{1,0:T(8,128)S(1)}, f32[256,128]{1,0:T(8,128)S(1)}, u32[]{:S(2)}, u32[]{:S(2)}) collective-permute-start(f32[256,128]{1,0:T(8,128)S(1)} %get-tuple-element.52), channel_id=1, source_target_pairs={{0,16},{4,20},{8,24},{12,28},{16,0},{20,4},{24,8},{28,12},{1,17},{... | collective-permute-start | bytes 393224 | tf_op jit(solution)/shard_map/ppermute | solution.py:323
  46.6 1.2 %collective-permute-start.15 = (f32[256,128]{1,0:T(8,128)S(1)}, f32[256,128]{1,0:T(8,128)S(1)}, u32[]{:S(2)}, u32[]{:S(2)}) collective-permute-start(f32[256,128]{1,0:T(8,128)S(1)} %get-tuple-element.53), channel_id=1, source_target_pairs={{0,24},{4,28},{8,16},{12,20},{16,8},{20,12},{24,0},{28,4},{1,25},{... | collective-permute-start | bytes 393224 | tf_op jit(solution)/shard_map/ppermute | solution.py:323
  47.8 0.0 collective-permute-start.16
  47.8 1.5 %collective-permute-done.13.rest_1_ = f32[256,128]{1,0:T(8,128)S(1)} collective-permute-done((f32[256,128]{1,0:T(8,128)S(1)}, f32[256,128]{1,0:T(8,128)S(1)}, u32[]{:S(2)}, u32[]{:S(2)}) %collective-permute-start.13) | collective-permute-done | bytes 131104 | tf_op jit(solution)/shard_map/ppermute | solution.py:323
  49.2 0.0 collective-permute-start.17
  49.2 0.8 %collective-permute-done.14.rest_2_ = f32[256,128]{1,0:T(8,128)S(1)} collective-permute-done((f32[256,128]{1,0:T(8,128)S(1)}, f32[256,128]{1,0:T(8,128)S(1)}, u32[]{:S(2)}, u32[]{:S(2)}) %collective-permute-start.14) | collective-permute-done | bytes 131104 | tf_op jit(solution)/shard_map/ppermute | solution.py:323
  50.0 0.0 collective-permute-start.18
  50.0 2.4 %collective-permute-done.15.rest_3_ = f32[256,128]{1,0:T(8,128)S(1)} collective-permute-done((f32[256,128]{1,0:T(8,128)S(1)}, f32[256,128]{1,0:T(8,128)S(1)}, u32[]{:S(2)}, u32[]{:S(2)}) %collective-permute-start.15) | collective-permute-done | bytes 131104 | tf_op jit(solution)/shard_map/ppermute | solution.py:323
  52.5 0.0 collective-permute-start.19
  52.5 0.0 collective-permute-done.16.rest_4_
  52.5 0.0 collective-permute-done.17.rest_5_
  52.5 0.0 collective-permute-done.18.rest_6_
  52.5 1.3 %collective-permute-done.19.rest_7_ = f32[256,128]{1,0:T(8,128)S(1)} collective-permute-done((f32[256,128]{1,0:T(8,128)S(1)}, f32[256,128]{1,0:T(8,128)S(1)}, u32[]{:S(2)}, u32[]{:S(2)}) %collective-permute-start.19) | collective-permute-done | bytes 131104 | tf_op jit(solution)/shard_map/ppermute | solution.py:329
  53.8 0.0 copy-done.10
  53.8 1.6 %mix_backward.1 = (f32[256,128]{1,0:T(8,128)S(1)}, f32[256,128]{1,0:T(8,128)S(1)}, f32[256,128]{1,0:T(8,128)S(1)}, f32[256,128]{1,0:T(8,128)S(1)}) custom-call(s32[8]{0:T(128)S(1)} %copy-done.7, s32[8]{0:T(128)S(1)} %copy-done.10, f32[8]{0:T(128)S(1)} %copy-done.8, f32[256,128]{1,0:T(8,128)S(1)} %get-tuple-element.50.rest_0_, ...), custom_call_target="tpu_custom_call" | custom-call | tf_op jit(solution)/shard_map/mix_backward/pallas_call | solution.py:385
  55.4 0.6 collective-permute-start.20
  56.0 1.2 %collective-permute-start.21 = (f32[256,128]{1,0:T(8,128)S(1)}, f32[256,128]{1,0:T(8,128)S(1)}, u32[]{:S(2)}, u32[]{:S(2)}) collective-permute-start(f32[256,128]{1,0:T(8,128)S(1)} %get-tuple-element.56), channel_id=1, source_target_pairs={{0,16},{4,20},{8,24},{12,28},{16,0},{20,4},{24,8},{28,12},{1,17},{... | collective-permute-start | bytes 393224 | tf_op jit(solution)/shard_map/ppermute | solution.py:323
  57.2 1.8 %collective-permute-start.22 = (f32[256,128]{1,0:T(8,128)S(1)}, f32[256,128]{1,0:T(8,128)S(1)}, u32[]{:S(2)}, u32[]{:S(2)}) collective-permute-start(f32[256,128]{1,0:T(8,128)S(1)} %get-tuple-element.57), channel_id=1, source_target_pairs={{0,24},{4,28},{8,16},{12,20},{16,8},{20,12},{24,0},{28,4},{1,25},{... | collective-permute-start | bytes 393224 | tf_op jit(solution)/shard_map/ppermute | solution.py:323
  59.0 5.9 %local_backward.2 = (bf16[512,1024]{1,0:T(8,128)(2,1)}, bf16[512,1024]{1,0:T(8,128)(2,1)}, bf16[512,1024]{1,0:T(8,128)(2,1)S(1)}, bf16[512,1024]{1,0:T(8,128)(2,1)S(1)}) custom-call(s32[8]{0:T(128)S(1)} %copy-done.7, f32[8]{0:T(128)S(1)} %copy-done.8, bf16[512,1024]{1,0:T(8,128)(2,1)S(1)} %copy-done.4, bf16[512,1024]{1,0:T(8,128)(2,1)S(1)} %copy-done.1, ...), custom_call_target="tpu_custom_call" | custom-call | flops 1073741824 | bytes 4194304 | tf_op jit(solution)/shard_map/local_backward/pallas_call | solution.py:425
  64.9 5.9 %local_backward.3 = (bf16[512,1024]{1,0:T(8,128)(2,1)}, bf16[512,1024]{1,0:T(8,128)(2,1)}, bf16[512,1024]{1,0:T(8,128)(2,1)S(1)}, bf16[512,1024]{1,0:T(8,128)(2,1)S(1)}) custom-call(s32[8]{0:T(128)S(1)} %copy-done.7, f32[8]{0:T(128)S(1)} %copy-done.8, ...), custom_call_target="tpu_custom_call", output_to_operand_aliasing={{0}: (16, {}), {1}: (17, {}), {2}: (18, {}), {3}: (19, {})} | custom-call | flops 1073741824 | bytes 4194304 | tf_op jit(solution)/shard_map/local_backward/pallas_call | solution.py:425
  70.8 0.0 collective-permute-done.20.rest_1_
  70.8 0.0 collective-permute-done.21.rest_2_
  70.8 0.0 collective-permute-done.22.rest_3_
  70.8 3.3 %finish.1 = (bf16[512,1024]{1,0:T(8,128)(2,1)}, bf16[512,1024]{1,0:T(8,128)(2,1)}) custom-call(s32[8]{0:T(128)S(1)} %copy-done.7, f32[8]{0:T(128)S(1)} %copy-done.8, bf16[512,1024]{1,0:T(8,128)(2,1)S(1)} %copy-done.1, bf16[512,1024]{1,0:T(8,128)(2,1)S(1)} %copy-done.3, bf16[512,1024]{1,0:T(8,128)(2,1)S(1)} %get-tuple-element.48.key_local_ref, ...), custom_call_target="tpu_custom_call" | custom-call | tf_op jit(solution)/shard_map/finish/pallas_call | solution.py:452
  (13 shorter events, 0.0 us)
Async XLA Ops:
  0.6 1.2 %copy-start = (bf16[512,1024]{1,0:T(8,128)(2,1)S(1)}, bf16[512,1024]{1,0:T(8,128)(2,1)}, u32[]{:S(2)}) copy-start(bf16[512,1024]{1,0:T(8,128)(2,1)} %key_ref.9) | copy-start | bytes 3145732
  1.9 1.2 %copy-start.2 = (bf16[512,1024]{1,0:T(8,128)(2,1)S(1)}, bf16[512,1024]{1,0:T(8,128)(2,1)}, u32[]{:S(2)}) copy-start(bf16[512,1024]{1,0:T(8,128)(2,1)} %value_ref.9) | copy-start | bytes 3145732
  3.1 0.7 copy-start.7
  3.7 0.7 copy-start.8
  4.4 20.6 %copy-start.1 = (bf16[512,1024]{1,0:T(8,128)(2,1)S(1)}, bf16[512,1024]{1,0:T(8,128)(2,1)}, u32[]{:S(2)}) copy-start(bf16[512,1024]{1,0:T(8,128)(2,1)} %key_ref.9) | copy-start | bytes 3145732
  4.4 20.6 %copy-start.3 = (bf16[512,1024]{1,0:T(8,128)(2,1)S(1)}, bf16[512,1024]{1,0:T(8,128)(2,1)}, u32[]{:S(2)}) copy-start(bf16[512,1024]{1,0:T(8,128)(2,1)} %value_ref.9) | copy-start | bytes 3145732
  4.4 20.6 %copy-start.4 = (bf16[512,1024]{1,0:T(8,128)(2,1)S(1)}, bf16[512,1024]{1,0:T(8,128)(2,1)}, u32[]{:S(2)}) copy-start(bf16[512,1024]{1,0:T(8,128)(2,1)} %query_ref.9) | copy-start | bytes 3145732
  6.8 6.9 %collective-permute-start = (f32[256,128]{1,0:T(8,128)S(1)}, f32[256,128]{1,0:T(8,128)S(1)}, u32[]{:S(2)}, u32[]{:S(2)}) collective-permute-start(f32[256,128]{1,0:T(8,128)S(1)} %get-tuple-element.33), channel_id=1, source_target_pairs={{0,8},{4,12},{8,0},{12,4},{16,24},{20,28},{24,16},{28,20},{1,9},{5... | collective-permute-start | bytes 393224 | tf_op jit(solution)/shard_map/ppermute | solution.py:323
  9.8 7.8 %collective-permute-start.1 = (f32[256,128]{1,0:T(8,128)S(1)}, f32[256,128]{1,0:T(8,128)S(1)}, u32[]{:S(2)}, u32[]{:S(2)}) collective-permute-start(f32[256,128]{1,0:T(8,128)S(1)} %get-tuple-element.34), channel_id=1, source_target_pairs={{0,16},{4,20},{8,24},{12,28},{16,0},{20,4},{24,8},{28,12},{1,17},{... | collective-permute-start | bytes 393224 | tf_op jit(solution)/shard_map/ppermute | solution.py:323
  11.3 6.3 %collective-permute-start.2 = (f32[256,128]{1,0:T(8,128)S(1)}, f32[256,128]{1,0:T(8,128)S(1)}, u32[]{:S(2)}, u32[]{:S(2)}) collective-permute-start(f32[256,128]{1,0:T(8,128)S(1)} %get-tuple-element.35), channel_id=1, source_target_pairs={{0,24},{4,28},{8,16},{12,20},{16,8},{20,12},{24,0},{28,4},{1,25},{... | collective-permute-start | bytes 393224 | tf_op jit(solution)/shard_map/ppermute | solution.py:323
  11.3 6.8 %collective-permute-start.3 = (f32[256,128]{1,0:T(8,128)S(1)}, f32[256,128]{1,0:T(8,128)S(1)}, u32[]{:S(2)}, u32[]{:S(2)}) collective-permute-start(f32[256,128]{1,0:T(8,128)S(1)} %get-tuple-element.32.rest_0_), channel_id=1, source_target_pairs={{0,4},{4,0},{8,12},{12,8},{16,20},{20,16},{24,28},{28,24},{1,5},{5... | collective-permute-start | bytes 393224 | tf_op jit(solution)/shard_map/ppermute | solution.py:329
  13.7 4.4 %collective-permute-start.4 = (f32[256,128]{1,0:T(8,128)S(1)}, f32[256,128]{1,0:T(8,128)S(1)}, u32[]{:S(2)}, u32[]{:S(2)}) collective-permute-start(f32[256,128]{1,0:T(8,128)S(1)} %collective-permute-done.rest_1_), channel_id=1, source_target_pairs={{0,4},{4,0},{8,12},{12,8},{16,20},{20,16},{24,28},{28,24},{1,5},{5... | collective-permute-start | bytes 393224 | tf_op jit(solution)/shard_map/ppermute | solution.py:329
  17.6 1.3 %collective-permute-start.5 = (f32[256,128]{1,0:T(8,128)S(1)}, f32[256,128]{1,0:T(8,128)S(1)}, u32[]{:S(2)}, u32[]{:S(2)}) collective-permute-start(f32[256,128]{1,0:T(8,128)S(1)} %collective-permute-done.1.rest_2_), channel_id=1, source_target_pairs={{0,4},{4,0},{8,12},{12,8},{16,20},{20,16},{24,28},{28,24},{1,5},{5... | collective-permute-start | bytes 393224 | tf_op jit(solution)/shard_map/ppermute | solution.py:329
  17.6 1.5 %collective-permute-start.6 = (f32[256,128]{1,0:T(8,128)S(1)}, f32[256,128]{1,0:T(8,128)S(1)}, u32[]{:S(2)}, u32[]{:S(2)}) collective-permute-start(f32[256,128]{1,0:T(8,128)S(1)} %collective-permute-done.2.rest_3_), channel_id=1, source_target_pairs={{0,4},{4,0},{8,12},{12,8},{16,20},{20,16},{24,28},{28,24},{1,5},{5... | collective-permute-start | bytes 393224 | tf_op jit(solution)/shard_map/ppermute | solution.py:329
  19.1 0.7 copy-start.9
  21.4 8.1 %collective-permute-start.7 = (f32[256,128]{1,0:T(8,128)S(1)}, f32[256,128]{1,0:T(8,128)S(1)}, u32[]{:S(2)}, u32[]{:S(2)}) collective-permute-start(f32[256,128]{1,0:T(8,128)S(1)} %get-tuple-element.37), channel_id=1, source_target_pairs={{0,8},{4,12},{8,0},{12,4},{16,24},{20,28},{24,16},{28,20},{1,9},{5... | collective-permute-start | bytes 393224 | tf_op jit(solution)/shard_map/ppermute | solution.py:323
  22.5 7.0 %collective-permute-start.8 = (f32[256,128]{1,0:T(8,128)S(1)}, f32[256,128]{1,0:T(8,128)S(1)}, u32[]{:S(2)}, u32[]{:S(2)}) collective-permute-start(f32[256,128]{1,0:T(8,128)S(1)} %get-tuple-element.38), channel_id=1, source_target_pairs={{0,16},{4,20},{8,24},{12,28},{16,0},{20,4},{24,8},{28,12},{1,17},{... | collective-permute-start | bytes 393224 | tf_op jit(solution)/shard_map/ppermute | solution.py:323
  23.5 7.4 %copy-start.5 = (bf16[512,1024]{1,0:T(8,128)(2,1)S(1)}, bf16[512,1024]{1,0:T(8,128)(2,1)}, u32[]{:S(2)}) copy-start(bf16[512,1024]{1,0:T(8,128)(2,1)} %upstream_ref.7) | copy-start | bytes 3145732
  23.5 7.4 %copy-start.6 = (f32[1024]{0:T(1024)S(1)}, f32[1024]{0:T(1024)}, u32[]{:S(2)}) copy-start(f32[1024]{0:T(1024)} %param.12) | copy-start | bytes 12292
  23.5 7.4 %collective-permute-start.9 = (f32[256,128]{1,0:T(8,128)S(1)}, f32[256,128]{1,0:T(8,128)S(1)}, u32[]{:S(2)}, u32[]{:S(2)}) collective-permute-start(f32[256,128]{1,0:T(8,128)S(1)} %get-tuple-element.39), channel_id=1, source_target_pairs={{0,24},{4,28},{8,16},{12,20},{16,8},{20,12},{24,0},{28,4},{1,25},{... | collective-permute-start | bytes 393224 | tf_op jit(solution)/shard_map/ppermute | solution.py:323
  32.8 4.5 %collective-permute-start.10 = (f32[8,128]{1,0:T(8,128)S(1)}, f32[8,128]{1,0:T(8,128)S(1)}, u32[]{:S(2)}, u32[]{:S(2)}) collective-permute-start(f32[8,128]{1,0:T(8,128)S(1)} %get-tuple-element.41.rest_0_), channel_id=1, source_target_pairs={{0,1},{1,0},{2,3},{3,2},{4,5},{5,4},{6,7},{7,6},{8,9},{9,8},{10,11... | collective-permute-start | bytes 12296 | tf_op jit(solution)/shard_map/ppermute | solution.py:334
  34.4 4.5 %collective-permute-start.11 = (f32[8,128]{1,0:T(8,128)S(1)}, f32[8,128]{1,0:T(8,128)S(1)}, u32[]{:S(2)}, u32[]{:S(2)}) collective-permute-start(f32[8,128]{1,0:T(8,128)S(1)} %get-tuple-element.41.rest_0_), channel_id=1, source_target_pairs={{0,2},{1,3},{2,0},{3,1},{4,6},{5,7},{6,4},{7,5},{8,10},{9,11},{10,... | collective-permute-start | bytes 12296 | tf_op jit(solution)/shard_map/ppermute | solution.py:334
  37.0 5.4 %collective-permute-start.12 = (f32[8,128]{1,0:T(8,128)S(1)}, f32[8,128]{1,0:T(8,128)S(1)}, u32[]{:S(2)}, u32[]{:S(2)}) collective-permute-start(f32[8,128]{1,0:T(8,128)S(1)} %get-tuple-element.41.rest_0_), channel_id=1, source_target_pairs={{0,3},{1,2},{2,1},{3,0},{4,7},{5,6},{6,5},{7,4},{8,11},{9,10},{10,... | collective-permute-start | bytes 12296 | tf_op jit(solution)/shard_map/ppermute | solution.py:334
  42.4 11.4 %copy-start.10 = (s32[8]{0:T(128)S(1)}, s32[8]{0:T(128)}, u32[]{:S(2)}) copy-start(s32[8]{0:T(128)} %parent_ref.3) | copy-start | bytes 100
  44.2 5.0 %collective-permute-start.13 = (f32[256,128]{1,0:T(8,128)S(1)}, f32[256,128]{1,0:T(8,128)S(1)}, u32[]{:S(2)}, u32[]{:S(2)}) collective-permute-start(f32[256,128]{1,0:T(8,128)S(1)} %get-tuple-element.51), channel_id=1, source_target_pairs={{0,8},{4,12},{8,0},{12,4},{16,24},{20,28},{24,16},{28,20},{1,9},{5... | collective-permute-start | bytes 393224 | tf_op jit(solution)/shard_map/ppermute | solution.py:323
  45.1 5.0 %collective-permute-start.14 = (f32[256,128]{1,0:T(8,128)S(1)}, f32[256,128]{1,0:T(8,128)S(1)}, u32[]{:S(2)}, u32[]{:S(2)}) collective-permute-start(f32[256,128]{1,0:T(8,128)S(1)} %get-tuple-element.52), channel_id=1, source_target_pairs={{0,16},{4,20},{8,24},{12,28},{16,0},{20,4},{24,8},{28,12},{1,17},{... | collective-permute-start | bytes 393224 | tf_op jit(solution)/shard_map/ppermute | solution.py:323
  46.6 5.9 %collective-permute-start.15 = (f32[256,128]{1,0:T(8,128)S(1)}, f32[256,128]{1,0:T(8,128)S(1)}, u32[]{:S(2)}, u32[]{:S(2)}) collective-permute-start(f32[256,128]{1,0:T(8,128)S(1)} %get-tuple-element.53), channel_id=1, source_target_pairs={{0,24},{4,28},{8,16},{12,20},{16,8},{20,12},{24,0},{28,4},{1,25},{... | collective-permute-start | bytes 393224 | tf_op jit(solution)/shard_map/ppermute | solution.py:323
  47.8 4.7 %collective-permute-start.16 = (f32[256,128]{1,0:T(8,128)S(1)}, f32[256,128]{1,0:T(8,128)S(1)}, u32[]{:S(2)}, u32[]{:S(2)}) collective-permute-start(f32[256,128]{1,0:T(8,128)S(1)} %get-tuple-element.50.rest_0_), channel_id=1, source_target_pairs={{0,4},{4,0},{8,12},{12,8},{16,20},{20,16},{24,28},{28,24},{1,5},{5... | collective-permute-start | bytes 393224 | tf_op jit(solution)/shard_map/ppermute | solution.py:329
  49.2 3.2 %collective-permute-start.17 = (f32[256,128]{1,0:T(8,128)S(1)}, f32[256,128]{1,0:T(8,128)S(1)}, u32[]{:S(2)}, u32[]{:S(2)}) collective-permute-start(f32[256,128]{1,0:T(8,128)S(1)} %collective-permute-done.13.rest_1_), channel_id=1, source_target_pairs={{0,4},{4,0},{8,12},{12,8},{16,20},{20,16},{24,28},{28,24},{1,5},{5... | collective-permute-start | bytes 393224 | tf_op jit(solution)/shard_map/ppermute | solution.py:329
  50.0 2.4 %collective-permute-start.18 = (f32[256,128]{1,0:T(8,128)S(1)}, f32[256,128]{1,0:T(8,128)S(1)}, u32[]{:S(2)}, u32[]{:S(2)}) collective-permute-start(f32[256,128]{1,0:T(8,128)S(1)} %collective-permute-done.14.rest_2_), channel_id=1, source_target_pairs={{0,4},{4,0},{8,12},{12,8},{16,20},{20,16},{24,28},{28,24},{1,5},{5... | collective-permute-start | bytes 393224 | tf_op jit(solution)/shard_map/ppermute | solution.py:329
  52.5 1.3 %collective-permute-start.19 = (f32[256,128]{1,0:T(8,128)S(1)}, f32[256,128]{1,0:T(8,128)S(1)}, u32[]{:S(2)}, u32[]{:S(2)}) collective-permute-start(f32[256,128]{1,0:T(8,128)S(1)} %collective-permute-done.15.rest_3_), channel_id=1, source_target_pairs={{0,4},{4,0},{8,12},{12,8},{16,20},{20,16},{24,28},{28,24},{1,5},{5... | collective-permute-start | bytes 393224 | tf_op jit(solution)/shard_map/ppermute | solution.py:329
  55.4 15.4 %collective-permute-start.20 = (f32[256,128]{1,0:T(8,128)S(1)}, f32[256,128]{1,0:T(8,128)S(1)}, u32[]{:S(2)}, u32[]{:S(2)}) collective-permute-start(f32[256,128]{1,0:T(8,128)S(1)} %get-tuple-element.55), channel_id=1, source_target_pairs={{0,8},{4,12},{8,0},{12,4},{16,24},{20,28},{24,16},{28,20},{1,9},{5... | collective-permute-start | bytes 393224 | tf_op jit(solution)/shard_map/ppermute | solution.py:323
  56.0 14.8 %collective-permute-start.21 = (f32[256,128]{1,0:T(8,128)S(1)}, f32[256,128]{1,0:T(8,128)S(1)}, u32[]{:S(2)}, u32[]{:S(2)}) collective-permute-start(f32[256,128]{1,0:T(8,128)S(1)} %get-tuple-element.56), channel_id=1, source_target_pairs={{0,16},{4,20},{8,24},{12,28},{16,0},{20,4},{24,8},{28,12},{1,17},{... | collective-permute-start | bytes 393224 | tf_op jit(solution)/shard_map/ppermute | solution.py:323
  57.2 13.6 %collective-permute-start.22 = (f32[256,128]{1,0:T(8,128)S(1)}, f32[256,128]{1,0:T(8,128)S(1)}, u32[]{:S(2)}, u32[]{:S(2)}) collective-permute-start(f32[256,128]{1,0:T(8,128)S(1)} %get-tuple-element.57), channel_id=1, source_target_pairs={{0,24},{4,28},{8,16},{12,20},{16,8},{20,12},{24,0},{28,4},{1,25},{... | collective-permute-start | bytes 393224 | tf_op jit(solution)/shard_map/ppermute | solution.py:323
where the time goes:
time: 74.3 us; the launch traced here: 74.1 us
  Pallas kernels  28.9 us (39%)
  starting transfers between devices  20.2 us (27%)
  waiting for transfers between devices  19.9 us (27%)
  local copies, waits for them, and re-layouts  4.43 us (6%)
  between operations  0.75 us (1%)
    ppermute x12, starting transfers between devices, exchange(): moved.append(lax.ppermute(pieces[offset], 'seg', pairs))  15.2 us
    ppermute x12, waiting for transfers between devices, exchange(): moved.append(lax.ppermute(pieces[offset], 'seg', pairs))  12.3 us
    pallas_call x2, Pallas kernels, backward(): pl.pallas_call(functools.partial(backward_kernel, chips, len(sum_parts),...  11.8 us
    ppermute x3, waiting for transfers between devices, head_sums(): lax.ppermute(sums, 'head', [(at, at ^ step) for at in range(count)])  5.18 us
    pallas_call x1, Pallas kernels, local(): pl.pallas_call(functools.partial(local_kernel, size, tile), grid=(steps,)...  4.56 us
    ppermute x3, starting transfers between devices, head_sums(): lax.ppermute(sums, 'head', [(at, at ^ step) for at in range(count)])  4.45 us
    unnamed x22, local copies, waits for them, and re-layouts  4.43 us
    pallas_call x1, Pallas kernels, local(): pl.pallas_call(functools.partial(finish_kernel, chips), out_shape=[shape(...  3.31 us
  transfers between devices with their start and end apart: 23, of which 11 were waited for; matrix products, arithmetic and copies ran while one was open for 0% of the time, Pallas kernels for 22%

commit v1 on v0

v1 whole, which is shorter than its diff:
```python
import functools

import jax
import jax.numpy as jnp
from jax import lax
from jax.experimental import pallas as pl
from jax.experimental.pallas import tpu as pltpu
from jax.sharding import PartitionSpec as P

norm_eps = 1e-05
f32 = jnp.float32
bf16 = jnp.bfloat16
VMEM_LIMIT = 40 * 1024 * 1024
FIRST_LIMIT = 504 * 1024 * 1024 // 10

SMEM_SPEC = pl.BlockSpec(memory_space=pltpu.SMEM)
VMEM_SPEC = pl.BlockSpec(memory_space=pltpu.VMEM)
ANY_SPEC = pl.BlockSpec(memory_space=pl.ANY)


def nn(a, b):
    return lax.dot_general(a, b, (((1,), (0,)), ((), ())), preferred_element_type=f32)


def nt(a, b):
    return lax.dot_general(a, b, (((1,), (1,)), ((), ())), preferred_element_type=f32)


def tn(a, b):
    return lax.dot_general(a, b, (((0,), (0,)), ((), ())), preferred_element_type=f32)


def row_index(rows, columns):
    return lax.broadcasted_iota(jnp.int32, (rows, columns), 0)


def key_scale(rows, size, length, rate):
    slot = row_index(rows, size).astype(f32)
    remaining = (length - 1) - slot
    return jnp.where(remaining >= 0, jnp.exp(-rate * remaining), 0.0)


def query_scale(rows, size, rate):
    return jnp.exp(-rate * (row_index(rows, size) + 1).astype(f32))


def masked_rows(array, length):
    return jnp.where(row_index(*array.shape) < length, array, jnp.zeros_like(array))


def column(row):
    count = row.shape[1]
    return jnp.broadcast_to(row, (count, count)).T


def write_pieces(whole, outs, chip):
    piece = outs[0].shape[0]
    for offset, out in enumerate(outs):
        at = pl.multiple_of((chip ^ offset) * piece, piece)
        out[...] = whole[pl.ds(at, piece), :]


def read_pieces(pieces, whole, chip):
    piece = pieces[0].shape[0]
    for offset, part in enumerate(pieces):
        at = pl.multiple_of((chip ^ offset) * piece, piece)
        whole[pl.ds(at, piece), :] = part[...]


def near_kernel(query_any, key_any, value_any, query_ref, key_ref, value_ref, sems):
    copies = [
        pltpu.make_async_copy(source, target, sems.at[at])
        for at, (source, target) in enumerate(((key_any, key_ref), (value_any, value_ref), (query_any, query_ref)))
    ]
    for copy in copies:
        copy.start()
    for copy in copies:
        copy.wait()


def state_kernel(chips, length_ref, rate_ref, key_ref, value_ref, *rest):
    outs, whole = rest[:chips], rest[chips]
    own = lax.axis_index("seg")
    rows, wide = key_ref.shape
    size = whole.shape[1]
    lengths = length_ref[...].astype(f32)
    mine = lax.broadcasted_iota(jnp.int32, lengths.shape, 1) == own
    length = jnp.sum(jnp.where(mine, lengths, 0.0), axis=1, keepdims=True)
    pair = min(2 * size, wide)
    for first in range(0, wide, pair):
        scaled = []
        for begin in range(first, first + pair, size):
            head = begin // size
            scale = key_scale(rows, size, length, rate_ref[:, head:head + 1])
            scaled.append((value_ref[:, begin:begin + size].astype(f32) * scale).astype(bf16))
        both = tn(key_ref[:, first:first + pair], jnp.concatenate(scaled, axis=1))
        for begin in range(0, pair, size):
            span = slice(begin, begin + size)
            whole[first + begin:first + begin + size, :] = both[span, span]
    write_pieces(whole, outs, own // 2)


def decay_tiles(tile, rate, count, transposed):
    u = lax.broadcasted_iota(jnp.int32, (tile, tile), 1 if transposed else 0)
    w = lax.broadcasted_iota(jnp.int32, (tile, tile), 0 if transposed else 1)
    base = jnp.exp((w - u).astype(f32) * rate)
    tiles = [jnp.where(u >= w, base, 0.0)]
    for gap in range(1, count):
        tiles.append(base * jnp.exp(jnp.full((1, tile), -(gap * tile), f32) * rate))
    return tiles


def tree_distances(length_ref, parent_ref, table, count):
    for at in range(count):
        table[at] = jnp.int32(-1)

    def one(block, carry):
        above = parent_ref[block]
        passed = length_ref[jnp.maximum(above, 0)]
        for at in range(count):
            distance = table[(above + 1) * count + at]
            distance = jnp.where(distance >= 0, distance + passed, distance)
            table[(block + 1) * count + at] = jnp.where(above == at, 0, distance)
        return carry

    lax.fori_loop(0, count, one, 0)


def weight_table(length_ref, parent_ref, rate_ref, distances, table_ref, chips, size, piece):
    own = lax.axis_index("seg")
    chip, core = own // 2, own % 2
    count = 2 * chips
    tree_distances(length_ref, parent_ref, distances, count)
    row = row_index(8, size)
    rates = jnp.full((8, size), rate_ref[(chip * piece) // size], f32)
    for at in range(1, piece // size):
        rates = jnp.where(row == at, rate_ref[(chip * piece) // size + at], rates)
    for backward in range(2):
        for target in range(chips):
            wanted = (chip ^ target) * 2 + core
            for offset in range(chips):
                for sibling in range(2):
                    source = (chip ^ offset) * 2 + (core ^ sibling)
                    place = (source + 1) * count + wanted if backward else (wanted + 1) * count + source
                    distance = distances[place].astype(f32)
                    linked = (distance >= 0.0).astype(f32)
                    slot = ((backward * chips + target) * chips + offset) * 2 + sibling
                    table_ref[slot] = jnp.exp(rates * -distance) * linked


def local_head(size, tile, head, near, rate, query, key_ref, value_ref, out_ref):
    span = slice(head * size, (head + 1) * size)
    count = query.shape[0] // tile
    decays = decay_tiles(tile, rate, count, False)
    for i in range(count):
        total = None
        for j in range(i + 1):
            w_span = slice(j * tile, (j + 1) * tile)
            scores = nt(query[i * tile:(i + 1) * tile], key_ref[w_span, span])
            weighted = (scores * decays[i - j]).astype(bf16)
            part = nn(weighted, value_ref[w_span, span])
            total = part if total is None else total + part
        out_ref[i * tile:(i + 1) * tile, near * size:(near + 1) * size] = total


def local_kernel(size, tile, chips, piece, picked, length_ref, parent_ref, rate_ref, query_ref, key_ref, value_ref, *rest):
    out_ref, masked_ref, table_ref, facts_ref, distances = rest
    own = lax.axis_index("seg")
    rows, wide = query_ref.shape
    heads = wide // size
    length = length_ref[own]
    weight_table(length_ref, parent_ref, rate_ref, distances, table_ref, chips, size, piece)
    for head in range(heads):
        facts_ref[head:head + 1, :] = jnp.full((1, size), rate_ref[head], f32)
    facts_ref[heads:, :] = jnp.full((1, size), length.astype(f32), f32)
    masked_ref[...] = masked_rows(query_ref[...], length)
    for head in picked:
        query = masked_ref[:, head * size:(head + 1) * size]
        local_head(size, tile, head, head - picked[0], rate_ref[head], query, key_ref, value_ref, out_ref)


def tile_pairs(count):
    return [(i, j) for j in range(count) for i in range(j, count)]


def weighted_kernel(size, tile, picked, facts_ref, query_ref, key_ref, value_ref, out_ref, local_ref):
    rows, wide = query_ref.shape
    count = rows // tile
    for head in range(wide // size):
        span = slice(head * size, (head + 1) * size)
        rate = facts_ref[head:head + 1, :1]
        decays = decay_tiles(tile, rate, count, True)
        for place, (i, j) in enumerate(tile_pairs(count)):
            scores = nt(key_ref[j * tile:(j + 1) * tile, span], query_ref[i * tile:(i + 1) * tile, span])
            out_ref[head, place] = (scores * decays[i - j]).astype(bf16)
        if head in picked:
            local_head(size, tile, head, head - picked[0], rate, query_ref[:, span], key_ref, value_ref, local_ref)


def pick(refs, size, head):
    for ref in refs:
        here = ref.shape[1] // size
        if head < here:
            return ref[:, head * size:(head + 1) * size]
        head -= here


def mix_kernel(chips, size, backward, table_ref, *rest):
    mine, other, outs = rest[:chips], rest[chips:2 * chips], rest[len(rest) - chips:]
    piece = mine[0].shape[0]
    part = min(piece, size)
    for at in range(piece // part):
        span = slice(at * part, (at + 1) * part)
        totals = [None] * chips
        for offset in range(chips):
            for sibling, sources in ((0, mine), (1, other)):
                data = sources[offset][span, :]
                for target in range(chips):
                    slot = ((backward * chips + target) * chips + offset) * 2 + sibling
                    term = table_ref[slot, at:at + 1, :] * data
                    totals[target] = term if totals[target] is None else totals[target] + term
        for target in range(chips):
            outs[target][span, :] = totals[target]


def attend_kernel(chips, parts, facts_ref, query_ref, upstream_ref, gain_ref, *rest):
    local_refs, rest = rest[:parts], rest[parts:]
    pieces, attended_ref, sums_ref, whole = rest[:chips], rest[-3], rest[-2], rest[-1]
    own = lax.axis_index("seg")
    rows, wide = query_ref.shape
    size = whole.shape[1]
    read_pieces(pieces, whole, own // 2)
    squares = jnp.zeros((rows, size), f32)
    inners = jnp.zeros((rows, size), f32)
    for head in range(wide // size):
        span = slice(head * size, (head + 1) * size)
        carried = whole[span, :].astype(bf16)
        scale = query_scale(rows, size, facts_ref[head:head + 1, :])
        attended = pick(local_refs, size, head) + scale * nn(query_ref[:, span], carried)
        attended_ref[:, span] = attended
        scaled = upstream_ref[:, span].astype(f32) * gain_ref[:, span]
        squares = squares + attended * attended
        inners = inners + scaled * attended
    groups = rows // size
    for at in range(groups):
        span = slice(at * size, (at + 1) * size)
        sums_ref[at:at + 1, :] = jnp.sum(squares[span].T, axis=0, keepdims=True)
        sums_ref[groups + at:groups + at + 1, :] = jnp.sum(inners[span].T, axis=0, keepdims=True)


def norm_columns(sum_refs, width, inverse_ref, factor_ref):
    total = sum_refs[0][...]
    for ref in sum_refs[1:]:
        total = total + ref[...]
    groups = total.shape[0] // 2
    size = total.shape[1]
    inverse = lax.rsqrt(total[:groups] / width + norm_eps)
    factor = inverse * inverse * inverse * total[groups:] / width
    for at in range(groups):
        span = slice(at * size, (at + 1) * size)
        inverse_ref[span, :] = column(inverse[at:at + 1])
        factor_ref[span, :] = column(factor[at:at + 1])


def state_grad_kernel(chips, sums, width, facts_ref, query_ref, upstream_ref, attended_ref, gain_ref, *rest):
    sum_refs, outs = rest[:sums], rest[sums:sums + chips]
    inverse_ref, factor_ref, whole = rest[sums + chips:]
    own = lax.axis_index("seg")
    rows, wide = query_ref.shape
    size = whole.shape[1]
    norm_columns(sum_refs, width, inverse_ref, factor_ref)
    inverse = inverse_ref[...]
    factor = factor_ref[...]
    heads = wide // size
    group = min(2, heads)
    for first in range(0, heads, group):
        parts = []
        for head in range(first, first + group):
            span = slice(head * size, (head + 1) * size)
            scaled = upstream_ref[:, span].astype(f32) * gain_ref[:, span]
            grad = inverse * scaled - factor * attended_ref[:, span]
            parts.append((grad * query_scale(rows, size, facts_ref[head:head + 1, :])).astype(bf16))
        span = slice(first * size, (first + group) * size)
        both = tn(query_ref[:, span], jnp.concatenate(parts, axis=1))
        for at in range(group):
            inner = slice(at * size, (at + 1) * size)
            whole[(first + at) * size:(first + at + 1) * size, :] = both[inner, inner]
    write_pieces(whole, outs, own // 2)


def backward_kernel(chips, sums, width, tile, heads, done, facts_ref, query_ref, key_ref, value_ref, upstream_ref, attended_ref, weighted_ref, gain_ref, *rest):
    sum_refs, pieces, rest = rest[:sums], rest[sums:sums + chips], rest[sums + chips:]
    earlier, rest = rest[:2 * done], rest[2 * done:]
    if done:
        out_any, query_grad_any, key_grad_ref, value_grad_ref, inverse_ref, factor_ref, whole, out_ref, query_grad_ref, sems = rest
    else:
        out_ref, query_grad_ref, key_grad_ref, value_grad_ref, token_ref, inverse_ref, factor_ref, whole = rest
        token_ref[...] = jnp.zeros_like(token_ref)
    own = lax.axis_index("seg")
    rows, wide = query_ref.shape
    size = whole.shape[1]
    count = rows // tile
    copies = []

    def send(source, target, columns):
        copies.append(pltpu.make_async_copy(source, target.at[:, columns], sems.at[len(copies)]))
        copies[-1].start()

    if done:
        for source, target in zip(earlier, (out_any, query_grad_any)):
            send(source, target, pl.ds(0, source.shape[1]))
    norm_columns(sum_refs, width, inverse_ref, factor_ref)
    read_pieces(pieces, whole, own // 2)
    length = facts_ref[wide // size:, :]
    used = row_index(rows, size).astype(f32) < length
    for head in heads:
        span = slice(head * size, (head + 1) * size)
        near = slice((head - heads[0]) * size, (head - heads[0] + 1) * size)
        rate = facts_ref[head:head + 1, :]
        query = query_ref[:, span]
        key = key_ref[:, span]
        value = value_ref[:, span]
        gain = gain_ref[:, span]
        inverse = inverse_ref[...]
        attended = attended_ref[:, span]
        out_ref[:, near] = (attended * inverse * gain).astype(bf16)
        scaled = upstream_ref[:, span].astype(f32) * gain
        grad = (inverse * scaled - factor_ref[...] * attended).astype(bf16)
        carried = whole[span, :].astype(bf16)
        query_grad = nt(grad, carried) * query_scale(rows, size, rate)
        decays = decay_tiles(tile, rate[:, :1], count, True)
        query_totals, key_totals, value_totals = [None] * count, [None] * count, [None] * count
        for place, (i, j) in enumerate(tile_pairs(count)):
            u_span, w_span = slice(i * tile, (i + 1) * tile), slice(j * tile, (j + 1) * tile)
            score_grad = (nt(value[w_span], grad[u_span]) * decays[i - j]).astype(bf16)
            for totals, index, part in (
                (value_totals, j, nn(weighted_ref[head, place], grad[u_span])),
                (key_totals, j, nn(score_grad, query[u_span])),
                (query_totals, i, tn(score_grad, key[w_span])),
            ):
                totals[index] = part if totals[index] is None else totals[index] + part
        key_grad_ref[:, near] = jnp.concatenate(key_totals, axis=0).astype(bf16)
        value_grad_ref[:, near] = jnp.concatenate(value_totals, axis=0).astype(bf16)
        query_grad = query_grad + jnp.concatenate(query_totals, axis=0)
        query_grad_ref[:, near] = jnp.where(used, query_grad, 0.0).astype(bf16)
        if done:
            for source, target in ((out_ref, out_any), (query_grad_ref, query_grad_any)):
                send(source.at[:, near], target, pl.ds(head * size, size))
    for copy in copies:
        copy.wait()


def finish_kernel(chips, parts, step, facts_ref, key_ref, value_ref, *rest):
    local_refs, rest = rest[:2 * parts], rest[2 * parts:]
    pieces, key_hbm, value_hbm = rest[:chips], rest[chips], rest[chips + 1]
    whole, key_grad_ref, value_grad_ref, sems = rest[chips + 2:]
    own = lax.axis_index("seg")
    rows, wide = key_ref.shape
    size = whole.shape[1]
    heads = wide // size
    length = facts_ref[heads:, :]
    read_pieces(pieces, whole, own // 2)
    copies = []
    for at in range(wide // step):
        for begin in range(at * step, (at + 1) * step, size):
            span = slice(begin, begin + size)
            head = begin // size
            scale = key_scale(rows, size, length, facts_ref[head:head + 1, :])
            state_grad = whole[span, :].astype(bf16)
            key_part = scale * nt(value_ref[:, span], state_grad)
            value_part = scale * nn(key_ref[:, span], state_grad)
            key_grad_ref[:, span] = (pick(local_refs[::2], size, head).astype(f32) + key_part).astype(bf16)
            value_grad_ref[:, span] = (pick(local_refs[1::2], size, head).astype(f32) + value_part).astype(bf16)
        span = pl.ds(at * step, step)
        for kind, (source, target) in enumerate(((key_grad_ref, key_hbm), (value_grad_ref, value_hbm))):
            copy = pltpu.make_async_copy(source.at[:, span], target.at[:, span], sems.at[2 * at + kind])
            copy.start()
            copies.append(copy)
    for copy in copies:
        copy.wait()


def params(limit=VMEM_LIMIT):
    return pltpu.CompilerParams(vmem_limit_bytes=limit)


def shape(dims, dtype):
    return jax.ShapeDtypeStruct(dims, dtype)


def pass_on(piece_ref, before_ref, out_ref):
    pass


def after(piece, before):
    return pl.pallas_call(
        pass_on,
        out_shape=shape(piece.shape, piece.dtype),
        in_specs=[ANY_SPEC] * 2,
        out_specs=ANY_SPEC,
        input_output_aliases={0: 0},
        compiler_params=params(),
        name="after",
    )(piece, before)


def exchange(pieces, count):
    moved = [pieces[0]]
    for offset in range(1, len(pieces)):
        pairs = [(at, at ^ (2 * offset)) for at in range(count)]
        moved.append(lax.ppermute(pieces[offset], "seg", pairs))
    return moved


def swap_cores(pieces, count):
    pairs = [(at, at ^ 1) for at in range(count)]
    return [lax.ppermute(piece, "seg", pairs) for piece in pieces]


def add_kernel(left_ref, right_ref, out_ref):
    out_ref[...] = left_ref[...] + right_ref[...]


def head_sums(sums, count):
    step = 1
    parts = [sums]
    while step < count:
        if len(parts) == 2:
            parts = [
                pl.pallas_call(
                    add_kernel,
                    out_shape=shape(sums.shape, sums.dtype),
                    in_specs=[VMEM_SPEC] * 2,
                    out_specs=VMEM_SPEC,
                    compiler_params=params(),
                    name="add_sums",
                )(*parts)
            ]
        parts.append(lax.ppermute(parts[0], "head", [(at, at ^ step) for at in range(count)]))
        step *= 2
    return parts


def local(seg_count, head_count, queries, key_tokens, values, upstream, norm_gain, decay_rate, block_length, parent):
    rows, wide = queries.shape
    heads = decay_rate.shape[0]
    size = wide // heads
    width = wide * head_count
    chips = seg_count // 2
    piece = wide // chips
    group = min(2, heads) * size
    tile = min(256, rows)
    gain = norm_gain[None, :]
    piece_shapes = [shape((piece, size), f32)] * chips
    piece_specs = [VMEM_SPEC] * chips
    whole = pltpu.VMEM((wide, size), f32)
    tokens = pltpu.VMEM((rows, wide), bf16)

    query_near, key_near, value_near = pl.pallas_call(
        near_kernel,
        out_shape=[shape((rows, wide), bf16)] * 3,
        in_specs=[ANY_SPEC] * 3,
        out_specs=[VMEM_SPEC] * 3,
        scratch_shapes=[pltpu.SemaphoreType.DMA((3,))],
        compiler_params=params(FIRST_LIMIT),
        name="bring_near",
    )(queries, key_tokens, values)

    states = pl.pallas_call(
        functools.partial(state_kernel, chips),
        out_shape=piece_shapes,
        in_specs=[VMEM_SPEC] * 4,
        out_specs=piece_specs,
        scratch_shapes=[whole],
        compiler_params=params(),
        name="block_state",
    )(block_length[None, :], decay_rate[None, :], key_near, value_near)

    slots = 2 * chips * chips * 2
    half = heads // 2
    first_heads, last_heads = range(half), range(half, heads)
    first_local, masked, table, facts = pl.pallas_call(
        functools.partial(local_kernel, size, tile, chips, piece, first_heads),
        out_shape=[
            shape((rows, half * size), f32),
            shape((rows, wide), bf16),
            shape((slots, 8, size), f32),
            shape((heads + 1, size), f32),
        ],
        in_specs=[SMEM_SPEC] * 3 + [VMEM_SPEC] * 3,
        out_specs=[VMEM_SPEC] * 4,
        scratch_shapes=[pltpu.SMEM((seg_count * (seg_count + 1),), jnp.int32)],
        compiler_params=params(),
        cost_estimate=pl.CostEstimate(flops=2 * rows * rows * wide, bytes_accessed=10 * rows * wide, transcendentals=rows * rows * half),
        name="local_attention",
    )(block_length, parent, decay_rate, query_near, key_near, value_near)

    pairs = len(tile_pairs(rows // tile))
    weighted, last_local = pl.pallas_call(
        functools.partial(weighted_kernel, size, tile, last_heads),
        out_shape=[shape((heads, pairs, tile, tile), bf16), shape((rows, (heads - half) * size), f32)],
        in_specs=[VMEM_SPEC] * 4,
        out_specs=[VMEM_SPEC] * 2,
        compiler_params=params(),
        cost_estimate=pl.CostEstimate(flops=4 * rows * rows * wide, bytes_accessed=10 * rows * wide, transcendentals=rows * rows * heads),
        name="weighted_scores",
    )(facts, masked, key_near, value_near)

    def mix(pieces, backward, before):
        mine = exchange(pieces, seg_count)
        mine = mine[:1] + [after(piece, before) for piece in mine[1:]]
        other = swap_cores(mine, seg_count)
        mixed = pl.pallas_call(
            functools.partial(mix_kernel, chips, size, backward),
            out_shape=piece_shapes,
            in_specs=[VMEM_SPEC] + piece_specs * 2,
            out_specs=piece_specs,
            compiler_params=params(),
            name="mix_backward" if backward else "mix_forward",
        )(table, *mine, *other)
        return exchange(mixed, seg_count)

    carried = mix(states, 0, table)

    attended, sums = pl.pallas_call(
        functools.partial(attend_kernel, chips, 2),
        out_shape=[shape((rows, wide), f32), shape((2 * rows // size, size), f32)],
        in_specs=[VMEM_SPEC] * (6 + chips),
        out_specs=[VMEM_SPEC] * 2,
        scratch_shapes=[whole],
        compiler_params=params(),
        name="attend",
    )(facts, masked, upstream, gain, first_local, last_local, *carried)

    sum_parts = head_sums(sums, head_count)
    columns = pltpu.VMEM((rows, size), f32)

    state_grads = pl.pallas_call(
        functools.partial(state_grad_kernel, chips, len(sum_parts), width),
        out_shape=piece_shapes,
        in_specs=[VMEM_SPEC] * (5 + len(sum_parts)),
        out_specs=piece_specs,
        scratch_shapes=[columns, columns, whole],
        compiler_params=params(),
        name="state_grad",
    )(facts, masked, upstream, attended, gain, *sum_parts)

    def backward(picked, earlier):
        done = len(earlier) // 2
        near = (rows, len(picked) * size)
        if done:
            out_shape = [shape((rows, wide), bf16)] * 2 + [shape(near, bf16)] * 2
            out_specs = [ANY_SPEC] * 2 + [VMEM_SPEC] * 2
            scratch = [pltpu.VMEM(near, bf16)] * 2 + [pltpu.SemaphoreType.DMA((2 * (done + len(picked)),))]
        else:
            out_shape = [shape(near, bf16)] * 4 + [shape((8, size), f32)]
            out_specs = [VMEM_SPEC] * 5
            scratch = []
        return pl.pallas_call(
            functools.partial(backward_kernel, chips, len(sum_parts), width, tile, picked, done),
            out_shape=out_shape,
            in_specs=[VMEM_SPEC] * (8 + len(sum_parts) + chips + len(earlier)),
            out_specs=out_specs,
            scratch_shapes=[columns, columns, whole] + scratch,
            compiler_params=params(),
            cost_estimate=pl.CostEstimate(
                flops=8 * rows * rows * near[1], bytes_accessed=16 * rows * near[1], transcendentals=rows * rows * len(picked)
            ),
            name="local_backward",
        )(facts, masked, key_near, value_near, upstream, attended, weighted, gain, *sum_parts, *carried, *earlier)

    out_part, query_part, *local_grads, token = backward(first_heads, [])
    state_sums = mix(state_grads, 1, token)
    attention_out, query_grad, *more = backward(last_heads, [out_part, query_part])
    local_grads = local_grads + more

    key_grad, value_grad = pl.pallas_call(
        functools.partial(finish_kernel, chips, len(local_grads) // 2, size),
        out_shape=[shape((rows, wide), bf16)] * 2,
        in_specs=[VMEM_SPEC] * (3 + len(local_grads) + chips),
        out_specs=[ANY_SPEC] * 2,
        scratch_shapes=[whole, tokens, tokens, pltpu.SemaphoreType.DMA((2 * heads,))],
        compiler_params=params(),
        name="finish",
    )(facts, key_near, value_near, *local_grads, *state_sums)
    return attention_out, query_grad, key_grad, value_grad


def solution(mesh):
    sizes = dict(mesh.shape)
    tokens = P("seg", "head")
    return jax.shard_map(
        functools.partial(local, sizes["seg"], sizes["head"]),
        mesh=mesh,
        in_specs=(tokens, tokens, tokens, tokens, P("head"), P("head"), P(), P()),
        out_specs=(tokens, tokens, tokens, tokens),
        check_vma=False,
    )
```

time: 74.3 us -> 57.3 us (0.77)
  Pallas kernels: 28.9 us -> 20.8 us
  waiting for transfers between devices: 19.9 us -> 14.2 us
  local copies, waits for them, and re-layouts: 4.43 us -> 0.03 us
  starting transfers between devices: 20.2 us -> 21.2 us
    ppermute x12, waiting for transfers between devices: 12.3 us -> 7.84 us  [exchange(): moved.append(lax.ppermute(pieces[offset], 'seg', pairs))]
    unnamed x22 -> x10, local copies, waits for them, and re-layouts: 4.43 us -> 0.03 us
    pallas_call x2, Pallas kernels: 11.8 us -> 7.73 us  [backward(): pl.pallas_call(functools.partial(backward_kernel, chips, len(sum_parts),...]
    pallas_call x2, Pallas kernels: 3.27 us -> 0.58 us  [mix(): pl.pallas_call(functools.partial(mix_kernel, chips, size, backward), out_...]
    ppermute x3 -> x2, waiting for transfers between devices: 5.18 us -> 3.95 us  [head_sums(): lax.ppermute(parts[0], 'head', [(at, at ^ step) for at in range(count)])]
    ppermute x8, starting transfers between devices: 0.53 us -> 1.76 us  [swap_cores(): return [lax.ppermute(piece, 'seg', pairs) for piece in pieces]]
    pallas_call x4 -> x13, Pallas kernels: 12 us -> 11.3 us  [the longest x1 2.79 us: local(): pl.pallas_call(functools.partial(local_kernel, size, tile, chips, piece,...]
    ppermute x3 -> x2, starting transfers between devices: 4.45 us -> 4.23 us  [head_sums(): lax.ppermute(parts[0], 'head', [(at, at ^ step) for at in range(count)])]
  transfers between devices with their start and end apart: 23 -> 22, of which waited for: 11 -> 13; matrix products, arithmetic and copies ran while one was open for 0% -> 0% of each run, Pallas kernels for 22% -> 23%
where the time goes in v1:
time: 57.3 us; the launch traced here: 57.1 us
  starting transfers between devices  21.2 us (37%)
  Pallas kernels  20.8 us (36%)
  waiting for transfers between devices  14.2 us (25%)
  between operations  0.97 us (2%)
    ppermute x12, starting transfers between devices, exchange(): moved.append(lax.ppermute(pieces[offset], 'seg', pairs))  15.2 us
    ppermute x12, waiting for transfers between devices, exchange(): moved.append(lax.ppermute(pieces[offset], 'seg', pairs))  7.84 us
    pallas_call x2, Pallas kernels, backward(): pl.pallas_call(functools.partial(backward_kernel, chips, len(sum_parts),...  7.73 us
    ppermute x2, starting transfers between devices, head_sums(): lax.ppermute(parts[0], 'head', [(at, at ^ step) for at in range(count)])  4.23 us
    ppermute x2, waiting for transfers between devices, head_sums(): lax.ppermute(parts[0], 'head', [(at, at ^ step) for at in range(count)])  3.95 us
    pallas_call x1, Pallas kernels, local(): pl.pallas_call(functools.partial(local_kernel, size, tile, chips, piece,...  2.79 us
    ppermute x8, waiting for transfers between devices, swap_cores(): return [lax.ppermute(piece, 'seg', pairs) for piece in pieces]  2.36 us
    pallas_call x1, Pallas kernels, local(): pl.pallas_call(functools.partial(weighted_kernel, size, tile, last_heads)...  2.34 us
  transfers between devices with their start and end apart: 22, of which 13 were waited for; matrix products, arithmetic and copies ran while one was open for 0% of the time, Pallas kernels for 23%

profile of v1, /device:TPU:0, one launch (start us, length us, event | category | flops | bytes accessed | tf_op | source)
XLA Modules:
  0.0 57.1 jit_solution(6251434947099982639)
XLA Ops:
  0.6 0.0 copy-start.2
  0.6 0.0 copy-start.3
  0.7 0.0 copy-start.4
  0.7 1.9 %bring_near.1 = (bf16[512,1024]{1,0:T(8,128)(2,1)S(1)}, bf16[512,1024]{1,0:T(8,128)(2,1)S(1)}, bf16[512,1024]{1,0:T(8,128)(2,1)S(1)}) custom-call(bf16[512,1024]{1,0:T(8,128)(2,1)} %query_any.1, bf16[512,1024]{1,0:T(8,128)(2,1)} %key_any.1, bf16[512,1024]{1,0:T(8,128)(2,1)} %value_any.1), custom_call_target="tpu_custom_call" | custom-call | tf_op jit(solution)/shard_map/bring_near/pallas_call | solution.py:459
  2.6 0.0 copy-done.2
  2.6 0.0 copy-done.3
  2.6 0.9 %block_state.1 = (f32[256,128]{1,0:T(8,128)S(1)}, f32[256,128]{1,0:T(8,128)S(1)}, f32[256,128]{1,0:T(8,128)S(1)}, f32[256,128]{1,0:T(8,128)S(1)}) custom-call(s32[1,8]{1,0:T(1,128)S(1)} %bitcast.7, f32[1,8]{1,0:T(1,128)S(1)} %bitcast.8, bf16[512,1024]{1,0:T(8,128)(2,1)S(1)} %get-tuple-element.43.key_ref, bf16[512,1024]{1,0:T(8,128)(2,1)S(1)} %get-tuple-element.44.value_ref), custom_call_target="tpu_custom_call" | custom-call | tf_op jit(solution)/shard_map/block_state/pallas_call | solution.py:469
  3.5 3.0 %collective-permute-start = (f32[256,128]{1,0:T(8,128)S(1)}, f32[256,128]{1,0:T(8,128)S(1)}, u32[]{:S(2)}, u32[]{:S(2)}) collective-permute-start(f32[256,128]{1,0:T(8,128)S(1)} %get-tuple-element.51), channel_id=1, source_target_pairs={{0,8},{4,12},{8,0},{12,4},{16,24},{20,28},{24,16},{28,20},{1,9},{5... | collective-permute-start | bytes 393224 | tf_op jit(solution)/shard_map/ppermute | solution.py:411
  6.5 1.5 %collective-permute-start.1 = (f32[256,128]{1,0:T(8,128)S(1)}, f32[256,128]{1,0:T(8,128)S(1)}, u32[]{:S(2)}, u32[]{:S(2)}) collective-permute-start(f32[256,128]{1,0:T(8,128)S(1)} %get-tuple-element.52), channel_id=1, source_target_pairs={{0,16},{4,20},{8,24},{12,28},{16,0},{20,4},{24,8},{28,12},{1,17},{... | collective-permute-start | bytes 393224 | tf_op jit(solution)/shard_map/ppermute | solution.py:411
  8.1 0.0 collective-permute-start.2
  8.1 0.0 collective-permute-start.3
  8.1 0.0 copy-done.4
  8.1 2.8 %local_attention.1 = (f32[512,512]{1,0:T(8,128)S(1)}, bf16[512,1024]{1,0:T(8,128)(2,1)S(1)}, f32[64,8,128]{2,1,0:T(8,128)S(1)}, f32[9,128]{1,0:T(8,128)S(1)}) custom-call(s32[8]{0:T(128)S(1)} %copy-done.2, s32[8]{0:T(128)S(1)} %copy-done.4, f32[8]{0:T(128)S(1)} %copy-done.3, bf16[512,1024]{1,0:T(8,128)(2,1)S(1)} %get-tuple-element.42.query_ref, ...), custom_call_target="tpu_custom_call" | custom-call | flops 536870912 | bytes 5242880 | tf_op jit(solution)/shard_map/local_attention/pallas_call | solution.py:482
  10.9 0.0 collective-permute-done.piece_ref
  10.9 0.0 copy-start
  10.9 0.0 copy-start.1
  10.9 0.6 %collective-permute-start.4 = (f32[256,128]{1,0:T(8,128)S(1)}, f32[256,128]{1,0:T(8,128)S(1)}, u32[]{:S(2)}, u32[]{:S(2)}) collective-permute-start(f32[256,128]{1,0:T(8,128)S(1)} %after.6.rest_1_), channel_id=1, source_target_pairs={{0,4},{4,0},{8,12},{12,8},{16,20},{20,16},{24,28},{28,24},{1,5},{5... | collective-permute-start | bytes 393224 | tf_op jit(solution)/shard_map/ppermute | solution.py:417
  11.5 2.8 %collective-permute-done.1.piece_ref = f32[256,128]{1,0:T(8,128)S(1)} collective-permute-done((f32[256,128]{1,0:T(8,128)S(1)}, f32[256,128]{1,0:T(8,128)S(1)}, u32[]{:S(2)}, u32[]{:S(2)}) %collective-permute-start.1) | collective-permute-done | bytes 131104 | tf_op jit(solution)/shard_map/ppermute | solution.py:411
  14.3 0.0 collective-permute-start.5
  14.3 0.0 collective-permute-done.2.piece_ref
  14.3 0.5 collective-permute-start.6
  14.8 0.0 collective-permute-done.3.rest_4_
  14.8 0.0 collective-permute-done.4.rest_5_
  14.8 0.8 %collective-permute-done.5.rest_6_ = f32[256,128]{1,0:T(8,128)S(1)} collective-permute-done((f32[256,128]{1,0:T(8,128)S(1)}, f32[256,128]{1,0:T(8,128)S(1)}, u32[]{:S(2)}, u32[]{:S(2)}) %collective-permute-start.5) | collective-permute-done | bytes 131104 | tf_op jit(solution)/shard_map/ppermute | solution.py:417
  15.7 0.2 collective-permute-done.6.rest_7_
  15.9 0.3 mix_forward.1
  16.1 1.1 %collective-permute-start.7 = (f32[256,128]{1,0:T(8,128)S(1)}, f32[256,128]{1,0:T(8,128)S(1)}, u32[]{:S(2)}, u32[]{:S(2)}) collective-permute-start(f32[256,128]{1,0:T(8,128)S(1)} %get-tuple-element.55), channel_id=1, source_target_pairs={{0,8},{4,12},{8,0},{12,4},{16,24},{20,28},{24,16},{28,20},{1,9},{5... | collective-permute-start | bytes 393224 | tf_op jit(solution)/shard_map/ppermute | solution.py:411
  17.3 1.0 %collective-permute-start.8 = (f32[256,128]{1,0:T(8,128)S(1)}, f32[256,128]{1,0:T(8,128)S(1)}, u32[]{:S(2)}, u32[]{:S(2)}) collective-permute-start(f32[256,128]{1,0:T(8,128)S(1)} %get-tuple-element.56), channel_id=1, source_target_pairs={{0,16},{4,20},{8,24},{12,28},{16,0},{20,4},{24,8},{28,12},{1,17},{... | collective-permute-start | bytes 393224 | tf_op jit(solution)/shard_map/ppermute | solution.py:411
  18.3 1.4 %collective-permute-start.9 = (f32[256,128]{1,0:T(8,128)S(1)}, f32[256,128]{1,0:T(8,128)S(1)}, u32[]{:S(2)}, u32[]{:S(2)}) collective-permute-start(f32[256,128]{1,0:T(8,128)S(1)} %get-tuple-element.57), channel_id=1, source_target_pairs={{0,24},{4,28},{8,16},{12,20},{16,8},{20,12},{24,0},{28,4},{1,25},{... | collective-permute-start | bytes 393224 | tf_op jit(solution)/shard_map/ppermute | solution.py:411
  19.7 2.3 %weighted_scores.1 = (bf16[8,3,256,256]{3,2,1,0:T(8,128)(2,1)S(1)}, f32[512,512]{1,0:T(8,128)S(1)}) custom-call(f32[9,128]{1,0:T(8,128)S(1)} %get-tuple-element.45.facts_ref, bf16[512,1024]{1,0:T(8,128)(2,1)S(1)} %get-tuple-element.46.query_ref, bf16[512,1024]{1,0:T(8,128)(2,1)S(1)} %get-tuple-element.43.key_ref, ...), custom_call_target="tpu_custom_call" | custom-call | flops 1073741824 | bytes 5242880 | tf_op jit(solution)/shard_map/weighted_scores/pallas_call | solution.py:499
  22.1 0.5 collective-permute-done.7.rest_3_
  22.5 1.5 %collective-permute-done.8.rest_4_ = f32[256,128]{1,0:T(8,128)S(1)} collective-permute-done((f32[256,128]{1,0:T(8,128)S(1)}, f32[256,128]{1,0:T(8,128)S(1)}, u32[]{:S(2)}, u32[]{:S(2)}) %collective-permute-start.8) | collective-permute-done | bytes 131104 | tf_op jit(solution)/shard_map/ppermute | solution.py:411
  24.1 1.6 %collective-permute-done.9.rest_5_ = f32[256,128]{1,0:T(8,128)S(1)} collective-permute-done((f32[256,128]{1,0:T(8,128)S(1)}, f32[256,128]{1,0:T(8,128)S(1)}, u32[]{:S(2)}, u32[]{:S(2)}) %collective-permute-start.9) | collective-permute-done | bytes 131104 | tf_op jit(solution)/shard_map/ppermute | solution.py:411
  25.7 0.0 copy-done
  25.7 1.2 %attend.1 = (f32[512,1024]{1,0:T(8,128)S(1)}, f32[8,128]{1,0:T(8,128)S(1)}) custom-call(f32[9,128]{1,0:T(8,128)S(1)} %get-tuple-element.45.facts_ref, bf16[512,1024]{1,0:T(8,128)(2,1)S(1)} %get-tuple-element.46.query_ref, bf16[512,1024]{1,0:T(8,128)(2,1)S(1)} %copy-done, f32[1,1024]{1,0:T(1,128)S(1)} %bitcast.3, f32[512,512]{1,0:T(8,128)S(1)} %get-tuple-element.47.rest_0_, ...), custom_call_target="tpu_custom_call" | custom-call | tf_op jit(solution)/shard_map/attend/pallas_call | solution.py:525
  26.9 1.6 %collective-permute-start.10 = (f32[8,128]{1,0:T(8,128)S(1)}, f32[8,128]{1,0:T(8,128)S(1)}, u32[]{:S(2)}, u32[]{:S(2)}) collective-permute-start(f32[8,128]{1,0:T(8,128)S(1)} %get-tuple-element.60.left_ref), channel_id=1, source_target_pairs={{0,1},{1,0},{2,3},{3,2},{4,5},{5,4},{6,7},{7,6},{8,9},{9,8},{10,11... | collective-permute-start | bytes 12296 | tf_op jit(solution)/shard_map/ppermute | solution.py:439
  28.5 2.0 %collective-permute-done.10.right_ref = f32[8,128]{1,0:T(8,128)S(1)} collective-permute-done((f32[8,128]{1,0:T(8,128)S(1)}, f32[8,128]{1,0:T(8,128)S(1)}, u32[]{:S(2)}, u32[]{:S(2)}) %collective-permute-start.10) | collective-permute-done | bytes 4128 | tf_op jit(solution)/shard_map/ppermute | solution.py:439
  30.6 2.6 %collective-permute-start.11 = (f32[8,128]{1,0:T(8,128)S(1)}, f32[8,128]{1,0:T(8,128)S(1)}, u32[]{:S(2)}, u32[]{:S(2)}) collective-permute-start(f32[8,128]{1,0:T(8,128)S(1)} %add_sums.1.rest_0_), channel_id=1, source_target_pairs={{0,2},{1,3},{2,0},{3,1},{4,6},{5,7},{6,4},{7,5},{8,10},{9,11},{10,... | collective-permute-start | bytes 12296 | tf_op jit(solution)/shard_map/ppermute | solution.py:439
  33.1 1.9 %collective-permute-done.11.rest_1_ = f32[8,128]{1,0:T(8,128)S(1)} collective-permute-done((f32[8,128]{1,0:T(8,128)S(1)}, f32[8,128]{1,0:T(8,128)S(1)}, u32[]{:S(2)}, u32[]{:S(2)}) %collective-permute-start.11) | collective-permute-done | bytes 4128 | tf_op jit(solution)/shard_map/ppermute | solution.py:439
  35.1 1.2 %state_grad.1 = (f32[256,128]{1,0:T(8,128)S(1)}, f32[256,128]{1,0:T(8,128)S(1)}, f32[256,128]{1,0:T(8,128)S(1)}, f32[256,128]{1,0:T(8,128)S(1)}) custom-call(f32[9,128]{1,0:T(8,128)S(1)} %get-tuple-element.45.facts_ref, bf16[512,1024]{1,0:T(8,128)(2,1)S(1)} %get-tuple-element.46.query_ref, bf16[512,1024]{1,0:T(8,128)(2,1)S(1)} %copy-done, ...), custom_call_target="tpu_custom_call" | custom-call | tf_op jit(solution)/shard_map/state_grad/pallas_call | solution.py:538
  36.3 0.9 %collective-permute-start.12 = (f32[256,128]{1,0:T(8,128)S(1)}, f32[256,128]{1,0:T(8,128)S(1)}, u32[]{:S(2)}, u32[]{:S(2)}) collective-permute-start(f32[256,128]{1,0:T(8,128)S(1)} %get-tuple-element.70), channel_id=1, source_target_pairs={{0,8},{4,12},{8,0},{12,4},{16,24},{20,28},{24,16},{28,20},{1,9},{5... | collective-permute-start | bytes 393224 | tf_op jit(solution)/shard_map/ppermute | solution.py:411
  37.1 1.5 %collective-permute-start.13 = (f32[256,128]{1,0:T(8,128)S(1)}, f32[256,128]{1,0:T(8,128)S(1)}, u32[]{:S(2)}, u32[]{:S(2)}) collective-permute-start(f32[256,128]{1,0:T(8,128)S(1)} %get-tuple-element.72), channel_id=1, source_target_pairs={{0,16},{4,20},{8,24},{12,28},{16,0},{20,4},{24,8},{28,12},{1,17},{... | collective-permute-start | bytes 393224 | tf_op jit(solution)/shard_map/ppermute | solution.py:411
  38.6 1.2 %collective-permute-start.14 = (f32[256,128]{1,0:T(8,128)S(1)}, f32[256,128]{1,0:T(8,128)S(1)}, u32[]{:S(2)}, u32[]{:S(2)}) collective-permute-start(f32[256,128]{1,0:T(8,128)S(1)} %get-tuple-element.73), channel_id=1, source_target_pairs={{0,24},{4,28},{8,16},{12,20},{16,8},{20,12},{24,0},{28,4},{1,25},{... | collective-permute-start | bytes 393224 | tf_op jit(solution)/shard_map/ppermute | solution.py:411
  39.8 0.0 collective-permute-start.15
  39.8 3.4 %local_backward.2 = (bf16[512,512]{1,0:T(8,128)(2,1)S(1)}, bf16[512,512]{1,0:T(8,128)(2,1)S(1)}, bf16[512,512]{1,0:T(8,128)(2,1)S(1)}, bf16[512,512]{1,0:T(8,128)(2,1)S(1)}, f32[8,128]{1,0:T(8,128)S(1)}) custom-call(f32[9,128]{1,0:T(8,128)S(1)} %get-tuple-element.45.facts_ref, bf16[512,1024]{1,0:T(8,128)(2,1)S(1)} %get-tuple-element.46.query_ref, ...), custom_call_target="tpu_custom_call" | custom-call | flops 1073741824 | bytes 4194304 | tf_op jit(solution)/shard_map/local_backward/pallas_call | solution.py:559
  43.2 0.0 collective-permute-done.12.piece_ref
  43.2 0.6 %collective-permute-start.16 = (f32[256,128]{1,0:T(8,128)S(1)}, f32[256,128]{1,0:T(8,128)S(1)}, u32[]{:S(2)}, u32[]{:S(2)}) collective-permute-start(f32[256,128]{1,0:T(8,128)S(1)} %after.9.rest_1_), channel_id=1, source_target_pairs={{0,4},{4,0},{8,12},{12,8},{16,20},{20,16},{24,28},{28,24},{1,5},{5... | collective-permute-start | bytes 393224 | tf_op jit(solution)/shard_map/ppermute | solution.py:417
  43.8 0.0 collective-permute-done.13.piece_ref
  43.8 0.1 collective-permute-start.17
  43.9 0.6 %collective-permute-done.14.piece_ref = f32[256,128]{1,0:T(8,128)S(1)} collective-permute-done((f32[256,128]{1,0:T(8,128)S(1)}, f32[256,128]{1,0:T(8,128)S(1)}, u32[]{:S(2)}, u32[]{:S(2)}) %collective-permute-start.14) | collective-permute-done | bytes 131104 | tf_op jit(solution)/shard_map/ppermute | solution.py:411
  44.5 0.0 collective-permute-start.18
  44.5 0.0 collective-permute-done.15.rest_4_
  44.5 0.2 collective-permute-done.16.rest_5_
  44.8 0.4 collective-permute-done.17.rest_6_
  45.1 0.7 %collective-permute-done.18.rest_7_ = f32[256,128]{1,0:T(8,128)S(1)} collective-permute-done((f32[256,128]{1,0:T(8,128)S(1)}, f32[256,128]{1,0:T(8,128)S(1)}, u32[]{:S(2)}, u32[]{:S(2)}) %collective-permute-start.18) | collective-permute-done | bytes 131104 | tf_op jit(solution)/shard_map/ppermute | solution.py:417
  45.9 0.3 mix_backward.1
  46.2 0.6 %collective-permute-start.19 = (f32[256,128]{1,0:T(8,128)S(1)}, f32[256,128]{1,0:T(8,128)S(1)}, u32[]{:S(2)}, u32[]{:S(2)}) collective-permute-start(f32[256,128]{1,0:T(8,128)S(1)} %get-tuple-element.75), channel_id=1, source_target_pairs={{0,8},{4,12},{8,0},{12,4},{16,24},{20,28},{24,16},{28,20},{1,9},{5... | collective-permute-start | bytes 393224 | tf_op jit(solution)/shard_map/ppermute | solution.py:411
  46.8 1.2 %collective-permute-start.20 = (f32[256,128]{1,0:T(8,128)S(1)}, f32[256,128]{1,0:T(8,128)S(1)}, u32[]{:S(2)}, u32[]{:S(2)}) collective-permute-start(f32[256,128]{1,0:T(8,128)S(1)} %get-tuple-element.76), channel_id=1, source_target_pairs={{0,16},{4,20},{8,24},{12,28},{16,0},{20,4},{24,8},{28,12},{1,17},{... | collective-permute-start | bytes 393224 | tf_op jit(solution)/shard_map/ppermute | solution.py:411
  48.0 1.7 %collective-permute-start.21 = (f32[256,128]{1,0:T(8,128)S(1)}, f32[256,128]{1,0:T(8,128)S(1)}, u32[]{:S(2)}, u32[]{:S(2)}) collective-permute-start(f32[256,128]{1,0:T(8,128)S(1)} %get-tuple-element.77), channel_id=1, source_target_pairs={{0,24},{4,28},{8,16},{12,20},{16,8},{20,12},{24,0},{28,4},{1,25},{... | collective-permute-start | bytes 393224 | tf_op jit(solution)/shard_map/ppermute | solution.py:411
  49.7 4.4 %local_backward.3 = (bf16[512,1024]{1,0:T(8,128)(2,1)}, bf16[512,1024]{1,0:T(8,128)(2,1)}, bf16[512,512]{1,0:T(8,128)(2,1)S(1)}, bf16[512,512]{1,0:T(8,128)(2,1)S(1)}) custom-call(f32[9,128]{1,0:T(8,128)S(1)} %get-tuple-element.45.facts_ref, bf16[512,1024]{1,0:T(8,128)(2,1)S(1)} %get-tuple-element.46.query_ref, ...), custom_call_target="tpu_custom_call" | custom-call | flops 1073741824 | bytes 4194304 | tf_op jit(solution)/shard_map/local_backward/pallas_call | solution.py:559
  54.1 0.0 collective-permute-done.19.rest_5_
  54.1 0.7 %collective-permute-done.20.rest_6_ = f32[256,128]{1,0:T(8,128)S(1)} collective-permute-done((f32[256,128]{1,0:T(8,128)S(1)}, f32[256,128]{1,0:T(8,128)S(1)}, u32[]{:S(2)}, u32[]{:S(2)}) %collective-permute-start.20) | collective-permute-done | bytes 131104 | tf_op jit(solution)/shard_map/ppermute | solution.py:411
  54.8 0.0 collective-permute-done.21.rest_7_
  54.8 2.1 %finish.1 = (bf16[512,1024]{1,0:T(8,128)(2,1)}, bf16[512,1024]{1,0:T(8,128)(2,1)}) custom-call(f32[9,128]{1,0:T(8,128)S(1)} %get-tuple-element.45.facts_ref, bf16[512,1024]{1,0:T(8,128)(2,1)S(1)} %get-tuple-element.43.key_ref, bf16[512,1024]{1,0:T(8,128)(2,1)S(1)} %get-tuple-element.44.value_ref, bf16[512,512]{1,0:T(8,128)(2,1)S(1)} %get-tuple-element.65.rest_0_, ...), custom_call_target="tpu_custom_call" | custom-call | tf_op jit(solution)/shard_map/finish/pallas_call | solution.py:577
  (8 shorter events, 0.0 us)
Async XLA Ops:
  0.6 1.9 %copy-start.2 = (s32[8]{0:T(128)S(1)}, s32[8]{0:T(128)}, u32[]{:S(2)}) copy-start(s32[8]{0:T(128)} %length_ref.1) | copy-start | bytes 100
  0.6 1.9 %copy-start.3 = (f32[8]{0:T(128)S(1)}, f32[8]{0:T(128)}, u32[]{:S(2)}) copy-start(f32[8]{0:T(128)} %rate_ref.1) | copy-start | bytes 100
  0.7 7.4 %copy-start.4 = (s32[8]{0:T(128)S(1)}, s32[8]{0:T(128)}, u32[]{:S(2)}) copy-start(s32[8]{0:T(128)} %parent_ref.1) | copy-start | bytes 100
  3.5 7.3 %collective-permute-start = (f32[256,128]{1,0:T(8,128)S(1)}, f32[256,128]{1,0:T(8,128)S(1)}, u32[]{:S(2)}, u32[]{:S(2)}) collective-permute-start(f32[256,128]{1,0:T(8,128)S(1)} %get-tuple-element.51), channel_id=1, source_target_pairs={{0,8},{4,12},{8,0},{12,4},{16,24},{20,28},{24,16},{28,20},{1,9},{5... | collective-permute-start | bytes 393224 | tf_op jit(solution)/shard_map/ppermute | solution.py:411
  6.5 7.8 %collective-permute-start.1 = (f32[256,128]{1,0:T(8,128)S(1)}, f32[256,128]{1,0:T(8,128)S(1)}, u32[]{:S(2)}, u32[]{:S(2)}) collective-permute-start(f32[256,128]{1,0:T(8,128)S(1)} %get-tuple-element.52), channel_id=1, source_target_pairs={{0,16},{4,20},{8,24},{12,28},{16,0},{20,4},{24,8},{28,12},{1,17},{... | collective-permute-start | bytes 393224 | tf_op jit(solution)/shard_map/ppermute | solution.py:411
  8.1 6.3 %collective-permute-start.2 = (f32[256,128]{1,0:T(8,128)S(1)}, f32[256,128]{1,0:T(8,128)S(1)}, u32[]{:S(2)}, u32[]{:S(2)}) collective-permute-start(f32[256,128]{1,0:T(8,128)S(1)} %get-tuple-element.53), channel_id=1, source_target_pairs={{0,24},{4,28},{8,16},{12,20},{16,8},{20,12},{24,0},{28,4},{1,25},{... | collective-permute-start | bytes 393224 | tf_op jit(solution)/shard_map/ppermute | solution.py:411
  8.1 6.8 %collective-permute-start.3 = (f32[256,128]{1,0:T(8,128)S(1)}, f32[256,128]{1,0:T(8,128)S(1)}, u32[]{:S(2)}, u32[]{:S(2)}) collective-permute-start(f32[256,128]{1,0:T(8,128)S(1)} %get-tuple-element.50.rest_0_), channel_id=1, source_target_pairs={{0,4},{4,0},{8,12},{12,8},{16,20},{20,16},{24,28},{28,24},{1,5},{5... | collective-permute-start | bytes 393224 | tf_op jit(solution)/shard_map/ppermute | solution.py:417
  10.9 14.8 %copy-start = (bf16[512,1024]{1,0:T(8,128)(2,1)S(1)}, bf16[512,1024]{1,0:T(8,128)(2,1)}, u32[]{:S(2)}) copy-start(bf16[512,1024]{1,0:T(8,128)(2,1)} %upstream_ref.7) | copy-start | bytes 3145732
  10.9 14.8 %copy-start.1 = (f32[1024]{0:T(1024)S(1)}, f32[1024]{0:T(1024)}, u32[]{:S(2)}) copy-start(f32[1024]{0:T(1024)} %param.12) | copy-start | bytes 12292
  10.9 3.9 %collective-permute-start.4 = (f32[256,128]{1,0:T(8,128)S(1)}, f32[256,128]{1,0:T(8,128)S(1)}, u32[]{:S(2)}, u32[]{:S(2)}) collective-permute-start(f32[256,128]{1,0:T(8,128)S(1)} %after.6.rest_1_), channel_id=1, source_target_pairs={{0,4},{4,0},{8,12},{12,8},{16,20},{20,16},{24,28},{28,24},{1,5},{5... | collective-permute-start | bytes 393224 | tf_op jit(solution)/shard_map/ppermute | solution.py:417
  14.3 1.3 %collective-permute-start.5 = (f32[256,128]{1,0:T(8,128)S(1)}, f32[256,128]{1,0:T(8,128)S(1)}, u32[]{:S(2)}, u32[]{:S(2)}) collective-permute-start(f32[256,128]{1,0:T(8,128)S(1)} %after.7.rest_2_), channel_id=1, source_target_pairs={{0,4},{4,0},{8,12},{12,8},{16,20},{20,16},{24,28},{28,24},{1,5},{5... | collective-permute-start | bytes 393224 | tf_op jit(solution)/shard_map/ppermute | solution.py:417
  14.3 1.5 %collective-permute-start.6 = (f32[256,128]{1,0:T(8,128)S(1)}, f32[256,128]{1,0:T(8,128)S(1)}, u32[]{:S(2)}, u32[]{:S(2)}) collective-permute-start(f32[256,128]{1,0:T(8,128)S(1)} %after.8.rest_3_), channel_id=1, source_target_pairs={{0,4},{4,0},{8,12},{12,8},{16,20},{20,16},{24,28},{28,24},{1,5},{5... | collective-permute-start | bytes 393224 | tf_op jit(solution)/shard_map/ppermute | solution.py:417
  16.1 6.4 %collective-permute-start.7 = (f32[256,128]{1,0:T(8,128)S(1)}, f32[256,128]{1,0:T(8,128)S(1)}, u32[]{:S(2)}, u32[]{:S(2)}) collective-permute-start(f32[256,128]{1,0:T(8,128)S(1)} %get-tuple-element.55), channel_id=1, source_target_pairs={{0,8},{4,12},{8,0},{12,4},{16,24},{20,28},{24,16},{28,20},{1,9},{5... | collective-permute-start | bytes 393224 | tf_op jit(solution)/shard_map/ppermute | solution.py:411
  17.3 6.8 %collective-permute-start.8 = (f32[256,128]{1,0:T(8,128)S(1)}, f32[256,128]{1,0:T(8,128)S(1)}, u32[]{:S(2)}, u32[]{:S(2)}) collective-permute-start(f32[256,128]{1,0:T(8,128)S(1)} %get-tuple-element.56), channel_id=1, source_target_pairs={{0,16},{4,20},{8,24},{12,28},{16,0},{20,4},{24,8},{28,12},{1,17},{... | collective-permute-start | bytes 393224 | tf_op jit(solution)/shard_map/ppermute | solution.py:411
  18.3 7.4 %collective-permute-start.9 = (f32[256,128]{1,0:T(8,128)S(1)}, f32[256,128]{1,0:T(8,128)S(1)}, u32[]{:S(2)}, u32[]{:S(2)}) collective-permute-start(f32[256,128]{1,0:T(8,128)S(1)} %get-tuple-element.57), channel_id=1, source_target_pairs={{0,24},{4,28},{8,16},{12,20},{16,8},{20,12},{24,0},{28,4},{1,25},{... | collective-permute-start | bytes 393224 | tf_op jit(solution)/shard_map/ppermute | solution.py:411
  26.9 3.7 %collective-permute-start.10 = (f32[8,128]{1,0:T(8,128)S(1)}, f32[8,128]{1,0:T(8,128)S(1)}, u32[]{:S(2)}, u32[]{:S(2)}) collective-permute-start(f32[8,128]{1,0:T(8,128)S(1)} %get-tuple-element.60.left_ref), channel_id=1, source_target_pairs={{0,1},{1,0},{2,3},{3,2},{4,5},{5,4},{6,7},{7,6},{8,9},{9,8},{10,11... | collective-permute-start | bytes 12296 | tf_op jit(solution)/shard_map/ppermute | solution.py:439
  30.6 4.5 %collective-permute-start.11 = (f32[8,128]{1,0:T(8,128)S(1)}, f32[8,128]{1,0:T(8,128)S(1)}, u32[]{:S(2)}, u32[]{:S(2)}) collective-permute-start(f32[8,128]{1,0:T(8,128)S(1)} %add_sums.1.rest_0_), channel_id=1, source_target_pairs={{0,2},{1,3},{2,0},{3,1},{4,6},{5,7},{6,4},{7,5},{8,10},{9,11},{10,... | collective-permute-start | bytes 12296 | tf_op jit(solution)/shard_map/ppermute | solution.py:439
  36.3 6.9 %collective-permute-start.12 = (f32[256,128]{1,0:T(8,128)S(1)}, f32[256,128]{1,0:T(8,128)S(1)}, u32[]{:S(2)}, u32[]{:S(2)}) collective-permute-start(f32[256,128]{1,0:T(8,128)S(1)} %get-tuple-element.70), channel_id=1, source_target_pairs={{0,8},{4,12},{8,0},{12,4},{16,24},{20,28},{24,16},{28,20},{1,9},{5... | collective-permute-start | bytes 393224 | tf_op jit(solution)/shard_map/ppermute | solution.py:411
  37.1 6.6 %collective-permute-start.13 = (f32[256,128]{1,0:T(8,128)S(1)}, f32[256,128]{1,0:T(8,128)S(1)}, u32[]{:S(2)}, u32[]{:S(2)}) collective-permute-start(f32[256,128]{1,0:T(8,128)S(1)} %get-tuple-element.72), channel_id=1, source_target_pairs={{0,16},{4,20},{8,24},{12,28},{16,0},{20,4},{24,8},{28,12},{1,17},{... | collective-permute-start | bytes 393224 | tf_op jit(solution)/shard_map/ppermute | solution.py:411
  38.6 5.9 %collective-permute-start.14 = (f32[256,128]{1,0:T(8,128)S(1)}, f32[256,128]{1,0:T(8,128)S(1)}, u32[]{:S(2)}, u32[]{:S(2)}) collective-permute-start(f32[256,128]{1,0:T(8,128)S(1)} %get-tuple-element.73), channel_id=1, source_target_pairs={{0,24},{4,28},{8,16},{12,20},{16,8},{20,12},{24,0},{28,4},{1,25},{... | collective-permute-start | bytes 393224 | tf_op jit(solution)/shard_map/ppermute | solution.py:411
  39.8 4.7 %collective-permute-start.15 = (f32[256,128]{1,0:T(8,128)S(1)}, f32[256,128]{1,0:T(8,128)S(1)}, u32[]{:S(2)}, u32[]{:S(2)}) collective-permute-start(f32[256,128]{1,0:T(8,128)S(1)} %get-tuple-element.69.rest_0_), channel_id=1, source_target_pairs={{0,4},{4,0},{8,12},{12,8},{16,20},{20,16},{24,28},{28,24},{1,5},{5... | collective-permute-start | bytes 393224 | tf_op jit(solution)/shard_map/ppermute | solution.py:417
  43.2 1.6 %collective-permute-start.16 = (f32[256,128]{1,0:T(8,128)S(1)}, f32[256,128]{1,0:T(8,128)S(1)}, u32[]{:S(2)}, u32[]{:S(2)}) collective-permute-start(f32[256,128]{1,0:T(8,128)S(1)} %after.9.rest_1_), channel_id=1, source_target_pairs={{0,4},{4,0},{8,12},{12,8},{16,20},{20,16},{24,28},{28,24},{1,5},{5... | collective-permute-start | bytes 393224 | tf_op jit(solution)/shard_map/ppermute | solution.py:417
  43.8 1.3 %collective-permute-start.17 = (f32[256,128]{1,0:T(8,128)S(1)}, f32[256,128]{1,0:T(8,128)S(1)}, u32[]{:S(2)}, u32[]{:S(2)}) collective-permute-start(f32[256,128]{1,0:T(8,128)S(1)} %after.10.rest_2_), channel_id=1, source_target_pairs={{0,4},{4,0},{8,12},{12,8},{16,20},{20,16},{24,28},{28,24},{1,5},{5... | collective-permute-start | bytes 393224 | tf_op jit(solution)/shard_map/ppermute | solution.py:417
  44.5 1.3 %collective-permute-start.18 = (f32[256,128]{1,0:T(8,128)S(1)}, f32[256,128]{1,0:T(8,128)S(1)}, u32[]{:S(2)}, u32[]{:S(2)}) collective-permute-start(f32[256,128]{1,0:T(8,128)S(1)} %after.11.rest_3_), channel_id=1, source_target_pairs={{0,4},{4,0},{8,12},{12,8},{16,20},{20,16},{24,28},{28,24},{1,5},{5... | collective-permute-start | bytes 393224 | tf_op jit(solution)/shard_map/ppermute | solution.py:417
  46.2 7.9 %collective-permute-start.19 = (f32[256,128]{1,0:T(8,128)S(1)}, f32[256,128]{1,0:T(8,128)S(1)}, u32[]{:S(2)}, u32[]{:S(2)}) collective-permute-start(f32[256,128]{1,0:T(8,128)S(1)} %get-tuple-element.75), channel_id=1, source_target_pairs={{0,8},{4,12},{8,0},{12,4},{16,24},{20,28},{24,16},{28,20},{1,9},{5... | collective-permute-start | bytes 393224 | tf_op jit(solution)/shard_map/ppermute | solution.py:411
  46.8 8.1 %collective-permute-start.20 = (f32[256,128]{1,0:T(8,128)S(1)}, f32[256,128]{1,0:T(8,128)S(1)}, u32[]{:S(2)}, u32[]{:S(2)}) collective-permute-start(f32[256,128]{1,0:T(8,128)S(1)} %get-tuple-element.76), channel_id=1, source_target_pairs={{0,16},{4,20},{8,24},{12,28},{16,0},{20,4},{24,8},{28,12},{1,17},{... | collective-permute-start | bytes 393224 | tf_op jit(solution)/shard_map/ppermute | solution.py:411
  48.0 6.8 %collective-permute-start.21 = (f32[256,128]{1,0:T(8,128)S(1)}, f32[256,128]{1,0:T(8,128)S(1)}, u32[]{:S(2)}, u32[]{:S(2)}) collective-permute-start(f32[256,128]{1,0:T(8,128)S(1)} %get-tuple-element.77), channel_id=1, source_target_pairs={{0,24},{4,28},{8,16},{12,20},{16,8},{20,12},{24,0},{28,4},{1,25},{... | collective-permute-start | bytes 393224 | tf_op jit(solution)/shard_map/ppermute | solution.py:411

commit v2 on v1

v2 whole, which is shorter than its diff:
```python
import functools

import jax
import jax.numpy as jnp
from jax import lax
from jax.experimental import pallas as pl
from jax.experimental.pallas import tpu as pltpu
from jax.sharding import PartitionSpec as P

norm_eps = 1e-05
f32 = jnp.float32
bf16 = jnp.bfloat16
VMEM_LIMIT = 40 * 1024 * 1024
FIRST_LIMIT = 504 * 1024 * 1024 // 10

SMEM_SPEC = pl.BlockSpec(memory_space=pltpu.SMEM)
VMEM_SPEC = pl.BlockSpec(memory_space=pltpu.VMEM)
ANY_SPEC = pl.BlockSpec(memory_space=pl.ANY)


def nn(a, b):
    return lax.dot_general(a, b, (((1,), (0,)), ((), ())), preferred_element_type=f32)


def nt(a, b):
    return lax.dot_general(a, b, (((1,), (1,)), ((), ())), preferred_element_type=f32)


def tn(a, b):
    return lax.dot_general(a, b, (((0,), (0,)), ((), ())), preferred_element_type=f32)


def side_by_side(parts):
    return jnp.concatenate(parts, axis=1)


def block_diagonal(blocks):
    zero = jnp.zeros_like(blocks[0])
    return jnp.concatenate([side_by_side([block if i == j else zero for j in range(len(blocks))]) for i, block in enumerate(blocks)], axis=0)


def row_index(rows, columns):
    return lax.broadcasted_iota(jnp.int32, (rows, columns), 0)


def key_scale(rows, size, length, rate):
    slot = row_index(rows, size).astype(f32)
    remaining = (length - 1) - slot
    return jnp.where(remaining >= 0, jnp.exp(-rate * remaining), 0.0)


def query_scale(rows, size, rate):
    return jnp.exp(-rate * (row_index(rows, size) + 1).astype(f32))


def masked_rows(array, length):
    return jnp.where(row_index(*array.shape) < length, array, jnp.zeros_like(array))


def column(row):
    count = row.shape[1]
    return jnp.broadcast_to(row, (count, count)).T


def add_to(totals, index, part):
    totals[index] = part if totals[index] is None else totals[index] + part


def core_offset(slot, core):
    crossed = (slot & ~3) | ((slot & 1) << 1) | ((slot & 2) >> 1)
    return slot + core * (crossed - slot)


class Layout:
    def __init__(self, rows, wide, size, chips):
        self.rows, self.wide, self.size, self.chips = rows, wide, size, chips
        self.heads = wide // size
        self.piece = wide // chips
        self.each = self.piece // size
        self.tile = min(256, rows)
        self.count = rows // self.tile

    def chip(self, slot, sibling=0):
        own = lax.axis_index("seg")
        crossing = False
        return (own // 2) ^ (core_offset(slot, (own % 2) ^ sibling) if crossing else slot)

    def head(self, place):
        if not self.each:
            return place
        return self.chip(place // self.each) * self.each + place % self.each

    def span(self, place):
        if not self.each:
            return pl.ds(place * self.size, self.size)
        return pl.ds(pl.multiple_of(self.head(place) * self.size, self.size), self.size)

    def near(self, places, place):
        at = list(places).index(place)
        return slice(at * self.size, (at + 1) * self.size)

    def places(self, offsets):
        if not self.each:
            return list(range(self.heads)) if 0 in offsets else []
        return [offset * self.each + at for offset in offsets for at in range(self.each)]

    def pairs(self, places):
        return [places[at:at + 2] for at in range(0, len(places), 2)]

    def state(self, pieces, place):
        if self.each:
            at = place % self.each
            return pieces[place // self.each][at * self.size:(at + 1) * self.size, :]
        first = place * self.size // self.piece
        parts = []
        for owner in range(first, first + self.size // self.piece):
            part = pieces[0][...]
            for offset in range(1, self.chips):
                part = jnp.where(self.chip(offset) == owner, pieces[offset][...], part)
            parts.append(part)
        return jnp.concatenate(parts, axis=0)


def near_kernel(key_any, value_any, query_any, key_ref, value_ref, query_ref, sems):
    moves = ((key_any, key_ref), (value_any, value_ref), (query_any, query_ref))
    copies = [pltpu.make_async_copy(source, target, sems.at[at]) for at, (source, target) in enumerate(moves)]
    for copy in copies:
        copy.start()
    for copy in copies:
        copy.wait()


def write_states(layout, offsets, left, right, outs, whole):
    size = layout.size
    if layout.each:
        places = layout.places(offsets)
        targets = [(outs[place // size_of], place % size_of) for place, size_of in ((at, layout.each) for at in range(len(places)))]
    else:
        places = list(range(layout.heads))
        targets = [(whole, place) for place in places]
    group = min(2, len(places))
    for first in range(0, len(places), group):
        chosen = places[first:first + group]
        both = tn(
            jnp.concatenate([left(place) for place in chosen], axis=1),
            jnp.concatenate([right(place) for place in chosen], axis=1),
        )
        for at in range(len(chosen)):
            inner = slice(at * size, (at + 1) * size)
            target, row = targets[first + at]
            target[row * size:(row + 1) * size, :] = both[inner, inner]
    if not layout.each:
        for offset, out in zip(offsets, outs):
            begin = pl.multiple_of(layout.chip(offset) * layout.piece, layout.piece)
            out[...] = whole[pl.ds(begin, layout.piece), :]


def state_kernel(layout, offsets, length_ref, rate_ref, key_ref, value_ref, *rest):
    outs, whole = rest[:len(offsets)], rest[len(offsets)]
    rows, size = layout.rows, layout.size
    lengths = length_ref[...].astype(f32)
    mine = lax.broadcasted_iota(jnp.int32, lengths.shape, 1) == lax.axis_index("seg")
    length = jnp.sum(jnp.where(mine, lengths, 0.0), axis=1, keepdims=True)
    rates = rate_ref[...]
    lane = lax.broadcasted_iota(jnp.int32, rates.shape, 1)

    def left(place):
        return key_ref[:, layout.span(place)]

    def right(place):
        rate = jnp.sum(jnp.where(lane == layout.head(place), rates, 0.0), axis=1, keepdims=True)
        return (value_ref[:, layout.span(place)].astype(f32) * key_scale(rows, size, length, rate)).astype(bf16)

    write_states(layout, offsets, left, right, outs, whole)


def decay_tiles(tile, rate, count, transposed):
    u = lax.broadcasted_iota(jnp.int32, (tile, tile), 1 if transposed else 0)
    w = lax.broadcasted_iota(jnp.int32, (tile, tile), 0 if transposed else 1)
    base = jnp.exp((w - u).astype(f32) * rate)
    tiles = [jnp.where(u >= w, base, 0.0)]
    for gap in range(1, count):
        tiles.append(base * jnp.exp(jnp.full((1, tile), -(gap * tile), f32) * rate))
    return tiles


def tree_distances(length_ref, parent_ref, table, count):
    for at in range(count):
        table[at] = jnp.int32(-1)

    def one(block, carry):
        above = parent_ref[block]
        passed = length_ref[jnp.maximum(above, 0)]
        for at in range(count):
            distance = table[(above + 1) * count + at]
            distance = jnp.where(distance >= 0, distance + passed, distance)
            table[(block + 1) * count + at] = jnp.where(above == at, 0, distance)
        return carry

    lax.fori_loop(0, count, one, 0)


def weight_table(layout, length_ref, parent_ref, rate_ref, distances, table_ref):
    own = lax.axis_index("seg")
    chip, core = own // 2, own % 2
    chips, size, piece = layout.chips, layout.size, layout.piece
    count = 2 * chips
    tree_distances(length_ref, parent_ref, distances, count)
    row = row_index(8, size)
    rates = jnp.full((8, size), rate_ref[(chip * piece) // size], f32)
    for at in range(1, piece // size):
        rates = jnp.where(row == at, rate_ref[(chip * piece) // size + at], rates)
    for backward in range(2):
        for target in range(chips):
            wanted = layout.chip(target) * 2 + core
            for offset in range(chips):
                for sibling in range(2):
                    source = layout.chip(offset, sibling) * 2 + (core ^ sibling)
                    place = (source + 1) * count + wanted if backward else (wanted + 1) * count + source
                    distance = distances[place].astype(f32)
                    linked = (distance >= 0.0).astype(f32)
                    slot = ((backward * chips + target) * chips + offset) * 2 + sibling
                    table_ref[slot] = jnp.exp(rates * -distance) * linked


def local_head(layout, rate, query, key, value):
    tile, count = layout.tile, layout.count
    decays = decay_tiles(tile, rate, count, False)
    totals = [None] * count
    for i in range(count):
        for j in range(i + 1):
            w_span = slice(j * tile, (j + 1) * tile)
            scores = nt(query[i * tile:(i + 1) * tile], key[w_span])
            weighted = (scores * decays[i - j]).astype(bf16)
            add_to(totals, i, nn(weighted, value[w_span]))
    return jnp.concatenate(totals, axis=0)


def local_kernel(layout, places, length_ref, parent_ref, rate_ref, query_ref, key_ref, value_ref, out_ref, masked_ref, scaled_ref, table_ref, facts_ref, distances):
    length = length_ref[lax.axis_index("seg")]
    weight_table(layout, length_ref, parent_ref, rate_ref, distances, table_ref)
    heads, size = layout.heads, layout.size
    for place in range(heads):
        facts_ref[place:place + 1, :] = jnp.full((1, size), rate_ref[layout.head(place)], f32)
    facts_ref[heads:, :] = jnp.full((1, size), length.astype(f32), f32)
    masked_ref[...] = masked_rows(query_ref[...], length)
    for place in range(heads):
        span = layout.span(place)
        scale = query_scale(layout.rows, size, rate_ref[layout.head(place)])
        scaled_ref[:, span] = (masked_ref[:, span].astype(f32) * scale).astype(bf16)
    for place in places:
        span = layout.span(place)
        rate = rate_ref[layout.head(place)]
        out_ref[:, layout.near(places, place)] = local_head(layout, rate, masked_ref[:, span], key_ref[:, span], value_ref[:, span])


def tile_pairs(count):
    return [(i, j) for j in range(count) for i in range(j, count)]


def weighted_kernel(layout, places, facts_ref, query_ref, key_ref, value_ref, out_ref, local_ref, key_end_ref, value_end_ref):
    tile = layout.tile
    length = facts_ref[layout.heads:, :]
    for place in range(layout.heads):
        span = layout.span(place)
        scale = key_scale(layout.rows, layout.size, length, facts_ref[place:place + 1, :])
        key_end_ref[:, span] = (key_ref[:, span].astype(f32) * scale).astype(bf16)
        value_end_ref[:, span] = (value_ref[:, span].astype(f32) * scale).astype(bf16)
        rate = facts_ref[place:place + 1, :1]
        query, key = query_ref[:, span], key_ref[:, span]
        decays = decay_tiles(tile, rate, layout.count, True)
        for at, (i, j) in enumerate(tile_pairs(layout.count)):
            scores = nt(key[j * tile:(j + 1) * tile], query[i * tile:(i + 1) * tile])
            out_ref[place, at] = (scores * decays[i - j]).astype(bf16)
        if place in places:
            local_ref[:, layout.near(places, place)] = local_head(layout, rate, query, key, value_ref[:, span])


def mix_kernel(layout, backward, targets, table_ref, *rest):
    chips, size, piece = layout.chips, layout.size, layout.piece
    mine, other, outs = rest[:chips], rest[chips:2 * chips], rest[len(rest) - len(targets):]
    part = min(piece, size)
    for at in range(piece // part):
        span = slice(at * part, (at + 1) * part)
        totals = [None] * len(targets)
        for offset in range(chips):
            for sibling, sources in ((0, mine), (1, other)):
                data = sources[offset][span, :]
                for index, target in enumerate(targets):
                    slot = ((backward * chips + target) * chips + offset) * 2 + sibling
                    add_to(totals, index, table_ref[slot, at:at + 1, :] * data)
        for out, total in zip(outs, totals):
            out[span, :] = total


def attend_kernel(layout, places, last, scaled_ref, upstream_ref, gain_ref, local_ref, *rest):
    pieces, rest = rest[:layout.chips], rest[layout.chips:]
    rows, size = layout.rows, layout.size
    if last is None:
        attended_ref, squares_ref, inners_ref = rest
        squares = jnp.zeros((rows, size), f32)
        inners = jnp.zeros((rows, size), f32)
    else:
        *before, attended_ref, sums_ref = rest
        squares, inners = (before[0][...], before[1][...]) if before else (jnp.zeros((rows, size), f32),) * 2
    for chosen in layout.pairs(places):
        carried = block_diagonal([layout.state(pieces, place).astype(bf16) for place in chosen])
        both = nn(side_by_side([scaled_ref[:, layout.span(place)] for place in chosen]), carried)
        for at, place in enumerate(chosen):
            span, near = layout.span(place), layout.near(places, place)
            attended = local_ref[:, near] + both[:, at * size:(at + 1) * size]
            attended_ref[:, near] = attended
            scaled = upstream_ref[:, span].astype(f32) * gain_ref[:, span]
            squares = squares + attended * attended
            inners = inners + scaled * attended
    if last is None:
        squares_ref[...] = squares
        inners_ref[...] = inners
        return
    groups = rows // size
    for at in range(groups):
        span = slice(at * size, (at + 1) * size)
        sums_ref[at:at + 1, :] = jnp.sum(squares[span].T, axis=0, keepdims=True)
        sums_ref[groups + at:groups + at + 1, :] = jnp.sum(inners[span].T, axis=0, keepdims=True)


def norm_columns(sum_refs, width, inverse_ref, factor_ref):
    total = sum_refs[0][...]
    for ref in sum_refs[1:]:
        total = total + ref[...]
    groups = total.shape[0] // 2
    size = total.shape[1]
    inverse = lax.rsqrt(total[:groups] / width + norm_eps)
    factor = inverse * inverse * inverse * total[groups:] / width
    for at in range(groups):
        span = slice(at * size, (at + 1) * size)
        inverse_ref[span, :] = column(inverse[at:at + 1])
        factor_ref[span, :] = column(factor[at:at + 1])


def pick(layout, groups, refs, place, rows=slice(None)):
    for places, ref in zip(groups, refs):
        if place in places:
            return ref[rows, layout.near(places, place)]
    raise ValueError(place)


def state_grad_kernel(layout, groups, offsets, sums, width, facts_ref, query_ref, upstream_ref, gain_ref, *rest):
    attended_refs, rest = rest[:len(groups)], rest[len(groups):]
    if sums:
        sum_refs, rest = rest[:sums], rest[sums:]
        outs, (inverse_ref, factor_ref, whole) = rest[:len(offsets)], rest[len(offsets):]
        norm_columns(sum_refs, width, inverse_ref, factor_ref)
    else:
        inverse_ref, factor_ref, *outs, whole = rest
    rows, size = layout.rows, layout.size
    inverse = inverse_ref[...]
    factor = factor_ref[...]

    def left(place):
        return query_ref[:, layout.span(place)]

    def right(place):
        span = layout.span(place)
        scaled = upstream_ref[:, span].astype(f32) * gain_ref[:, span]
        grad = inverse * scaled - factor * pick(layout, groups, attended_refs, place)
        return (grad * query_scale(rows, size, facts_ref[place:place + 1, :])).astype(bf16)

    write_states(layout, offsets, left, right, outs, whole)


def send(layout, places, place, sources, targets, sems, copies):
    for source, target in zip(sources, targets):
        near = source.at[:, layout.near(places, place)]
        copies.append(pltpu.make_async_copy(near, target.at[:, layout.span(place)], sems.at[len(copies)]))
        copies[-1].start()


def send_all(layout, kept, earlier, targets, sems, copies):
    for at, places in enumerate(kept):
        for place in places:
            send(layout, places, place, earlier[2 * at:2 * at + 2], targets, sems, copies)


def backward_kernel(layout, groups, places, kept, last, facts_ref, query_ref, key_ref, value_ref, upstream_ref, weighted_ref, gain_ref, inverse_ref, factor_ref, *rest):
    attended_refs, rest = rest[:len(groups)], rest[len(groups):]
    pieces, rest = rest[:layout.chips], rest[layout.chips:]
    earlier, rest = rest[:2 * len(kept)], rest[2 * len(kept):]
    rows, size, tile, count = layout.rows, layout.size, layout.tile, layout.count
    copies = []
    if last:
        out_any, query_grad_any, key_grad_ref, value_grad_ref, out_ref, query_grad_ref, sems = rest
        targets = (out_any, query_grad_any)
        send_all(layout, kept, earlier, targets, sems, copies)
    else:
        out_ref, query_grad_ref, key_grad_ref, value_grad_ref, token_ref = rest
        token_ref[...] = jnp.zeros_like(token_ref)
    used = row_index(rows, size).astype(f32) < facts_ref[layout.heads:, :]
    for place in places:
        span, near = layout.span(place), layout.near(places, place)
        rate = facts_ref[place:place + 1, :]
        query = query_ref[:, span]
        key = key_ref[:, span]
        value = value_ref[:, span]
        gain = gain_ref[:, span]
        inverse = inverse_ref[...]
        attended = pick(layout, groups, attended_refs, place)
        out_ref[:, near] = (attended * inverse * gain).astype(bf16)
        scaled = upstream_ref[:, span].astype(f32) * gain
        grad = (inverse * scaled - factor_ref[...] * attended).astype(bf16)
        carried = layout.state(pieces, place).astype(bf16)
        query_grad = nt(grad, carried) * query_scale(rows, size, rate)
        decays = decay_tiles(tile, rate[:, :1], count, True)
        query_totals, key_totals, value_totals = [None] * count, [None] * count, [None] * count
        for at, (i, j) in enumerate(tile_pairs(count)):
            u_span, w_span = slice(i * tile, (i + 1) * tile), slice(j * tile, (j + 1) * tile)
            score_grad = (nt(value[w_span], grad[u_span]) * decays[i - j]).astype(bf16)
            add_to(value_totals, j, nn(weighted_ref[place, at], grad[u_span]))
            add_to(key_totals, j, nn(score_grad, query[u_span]))
            add_to(query_totals, i, tn(score_grad, key[w_span]))
        key_grad_ref[:, near] = jnp.concatenate(key_totals, axis=0).astype(bf16)
        value_grad_ref[:, near] = jnp.concatenate(value_totals, axis=0).astype(bf16)
        query_grad = query_grad + jnp.concatenate(query_totals, axis=0)
        query_grad_ref[:, near] = jnp.where(used, query_grad, 0.0).astype(bf16)
        if last:
            send(layout, places, place, (out_ref, query_grad_ref), targets, sems, copies)
    for copy in copies:
        copy.wait()


def finish_kernel(layout, groups, places, first, last, key_end_ref, value_end_ref, *rest):
    key_locals, value_locals, rest = rest[:len(groups)], rest[len(groups):2 * len(groups)], rest[2 * len(groups):]
    pieces, rest = rest[:layout.chips], rest[layout.chips + (0 if first else 2):]
    key_full, value_full, *rest = rest
    half = layout.rows // 2 if last else layout.rows
    states = [layout.state(pieces, place).astype(bf16) for place in places]
    copies = []
    for begin in range(0, layout.rows, half):
        part = slice(begin, begin + half)
        for state_grad, place in zip(states, places):
            span = layout.span(place)
            key_part = nt(value_end_ref[part, span], state_grad)
            value_part = nn(key_end_ref[part, span], state_grad)
            key_full[part, span] = (pick(layout, groups, key_locals, place, part).astype(f32) + key_part).astype(bf16)
            value_full[part, span] = (pick(layout, groups, value_locals, place, part).astype(f32) + value_part).astype(bf16)
        if last:
            key_any, value_any, sems = rest
            for source, target in ((key_full, key_any), (value_full, value_any)):
                copies.append(pltpu.make_async_copy(source.at[part, :], target.at[part, :], sems.at[len(copies)]))
                copies[-1].start()
    for copy in copies:
        copy.wait()


def params(limit=VMEM_LIMIT):
    return pltpu.CompilerParams(vmem_limit_bytes=limit)


def shape(dims, dtype):
    return jax.ShapeDtypeStruct(dims, dtype)


def pass_on(piece_ref, before_ref, out_ref):
    pass


def after(piece, before):
    return pl.pallas_call(
        pass_on,
        out_shape=shape(piece.shape, piece.dtype),
        in_specs=[ANY_SPEC] * 2,
        out_specs=ANY_SPEC,
        input_output_aliases={0: 0},
        compiler_params=params(),
        name="after",
    )(piece, before)


def exchange(pieces, count):
    moved = [pieces[0]]
    for slot in range(1, len(pieces)):
        pairs = [(at, at ^ (2 * (core_offset(slot, at % 2) if False else slot))) for at in range(count)]
        moved.append(lax.ppermute(pieces[slot], "seg", pairs))
    return moved


def one_by_one(pieces, before, order):
    taken = list(pieces)
    for slot in order:
        taken[slot] = before = after(pieces[slot], before)
    return taken


def swap_cores(pieces, count):
    pairs = [(at, at ^ 1) for at in range(count)]
    return [lax.ppermute(piece, "seg", pairs) for piece in pieces]


def add_kernel(left_ref, right_ref, out_ref):
    out_ref[...] = left_ref[...] + right_ref[...]


def head_sums(sums, count):
    step = 1
    parts = [sums]
    while step < count:
        if len(parts) == 2:
            parts = [
                pl.pallas_call(
                    add_kernel,
                    out_shape=shape(sums.shape, sums.dtype),
                    in_specs=[VMEM_SPEC] * 2,
                    out_specs=VMEM_SPEC,
                    compiler_params=params(),
                    name="add_sums",
                )(*parts)
            ]
        parts.append(lax.ppermute(parts[0], "head", [(at, at ^ step) for at in range(count)]))
        step *= 2
    return parts


def local(seg_count, head_count, queries, key_tokens, values, upstream, norm_gain, decay_rate, block_length, parent):
    rows, wide = queries.shape
    heads = decay_rate.shape[0]
    size = wide // heads
    width = wide * head_count
    chips = seg_count // 2
    layout = Layout(rows, wide, size, chips)
    gain = norm_gain[None, :]
    piece_shape = shape((layout.piece, size), f32)
    whole = pltpu.VMEM((wide, size), f32)
    columns = shape((rows, size), f32)
    offsets = list(range(chips))
    sends = [[slot for slot in offsets if 0 < slot < 3], [slot for slot in offsets if slot == 0 or slot >= 3]]
    groups = [group for group in (layout.places(offsets[:2]), layout.places(offsets[2:])) if group]
    whole_sends = [sends[0] + sends[1]]
    early, late = groups if len(groups) == 2 else (groups[0], [])

    def near_shape(places, dtype):
        return shape((rows, len(places) * size), dtype)

    def near_scratch(places, dtype):
        return pltpu.VMEM((rows, len(places) * size), dtype)

    def in_order(parts):
        return [dict(zip(sends[0] + sends[1], parts))[offset] for offset in offsets]

    key_near, value_near, query_near = pl.pallas_call(
        near_kernel,
        out_shape=[shape((rows, wide), bf16)] * 3,
        in_specs=[ANY_SPEC] * 3,
        out_specs=[VMEM_SPEC] * 3,
        scratch_shapes=[pltpu.SemaphoreType.DMA((3,))],
        compiler_params=params(FIRST_LIMIT),
        name="bring_near",
    )(key_tokens, values, queries)

    states = []
    for chosen in whole_sends:
        states += pl.pallas_call(
            functools.partial(state_kernel, layout, chosen),
            out_shape=[piece_shape] * len(chosen),
            in_specs=[VMEM_SPEC] * 4,
            out_specs=[VMEM_SPEC] * len(chosen),
            scratch_shapes=[whole],
            compiler_params=params(),
            name="block_state",
        )(block_length[None, :], decay_rate[None, :], key_near, value_near)

    early_local, masked, scaled, table, facts = pl.pallas_call(
        functools.partial(local_kernel, layout, early),
        out_shape=[
            near_shape(early, f32),
            shape((rows, wide), bf16),
            shape((rows, wide), bf16),
            shape((4 * chips * chips, 8, size), f32),
            shape((heads + 1, size), f32),
        ],
        in_specs=[SMEM_SPEC] * 3 + [VMEM_SPEC] * 3,
        out_specs=[VMEM_SPEC] * 5,
        scratch_shapes=[pltpu.SMEM((seg_count * (seg_count + 1),), jnp.int32)],
        compiler_params=params(),
        cost_estimate=pl.CostEstimate(flops=2 * rows * rows * wide, bytes_accessed=10 * rows * wide, transcendentals=rows * rows * heads),
        name="local_attention",
    )(block_length, parent, decay_rate, query_near, key_near, value_near)

    pairs = len(tile_pairs(layout.count))
    weighted, late_local, key_end, value_end = pl.pallas_call(
        functools.partial(weighted_kernel, layout, late),
        out_shape=[shape((heads, pairs, layout.tile, layout.tile), bf16), near_shape(late or [0], f32)] + [shape((rows, wide), bf16)] * 2,
        in_specs=[VMEM_SPEC] * 4,
        out_specs=[VMEM_SPEC] * 4,
        compiler_params=params(),
        cost_estimate=pl.CostEstimate(flops=4 * rows * rows * wide, bytes_accessed=10 * rows * wide, transcendentals=rows * rows * heads),
        name="weighted_scores",
    )(facts, masked, key_near, value_near)

    def mix(pieces, backward, before):
        mine = exchange(pieces, seg_count)
        mine = mine[:1] + [after(piece, before) for piece in mine[1:]]
        other = swap_cores(mine, seg_count)
        mixed = []
        for chosen in whole_sends:
            mixed += pl.pallas_call(
                functools.partial(mix_kernel, layout, backward, chosen),
                out_shape=[piece_shape] * len(chosen),
                in_specs=[VMEM_SPEC] * (1 + 2 * chips) + [ANY_SPEC] * len(mixed[:1]),
                out_specs=[VMEM_SPEC] * len(chosen),
                compiler_params=params(),
                cost_estimate=pl.CostEstimate(flops=rows * rows * wide, bytes_accessed=10 * rows * wide, transcendentals=0),
                name="mix_backward" if backward else "mix_forward",
            )(table, *mine, *other, *mixed[:1])
        return exchange(in_order(mixed), seg_count)

    def shown(pieces, places):
        if not layout.each:
            return pieces
        return [piece if offset * layout.each in places else pieces[0] for offset, piece in enumerate(pieces)]

    carried = mix(in_order(states), 0, table)

    attended, before = [], []
    for index, (places, local_out) in enumerate(zip(groups, (early_local, late_local))):
        last = True if index == len(groups) - 1 else None
        out_shape = [near_shape(places, f32)] + ([shape((2 * rows // size, size), f32)] if last else [columns] * 2)
        part, *before = pl.pallas_call(
            functools.partial(attend_kernel, layout, places, last),
            out_shape=out_shape,
            in_specs=[VMEM_SPEC] * (4 + chips + len(before)),
            out_specs=[VMEM_SPEC] * len(out_shape),
            compiler_params=params(),
            cost_estimate=pl.CostEstimate(flops=rows * rows * wide, bytes_accessed=10 * rows * wide, transcendentals=rows * wide),
            name="attend",
        )(scaled, upstream, gain, local_out, *shown(carried, places), *before)
        attended.append(part)
    sum_parts = head_sums(before[0], head_count)

    state_grads, norms = [], []
    for chosen in whole_sends:
        first = not norms
        parts = pl.pallas_call(
            functools.partial(state_grad_kernel, layout, groups, chosen, len(sum_parts) if first else 0, width),
            out_shape=[piece_shape] * len(chosen) + ([columns] * 2 if first else []),
            in_specs=[VMEM_SPEC] * (4 + len(groups) + (len(sum_parts) if first else 2)),
            out_specs=[VMEM_SPEC] * (len(chosen) + (2 if first else 0)),
            scratch_shapes=[whole],
            compiler_params=params(),
            name="state_grad",
        )(facts, masked, upstream, gain, *attended, *(sum_parts if first else norms))
        state_grads += parts[:len(chosen)]
        norms = norms or parts[len(chosen):]

    def ending(places, kept, last):
        if not last:
            return [near_shape(places, bf16)] * 2, [VMEM_SPEC] * 2, []
        amount = len(places) + sum(len(group) for group in kept)
        scratch = [near_scratch(places, bf16)] * 2 + [pltpu.SemaphoreType.DMA((2 * amount,))]
        return [shape((rows, wide), bf16)] * 2, [ANY_SPEC] * 2, scratch

    def backward(places, kept, earlier, last):
        out_shape, out_specs, scratch = ending(places, kept, last)
        out_shape = out_shape + [near_shape(places, bf16)] * 2 + ([] if last else [shape((8, size), f32)])
        return pl.pallas_call(
            functools.partial(backward_kernel, layout, groups, places, kept, last),
            out_shape=out_shape,
            in_specs=[VMEM_SPEC] * (9 + len(groups) + chips + len(earlier)),
            out_specs=out_specs + [VMEM_SPEC] * (len(out_shape) - 2),
            scratch_shapes=scratch,
            compiler_params=params(),
            cost_estimate=pl.CostEstimate(
                flops=8 * rows * rows * size * len(places),
                bytes_accessed=16 * rows * size * len(places),
                transcendentals=rows * rows * len(places),
            ),
            name="local_backward",
        )(facts, masked, key_near, value_near, upstream, weighted, gain, *norms, *attended, *carried, *earlier)

    cut = heads * 4 // 8 if heads > 2 else heads // 2
    halves = [list(range(cut)), list(range(cut, heads))]
    out_part, query_part, key_first, value_first, token = backward(halves[0], [], [], False)
    state_sums = mix(in_order(state_grads), 1, token)
    attention_out, query_grad, key_last, value_last = backward(halves[1], halves[:1], [out_part, query_part], True)

    fulls = []
    for index, places in enumerate(groups):
        first, last = index == 0, index == len(groups) - 1
        inputs = 6 + chips
        fulls = pl.pallas_call(
            functools.partial(finish_kernel, layout, halves, places, first, last),
            out_shape=[shape((rows, wide), bf16)] * (4 if last else 2),
            in_specs=[VMEM_SPEC] * (inputs + len(fulls)),
            out_specs=[VMEM_SPEC] * 2 + [ANY_SPEC] * (2 if last else 0),
            scratch_shapes=[pltpu.SemaphoreType.DMA((4,))] if last else [],
            input_output_aliases={inputs + at: at for at in range(len(fulls))},
            compiler_params=params(),
            cost_estimate=pl.CostEstimate(flops=rows * rows * wide, bytes_accessed=10 * rows * wide, transcendentals=rows * wide),
            name="finish",
        )(key_end, value_end, key_first, key_last, value_first, value_last, *shown(state_sums, places), *fulls)
    return attention_out, query_grad, *fulls[2:]


def solution(mesh):
    sizes = dict(mesh.shape)
    tokens = P("seg", "head")
    return jax.shard_map(
        functools.partial(local, sizes["seg"], sizes["head"]),
        mesh=mesh,
        in_specs=(tokens, tokens, tokens, tokens, P("head"), P("head"), P(), P()),
        out_specs=(tokens, tokens, tokens, tokens),
        check_vma=False,
    )
```

time: 57.3 us -> 56.5 us (0.986)
  waiting for transfers between devices: 14.2 us -> 11.9 us
  Pallas kernels: 20.8 us -> 22.7 us
    ppermute x12, waiting for transfers between devices: 7.84 us -> 5.59 us  [exchange(): moved.append(lax.ppermute(pieces[slot], 'seg', pairs))]
    pallas_call x10 -> x12, Pallas kernels: 18.9 us -> 20.8 us  [the longest x2 7.25 us: backward(): pl.pallas_call(functools.partial(backward_kernel, layout, groups, places,...]
  transfers between devices with their start and end apart: 22 -> 22, of which waited for: 13 -> 13; matrix products, arithmetic and copies ran while one was open for 0% -> 0% of each run, Pallas kernels for 23% -> 28%
where the time goes in v2:
time: 56.5 us; the launch traced here: 56.3 us
  Pallas kernels  22.7 us (40%)
  starting transfers between devices  20.7 us (37%)
  waiting for transfers between devices  11.9 us (21%)
  between operations  0.99 us (2%)
    ppermute x12, starting transfers between devices, exchange(): moved.append(lax.ppermute(pieces[slot], 'seg', pairs))  15.2 us
    pallas_call x2, Pallas kernels, backward(): pl.pallas_call(functools.partial(backward_kernel, layout, groups, places,...  7.25 us
    ppermute x12, waiting for transfers between devices, exchange(): moved.append(lax.ppermute(pieces[slot], 'seg', pairs))  5.59 us
    ppermute x2, starting transfers between devices, head_sums(): lax.ppermute(parts[0], 'head', [(at, at ^ step) for at in range(count)])  4.23 us
    ppermute x2, waiting for transfers between devices, head_sums(): lax.ppermute(parts[0], 'head', [(at, at ^ step) for at in range(count)])  3.95 us
    pallas_call x1, Pallas kernels, local(): pl.pallas_call(functools.partial(weighted_kernel, layout, late), out_shap...  3.93 us
    pallas_call x1, Pallas kernels, local(): pl.pallas_call(functools.partial(local_kernel, layout, early), out_shape=...  3.46 us
    ppermute x8, waiting for transfers between devices, swap_cores(): return [lax.ppermute(piece, 'seg', pairs) for piece in pieces]  2.35 us
  transfers between devices with their start and end apart: 22, of which 13 were waited for; matrix products, arithmetic and copies ran while one was open for 0% of the time, Pallas kernels for 28%

profile of v2, /device:TPU:0, one launch (start us, length us, event | category | flops | bytes accessed | tf_op | source)
XLA Modules:
  0.0 56.3 jit_solution(6422790520771036592)
XLA Ops:
  0.6 0.0 copy-start.2
  0.6 0.0 copy-start.3
  0.7 0.0 copy-start.4
  0.7 1.9 %bring_near.1 = (bf16[512,1024]{1,0:T(8,128)(2,1)S(1)}, bf16[512,1024]{1,0:T(8,128)(2,1)S(1)}, bf16[512,1024]{1,0:T(8,128)(2,1)S(1)}) custom-call(bf16[512,1024]{1,0:T(8,128)(2,1)} %key_any.1, bf16[512,1024]{1,0:T(8,128)(2,1)} %value_any.1, bf16[512,1024]{1,0:T(8,128)(2,1)} %query_any.1), custom_call_target="tpu_custom_call" | custom-call | tf_op jit(solution)/shard_map/bring_near/pallas_call | solution.py:549
  2.6 0.0 copy-done.2
  2.6 0.0 copy-done.3
  2.6 1.0 %block_state.1 = (f32[256,128]{1,0:T(8,128)S(1)}, f32[256,128]{1,0:T(8,128)S(1)}, f32[256,128]{1,0:T(8,128)S(1)}, f32[256,128]{1,0:T(8,128)S(1)}) custom-call(s32[1,8]{1,0:T(1,128)S(1)} %bitcast.8, f32[1,8]{1,0:T(1,128)S(1)} %bitcast.9, bf16[512,1024]{1,0:T(8,128)(2,1)S(1)} %get-tuple-element.53.key_ref, bf16[512,1024]{1,0:T(8,128)(2,1)S(1)} %get-tuple-element.54.value_ref), custom_call_target="tpu_custom_call" | custom-call | tf_op jit(solution)/shard_map/block_state/pallas_call | solution.py:561
  3.6 3.0 %collective-permute-start.1 = (f32[256,128]{1,0:T(8,128)S(1)}, f32[256,128]{1,0:T(8,128)S(1)}, u32[]{:S(2)}, u32[]{:S(2)}) collective-permute-start(f32[256,128]{1,0:T(8,128)S(1)} %get-tuple-element.63), channel_id=1, source_target_pairs={{0,16},{4,20},{8,24},{12,28},{16,0},{20,4},{24,8},{28,12},{1,17},{... | collective-permute-start | bytes 393224 | tf_op jit(solution)/shard_map/ppermute | solution.py:483
  6.7 1.4 %collective-permute-start.2 = (f32[256,128]{1,0:T(8,128)S(1)}, f32[256,128]{1,0:T(8,128)S(1)}, u32[]{:S(2)}, u32[]{:S(2)}) collective-permute-start(f32[256,128]{1,0:T(8,128)S(1)} %get-tuple-element.64), channel_id=1, source_target_pairs={{0,24},{4,28},{8,16},{12,20},{16,8},{20,12},{24,0},{28,4},{1,25},{... | collective-permute-start | bytes 393224 | tf_op jit(solution)/shard_map/ppermute | solution.py:483
  8.1 0.1 collective-permute-start
  8.2 0.0 collective-permute-start.3
  8.2 3.5 %local_attention.1 = (f32[512,512]{1,0:T(8,128)S(1)}, bf16[512,1024]{1,0:T(8,128)(2,1)S(1)}, bf16[512,1024]{1,0:T(8,128)(2,1)S(1)}, f32[64,8,128]{2,1,0:T(8,128)S(1)}, f32[9,128]{1,0:T(8,128)S(1)}) custom-call(s32[8]{0:T(128)S(1)} %copy-done.2, s32[8]{0:T(128)S(1)} %copy-done.4, f32[8]{0:T(128)S(1)} %copy-done.3, ...), custom_call_target="tpu_custom_call" | custom-call | flops 536870912 | bytes 5242880 | tf_op jit(solution)/shard_map/local_attention/pallas_call | solution.py:571
  11.7 0.6 collective-permute-done.1.piece_ref
  12.2 0.1 collective-permute-start.5
  12.3 1.7 %collective-permute-done.2.piece_ref = f32[256,128]{1,0:T(8,128)S(1)} collective-permute-done((f32[256,128]{1,0:T(8,128)S(1)}, f32[256,128]{1,0:T(8,128)S(1)}, u32[]{:S(2)}, u32[]{:S(2)}) %collective-permute-start.2) | collective-permute-done | bytes 131104 | tf_op jit(solution)/shard_map/ppermute | solution.py:483
  14.0 0.0 collective-permute-start.6
  14.0 0.3 collective-permute-done.piece_ref
  14.3 0.2 collective-permute-start.4
  14.5 0.0 collective-permute-done.3.rest_4_
  14.5 0.0 collective-permute-done.5.rest_6_
  14.5 0.8 %collective-permute-done.6.rest_7_ = f32[256,128]{1,0:T(8,128)S(1)} collective-permute-done((f32[256,128]{1,0:T(8,128)S(1)}, f32[256,128]{1,0:T(8,128)S(1)}, u32[]{:S(2)}, u32[]{:S(2)}) %collective-permute-start.6) | collective-permute-done | bytes 131104 | tf_op jit(solution)/shard_map/ppermute | solution.py:496
  15.3 0.3 collective-permute-done.4.rest_5_
  15.6 0.3 mix_forward.1
  15.9 1.7 %collective-permute-start.7 = (f32[256,128]{1,0:T(8,128)S(1)}, f32[256,128]{1,0:T(8,128)S(1)}, u32[]{:S(2)}, u32[]{:S(2)}) collective-permute-start(f32[256,128]{1,0:T(8,128)S(1)} %get-tuple-element.66), channel_id=1, source_target_pairs={{0,8},{4,12},{8,0},{12,4},{16,24},{20,28},{24,16},{28,20},{1,9},{5... | collective-permute-start | bytes 393224 | tf_op jit(solution)/shard_map/ppermute | solution.py:483
  17.6 1.5 %collective-permute-start.8 = (f32[256,128]{1,0:T(8,128)S(1)}, f32[256,128]{1,0:T(8,128)S(1)}, u32[]{:S(2)}, u32[]{:S(2)}) collective-permute-start(f32[256,128]{1,0:T(8,128)S(1)} %get-tuple-element.69), channel_id=1, source_target_pairs={{0,16},{4,20},{8,24},{12,28},{16,0},{20,4},{24,8},{28,12},{1,17},{... | collective-permute-start | bytes 393224 | tf_op jit(solution)/shard_map/ppermute | solution.py:483
  19.1 0.3 collective-permute-start.9
  19.5 3.9 %weighted_scores.1 = (bf16[8,3,256,256]{3,2,1,0:T(8,128)(2,1)S(1)}, f32[512,512]{1,0:T(8,128)S(1)}, bf16[512,1024]{1,0:T(8,128)(2,1)S(1)}, bf16[512,1024]{1,0:T(8,128)(2,1)S(1)}) custom-call(f32[9,128]{1,0:T(8,128)S(1)} %get-tuple-element.55.facts_ref, bf16[512,1024]{1,0:T(8,128)(2,1)S(1)} %get-tuple-element.56.query_ref, ...), custom_call_target="tpu_custom_call" | custom-call | flops 1073741824 | bytes 5242880 | tf_op jit(solution)/shard_map/weighted_scores/pallas_call | solution.py:589
  23.4 0.0 collective-permute-done.7.rest_1_.rest_3_
  23.4 0.0 copy-done
  23.4 0.0 copy-done.1
  23.4 0.5 attend.2
  23.9 1.8 %collective-permute-done.8.rest_2_.rest_4_ = f32[256,128]{1,0:T(8,128)S(1)} collective-permute-done((f32[256,128]{1,0:T(8,128)S(1)}, f32[256,128]{1,0:T(8,128)S(1)}, u32[]{:S(2)}, u32[]{:S(2)}) %collective-permute-start.8) | collective-permute-done | bytes 131104 | tf_op jit(solution)/shard_map/ppermute | solution.py:483
  25.7 0.0 collective-permute-done.9.rest_3_.rest_5_
  25.7 0.6 %attend.3 = (f32[512,512]{1,0:T(8,128)S(1)}, f32[8,128]{1,0:T(8,128)S(1)}) custom-call(bf16[512,1024]{1,0:T(8,128)(2,1)S(1)} %get-tuple-element.58.scaled_ref, bf16[512,1024]{1,0:T(8,128)(2,1)S(1)} %copy-done, f32[1,1024]{1,0:T(1,128)S(1)} %bitcast.4, f32[512,512]{1,0:T(8,128)S(1)} %get-tuple-element.68.local_ref, ...), custom_call_target="tpu_custom_call" | custom-call | flops 268435456 | bytes 5242880 | tf_op jit(solution)/shard_map/attend/pallas_call | solution.py:627
  26.3 1.6 %collective-permute-start.10 = (f32[8,128]{1,0:T(8,128)S(1)}, f32[8,128]{1,0:T(8,128)S(1)}, u32[]{:S(2)}, u32[]{:S(2)}) collective-permute-start(f32[8,128]{1,0:T(8,128)S(1)} %get-tuple-element.74.left_ref), channel_id=1, source_target_pairs={{0,1},{1,0},{2,3},{3,2},{4,5},{5,4},{6,7},{7,6},{8,9},{9,8},{10,11... | collective-permute-start | bytes 12296 | tf_op jit(solution)/shard_map/ppermute | solution.py:518
  28.0 2.0 %collective-permute-done.10.right_ref = f32[8,128]{1,0:T(8,128)S(1)} collective-permute-done((f32[8,128]{1,0:T(8,128)S(1)}, f32[8,128]{1,0:T(8,128)S(1)}, u32[]{:S(2)}, u32[]{:S(2)}) %collective-permute-start.10) | collective-permute-done | bytes 4128 | tf_op jit(solution)/shard_map/ppermute | solution.py:518
  30.0 2.6 %collective-permute-start.11 = (f32[8,128]{1,0:T(8,128)S(1)}, f32[8,128]{1,0:T(8,128)S(1)}, u32[]{:S(2)}, u32[]{:S(2)}) collective-permute-start(f32[8,128]{1,0:T(8,128)S(1)} %add_sums.1.rest_2_), channel_id=1, source_target_pairs={{0,2},{1,3},{2,0},{3,1},{4,6},{5,7},{6,4},{7,5},{8,10},{9,11},{10,... | collective-permute-start | bytes 12296 | tf_op jit(solution)/shard_map/ppermute | solution.py:518
  32.6 1.9 %collective-permute-done.11.rest_3_ = f32[8,128]{1,0:T(8,128)S(1)} collective-permute-done((f32[8,128]{1,0:T(8,128)S(1)}, f32[8,128]{1,0:T(8,128)S(1)}, u32[]{:S(2)}, u32[]{:S(2)}) %collective-permute-start.11) | collective-permute-done | bytes 4128 | tf_op jit(solution)/shard_map/ppermute | solution.py:518
  34.5 1.2 %state_grad.1 = (f32[256,128]{1,0:T(8,128)S(1)}, f32[256,128]{1,0:T(8,128)S(1)}, f32[256,128]{1,0:T(8,128)S(1)}, f32[256,128]{1,0:T(8,128)S(1)}, f32[512,128]{1,0:T(8,128)S(1)}, /*index=5*/f32[512,128]{1,0:T(8,128)S(1)}) custom-call(f32[9,128]{1,0:T(8,128)S(1)} %get-tuple-element.55.facts_ref, bf16[512,1024]{1,0:T(8,128)(2,1)S(1)} %get-tuple-element.56.query_ref, ...), custom_call_target="tpu_custom_call" | custom-call | tf_op jit(solution)/shard_map/state_grad/pallas_call | solution.py:642
  35.7 1.5 %collective-permute-start.14 = (f32[256,128]{1,0:T(8,128)S(1)}, f32[256,128]{1,0:T(8,128)S(1)}, u32[]{:S(2)}, u32[]{:S(2)}) collective-permute-start(f32[256,128]{1,0:T(8,128)S(1)} %get-tuple-element.91), channel_id=1, source_target_pairs={{0,24},{4,28},{8,16},{12,20},{16,8},{20,12},{24,0},{28,4},{1,25},{... | collective-permute-start | bytes 393224 | tf_op jit(solution)/shard_map/ppermute | solution.py:483
  37.3 1.2 %collective-permute-start.13 = (f32[256,128]{1,0:T(8,128)S(1)}, f32[256,128]{1,0:T(8,128)S(1)}, u32[]{:S(2)}, u32[]{:S(2)}) collective-permute-start(f32[256,128]{1,0:T(8,128)S(1)} %get-tuple-element.90), channel_id=1, source_target_pairs={{0,16},{4,20},{8,24},{12,28},{16,0},{20,4},{24,8},{28,12},{1,17},{... | collective-permute-start | bytes 393224 | tf_op jit(solution)/shard_map/ppermute | solution.py:483
  38.5 0.8 %collective-permute-start.12 = (f32[256,128]{1,0:T(8,128)S(1)}, f32[256,128]{1,0:T(8,128)S(1)}, u32[]{:S(2)}, u32[]{:S(2)}) collective-permute-start(f32[256,128]{1,0:T(8,128)S(1)} %get-tuple-element.88), channel_id=1, source_target_pairs={{0,8},{4,12},{8,0},{12,4},{16,24},{20,28},{24,16},{28,20},{1,9},{5... | collective-permute-start | bytes 393224 | tf_op jit(solution)/shard_map/ppermute | solution.py:483
  39.3 0.0 collective-permute-start.15
  39.3 3.2 %local_backward.2 = (bf16[512,512]{1,0:T(8,128)(2,1)S(1)}, bf16[512,512]{1,0:T(8,128)(2,1)S(1)}, bf16[512,512]{1,0:T(8,128)(2,1)S(1)}, bf16[512,512]{1,0:T(8,128)(2,1)S(1)}, f32[8,128]{1,0:T(8,128)S(1)}) custom-call(f32[9,128]{1,0:T(8,128)S(1)} %get-tuple-element.55.facts_ref, bf16[512,1024]{1,0:T(8,128)(2,1)S(1)} %get-tuple-element.56.query_ref, ...), custom_call_target="tpu_custom_call" | custom-call | flops 1073741824 | bytes 4194304 | tf_op jit(solution)/shard_map/local_backward/pallas_call | solution.py:664
  42.5 0.0 collective-permute-done.14.piece_ref
  42.5 0.6 %collective-permute-start.18 = (f32[256,128]{1,0:T(8,128)S(1)}, f32[256,128]{1,0:T(8,128)S(1)}, u32[]{:S(2)}, u32[]{:S(2)}) collective-permute-start(f32[256,128]{1,0:T(8,128)S(1)} %after.11.rest_3_), channel_id=1, source_target_pairs={{0,4},{4,0},{8,12},{12,8},{16,20},{20,16},{24,28},{28,24},{1,5},{5... | collective-permute-start | bytes 393224 | tf_op jit(solution)/shard_map/ppermute | solution.py:496
  43.1 0.0 collective-permute-done.13.piece_ref
  43.1 0.3 collective-permute-start.17
  43.4 0.1 collective-permute-done.12.piece_ref
  43.5 0.1 collective-permute-start.16
  43.6 0.0 collective-permute-done.15.rest_4_
  43.6 0.5 collective-permute-done.18.rest_7_
  44.1 0.4 collective-permute-done.17.rest_6_
  44.4 0.4 collective-permute-done.16.rest_5_
  44.8 0.3 mix_backward.1
  45.1 1.2 %collective-permute-start.21 = (f32[256,128]{1,0:T(8,128)S(1)}, f32[256,128]{1,0:T(8,128)S(1)}, u32[]{:S(2)}, u32[]{:S(2)}) collective-permute-start(f32[256,128]{1,0:T(8,128)S(1)} %get-tuple-element.95), channel_id=1, source_target_pairs={{0,8},{4,12},{8,0},{12,4},{16,24},{20,28},{24,16},{28,20},{1,9},{5... | collective-permute-start | bytes 393224 | tf_op jit(solution)/shard_map/ppermute | solution.py:483
  46.3 1.2 %collective-permute-start.19 = (f32[256,128]{1,0:T(8,128)S(1)}, f32[256,128]{1,0:T(8,128)S(1)}, u32[]{:S(2)}, u32[]{:S(2)}) collective-permute-start(f32[256,128]{1,0:T(8,128)S(1)} %get-tuple-element.93), channel_id=1, source_target_pairs={{0,16},{4,20},{8,24},{12,28},{16,0},{20,4},{24,8},{28,12},{1,17},{... | collective-permute-start | bytes 393224 | tf_op jit(solution)/shard_map/ppermute | solution.py:483
  47.5 1.2 %collective-permute-start.20 = (f32[256,128]{1,0:T(8,128)S(1)}, f32[256,128]{1,0:T(8,128)S(1)}, u32[]{:S(2)}, u32[]{:S(2)}) collective-permute-start(f32[256,128]{1,0:T(8,128)S(1)} %get-tuple-element.94), channel_id=1, source_target_pairs={{0,24},{4,28},{8,16},{12,20},{16,8},{20,12},{24,0},{28,4},{1,25},{... | collective-permute-start | bytes 393224 | tf_op jit(solution)/shard_map/ppermute | solution.py:483
  48.7 4.1 %local_backward.3 = (bf16[512,1024]{1,0:T(8,128)(2,1)}, bf16[512,1024]{1,0:T(8,128)(2,1)}, bf16[512,512]{1,0:T(8,128)(2,1)S(1)}, bf16[512,512]{1,0:T(8,128)(2,1)S(1)}) custom-call(f32[9,128]{1,0:T(8,128)S(1)} %get-tuple-element.55.facts_ref, bf16[512,1024]{1,0:T(8,128)(2,1)S(1)} %get-tuple-element.56.query_ref, ...), custom_call_target="tpu_custom_call" | custom-call | flops 1073741824 | bytes 4194304 | tf_op jit(solution)/shard_map/local_backward/pallas_call | solution.py:664
  52.8 0.0 collective-permute-done.21.rest_5_
  52.8 0.5 finish.2
  53.3 0.0 collective-permute-done.19.rest_6_
  53.3 1.2 %collective-permute-done.20.rest_7_ = f32[256,128]{1,0:T(8,128)S(1)} collective-permute-done((f32[256,128]{1,0:T(8,128)S(1)}, f32[256,128]{1,0:T(8,128)S(1)}, u32[]{:S(2)}, u32[]{:S(2)}) %collective-permute-start.20) | collective-permute-done | bytes 131104 | tf_op jit(solution)/shard_map/ppermute | solution.py:483
  54.5 1.7 %finish.3 = (bf16[512,1024]{1,0:T(8,128)(2,1)S(1)}, bf16[512,1024]{1,0:T(8,128)(2,1)S(1)}, bf16[512,1024]{1,0:T(8,128)(2,1)}, bf16[512,1024]{1,0:T(8,128)(2,1)}) custom-call(bf16[512,1024]{1,0:T(8,128)(2,1)S(1)} %get-tuple-element.81.key_end_ref, ...), custom_call_target="tpu_custom_call", output_to_operand_aliasing={{0}: (10, {}), {1}: (11, {})} | custom-call | flops 268435456 | bytes 5242880 | tf_op jit(solution)/shard_map/finish/pallas_call | solution.py:689
  (10 shorter events, 0.0 us)
Async XLA Ops:
  0.6 1.9 %copy-start.2 = (s32[8]{0:T(128)S(1)}, s32[8]{0:T(128)}, u32[]{:S(2)}) copy-start(s32[8]{0:T(128)} %length_ref.1) | copy-start | bytes 100
  0.6 1.9 %copy-start.3 = (f32[8]{0:T(128)S(1)}, f32[8]{0:T(128)}, u32[]{:S(2)}) copy-start(f32[8]{0:T(128)} %rate_ref.1) | copy-start | bytes 100
  0.7 7.6 %copy-start.4 = (s32[8]{0:T(128)S(1)}, s32[8]{0:T(128)}, u32[]{:S(2)}) copy-start(s32[8]{0:T(128)} %parent_ref.1) | copy-start | bytes 100
  3.6 8.6 %collective-permute-start.1 = (f32[256,128]{1,0:T(8,128)S(1)}, f32[256,128]{1,0:T(8,128)S(1)}, u32[]{:S(2)}, u32[]{:S(2)}) collective-permute-start(f32[256,128]{1,0:T(8,128)S(1)} %get-tuple-element.63), channel_id=1, source_target_pairs={{0,16},{4,20},{8,24},{12,28},{16,0},{20,4},{24,8},{28,12},{1,17},{... | collective-permute-start | bytes 393224 | tf_op jit(solution)/shard_map/ppermute | solution.py:483
  6.7 7.3 %collective-permute-start.2 = (f32[256,128]{1,0:T(8,128)S(1)}, f32[256,128]{1,0:T(8,128)S(1)}, u32[]{:S(2)}, u32[]{:S(2)}) collective-permute-start(f32[256,128]{1,0:T(8,128)S(1)} %get-tuple-element.64), channel_id=1, source_target_pairs={{0,24},{4,28},{8,16},{12,20},{16,8},{20,12},{24,0},{28,4},{1,25},{... | collective-permute-start | bytes 393224 | tf_op jit(solution)/shard_map/ppermute | solution.py:483
  8.1 6.2 %collective-permute-start = (f32[256,128]{1,0:T(8,128)S(1)}, f32[256,128]{1,0:T(8,128)S(1)}, u32[]{:S(2)}, u32[]{:S(2)}) collective-permute-start(f32[256,128]{1,0:T(8,128)S(1)} %get-tuple-element.62), channel_id=1, source_target_pairs={{0,8},{4,12},{8,0},{12,4},{16,24},{20,28},{24,16},{28,20},{1,9},{5... | collective-permute-start | bytes 393224 | tf_op jit(solution)/shard_map/ppermute | solution.py:483
  8.2 6.3 %collective-permute-start.3 = (f32[256,128]{1,0:T(8,128)S(1)}, f32[256,128]{1,0:T(8,128)S(1)}, u32[]{:S(2)}, u32[]{:S(2)}) collective-permute-start(f32[256,128]{1,0:T(8,128)S(1)} %get-tuple-element.61.rest_0_), channel_id=1, source_target_pairs={{0,4},{4,0},{8,12},{12,8},{16,20},{20,16},{24,28},{28,24},{1,5},{5... | collective-permute-start | bytes 393224 | tf_op jit(solution)/shard_map/ppermute | solution.py:496
  12.2 11.2 %copy-start = (bf16[512,1024]{1,0:T(8,128)(2,1)S(1)}, bf16[512,1024]{1,0:T(8,128)(2,1)}, u32[]{:S(2)}) copy-start(bf16[512,1024]{1,0:T(8,128)(2,1)} %upstream_ref.9) | copy-start | bytes 3145732
  12.2 11.2 %copy-start.1 = (f32[1024]{0:T(1024)S(1)}, f32[1024]{0:T(1024)}, u32[]{:S(2)}) copy-start(f32[1024]{0:T(1024)} %param.12) | copy-start | bytes 12292
  12.2 2.3 %collective-permute-start.5 = (f32[256,128]{1,0:T(8,128)S(1)}, f32[256,128]{1,0:T(8,128)S(1)}, u32[]{:S(2)}, u32[]{:S(2)}) collective-permute-start(f32[256,128]{1,0:T(8,128)S(1)} %after.7.rest_2_), channel_id=1, source_target_pairs={{0,4},{4,0},{8,12},{12,8},{16,20},{20,16},{24,28},{28,24},{1,5},{5... | collective-permute-start | bytes 393224 | tf_op jit(solution)/shard_map/ppermute | solution.py:496
  14.0 1.3 %collective-permute-start.6 = (f32[256,128]{1,0:T(8,128)S(1)}, f32[256,128]{1,0:T(8,128)S(1)}, u32[]{:S(2)}, u32[]{:S(2)}) collective-permute-start(f32[256,128]{1,0:T(8,128)S(1)} %after.8.rest_3_), channel_id=1, source_target_pairs={{0,4},{4,0},{8,12},{12,8},{16,20},{20,16},{24,28},{28,24},{1,5},{5... | collective-permute-start | bytes 393224 | tf_op jit(solution)/shard_map/ppermute | solution.py:496
  14.3 1.3 %collective-permute-start.4 = (f32[256,128]{1,0:T(8,128)S(1)}, f32[256,128]{1,0:T(8,128)S(1)}, u32[]{:S(2)}, u32[]{:S(2)}) collective-permute-start(f32[256,128]{1,0:T(8,128)S(1)} %after.6.rest_1_), channel_id=1, source_target_pairs={{0,4},{4,0},{8,12},{12,8},{16,20},{20,16},{24,28},{28,24},{1,5},{5... | collective-permute-start | bytes 393224 | tf_op jit(solution)/shard_map/ppermute | solution.py:496
  15.9 7.5 %collective-permute-start.7 = (f32[256,128]{1,0:T(8,128)S(1)}, f32[256,128]{1,0:T(8,128)S(1)}, u32[]{:S(2)}, u32[]{:S(2)}) collective-permute-start(f32[256,128]{1,0:T(8,128)S(1)} %get-tuple-element.66), channel_id=1, source_target_pairs={{0,8},{4,12},{8,0},{12,4},{16,24},{20,28},{24,16},{28,20},{1,9},{5... | collective-permute-start | bytes 393224 | tf_op jit(solution)/shard_map/ppermute | solution.py:483
  17.6 8.1 %collective-permute-start.8 = (f32[256,128]{1,0:T(8,128)S(1)}, f32[256,128]{1,0:T(8,128)S(1)}, u32[]{:S(2)}, u32[]{:S(2)}) collective-permute-start(f32[256,128]{1,0:T(8,128)S(1)} %get-tuple-element.69), channel_id=1, source_target_pairs={{0,16},{4,20},{8,24},{12,28},{16,0},{20,4},{24,8},{28,12},{1,17},{... | collective-permute-start | bytes 393224 | tf_op jit(solution)/shard_map/ppermute | solution.py:483
  19.1 6.6 %collective-permute-start.9 = (f32[256,128]{1,0:T(8,128)S(1)}, f32[256,128]{1,0:T(8,128)S(1)}, u32[]{:S(2)}, u32[]{:S(2)}) collective-permute-start(f32[256,128]{1,0:T(8,128)S(1)} %get-tuple-element.70), channel_id=1, source_target_pairs={{0,24},{4,28},{8,16},{12,20},{16,8},{20,12},{24,0},{28,4},{1,25},{... | collective-permute-start | bytes 393224 | tf_op jit(solution)/shard_map/ppermute | solution.py:483
  26.3 3.7 %collective-permute-start.10 = (f32[8,128]{1,0:T(8,128)S(1)}, f32[8,128]{1,0:T(8,128)S(1)}, u32[]{:S(2)}, u32[]{:S(2)}) collective-permute-start(f32[8,128]{1,0:T(8,128)S(1)} %get-tuple-element.74.left_ref), channel_id=1, source_target_pairs={{0,1},{1,0},{2,3},{3,2},{4,5},{5,4},{6,7},{7,6},{8,9},{9,8},{10,11... | collective-permute-start | bytes 12296 | tf_op jit(solution)/shard_map/ppermute | solution.py:518
  30.0 4.5 %collective-permute-start.11 = (f32[8,128]{1,0:T(8,128)S(1)}, f32[8,128]{1,0:T(8,128)S(1)}, u32[]{:S(2)}, u32[]{:S(2)}) collective-permute-start(f32[8,128]{1,0:T(8,128)S(1)} %add_sums.1.rest_2_), channel_id=1, source_target_pairs={{0,2},{1,3},{2,0},{3,1},{4,6},{5,7},{6,4},{7,5},{8,10},{9,11},{10,... | collective-permute-start | bytes 12296 | tf_op jit(solution)/shard_map/ppermute | solution.py:518
  35.7 6.8 %collective-permute-start.14 = (f32[256,128]{1,0:T(8,128)S(1)}, f32[256,128]{1,0:T(8,128)S(1)}, u32[]{:S(2)}, u32[]{:S(2)}) collective-permute-start(f32[256,128]{1,0:T(8,128)S(1)} %get-tuple-element.91), channel_id=1, source_target_pairs={{0,24},{4,28},{8,16},{12,20},{16,8},{20,12},{24,0},{28,4},{1,25},{... | collective-permute-start | bytes 393224 | tf_op jit(solution)/shard_map/ppermute | solution.py:483
  37.3 5.8 %collective-permute-start.13 = (f32[256,128]{1,0:T(8,128)S(1)}, f32[256,128]{1,0:T(8,128)S(1)}, u32[]{:S(2)}, u32[]{:S(2)}) collective-permute-start(f32[256,128]{1,0:T(8,128)S(1)} %get-tuple-element.90), channel_id=1, source_target_pairs={{0,16},{4,20},{8,24},{12,28},{16,0},{20,4},{24,8},{28,12},{1,17},{... | collective-permute-start | bytes 393224 | tf_op jit(solution)/shard_map/ppermute | solution.py:483
  38.5 5.0 %collective-permute-start.12 = (f32[256,128]{1,0:T(8,128)S(1)}, f32[256,128]{1,0:T(8,128)S(1)}, u32[]{:S(2)}, u32[]{:S(2)}) collective-permute-start(f32[256,128]{1,0:T(8,128)S(1)} %get-tuple-element.88), channel_id=1, source_target_pairs={{0,8},{4,12},{8,0},{12,4},{16,24},{20,28},{24,16},{28,20},{1,9},{5... | collective-permute-start | bytes 393224 | tf_op jit(solution)/shard_map/ppermute | solution.py:483
  39.3 4.3 %collective-permute-start.15 = (f32[256,128]{1,0:T(8,128)S(1)}, f32[256,128]{1,0:T(8,128)S(1)}, u32[]{:S(2)}, u32[]{:S(2)}) collective-permute-start(f32[256,128]{1,0:T(8,128)S(1)} %get-tuple-element.87.rest_0_), channel_id=1, source_target_pairs={{0,4},{4,0},{8,12},{12,8},{16,20},{20,16},{24,28},{28,24},{1,5},{5... | collective-permute-start | bytes 393224 | tf_op jit(solution)/shard_map/ppermute | solution.py:496
  42.5 1.6 %collective-permute-start.18 = (f32[256,128]{1,0:T(8,128)S(1)}, f32[256,128]{1,0:T(8,128)S(1)}, u32[]{:S(2)}, u32[]{:S(2)}) collective-permute-start(f32[256,128]{1,0:T(8,128)S(1)} %after.11.rest_3_), channel_id=1, source_target_pairs={{0,4},{4,0},{8,12},{12,8},{16,20},{20,16},{24,28},{28,24},{1,5},{5... | collective-permute-start | bytes 393224 | tf_op jit(solution)/shard_map/ppermute | solution.py:496
  43.1 1.3 %collective-permute-start.17 = (f32[256,128]{1,0:T(8,128)S(1)}, f32[256,128]{1,0:T(8,128)S(1)}, u32[]{:S(2)}, u32[]{:S(2)}) collective-permute-start(f32[256,128]{1,0:T(8,128)S(1)} %after.10.rest_2_), channel_id=1, source_target_pairs={{0,4},{4,0},{8,12},{12,8},{16,20},{20,16},{24,28},{28,24},{1,5},{5... | collective-permute-start | bytes 393224 | tf_op jit(solution)/shard_map/ppermute | solution.py:496
  43.5 1.3 %collective-permute-start.16 = (f32[256,128]{1,0:T(8,128)S(1)}, f32[256,128]{1,0:T(8,128)S(1)}, u32[]{:S(2)}, u32[]{:S(2)}) collective-permute-start(f32[256,128]{1,0:T(8,128)S(1)} %after.9.rest_1_), channel_id=1, source_target_pairs={{0,4},{4,0},{8,12},{12,8},{16,20},{20,16},{24,28},{28,24},{1,5},{5... | collective-permute-start | bytes 393224 | tf_op jit(solution)/shard_map/ppermute | solution.py:496
  45.1 7.6 %collective-permute-start.21 = (f32[256,128]{1,0:T(8,128)S(1)}, f32[256,128]{1,0:T(8,128)S(1)}, u32[]{:S(2)}, u32[]{:S(2)}) collective-permute-start(f32[256,128]{1,0:T(8,128)S(1)} %get-tuple-element.95), channel_id=1, source_target_pairs={{0,8},{4,12},{8,0},{12,4},{16,24},{20,28},{24,16},{28,20},{1,9},{5... | collective-permute-start | bytes 393224 | tf_op jit(solution)/shard_map/ppermute | solution.py:483
  46.3 7.0 %collective-permute-start.19 = (f32[256,128]{1,0:T(8,128)S(1)}, f32[256,128]{1,0:T(8,128)S(1)}, u32[]{:S(2)}, u32[]{:S(2)}) collective-permute-start(f32[256,128]{1,0:T(8,128)S(1)} %get-tuple-element.93), channel_id=1, source_target_pairs={{0,16},{4,20},{8,24},{12,28},{16,0},{20,4},{24,8},{28,12},{1,17},{... | collective-permute-start | bytes 393224 | tf_op jit(solution)/shard_map/ppermute | solution.py:483
  47.5 7.0 %collective-permute-start.20 = (f32[256,128]{1,0:T(8,128)S(1)}, f32[256,128]{1,0:T(8,128)S(1)}, u32[]{:S(2)}, u32[]{:S(2)}) collective-permute-start(f32[256,128]{1,0:T(8,128)S(1)} %get-tuple-element.94), channel_id=1, source_target_pairs={{0,24},{4,28},{8,16},{12,20},{16,8},{20,12},{24,0},{28,4},{1,25},{... | collective-permute-start | bytes 393224 | tf_op jit(solution)/shard_map/ppermute | solution.py:483

commit v3 on v2

--- a/solution.py
+++ b/solution.py
@@ -11,7 +11,7 @@
 f32 = jnp.float32
 bf16 = jnp.bfloat16
 VMEM_LIMIT = 40 * 1024 * 1024
-FIRST_LIMIT = 504 * 1024 * 1024 // 10
+FIRST_LIMIT = 514 * 1024 * 1024 // 10
 
 SMEM_SPEC = pl.BlockSpec(memory_space=pltpu.SMEM)
 VMEM_SPEC = pl.BlockSpec(memory_space=pltpu.VMEM)
@@ -121,8 +121,8 @@
         return jnp.concatenate(parts, axis=0)
 
 
-def near_kernel(key_any, value_any, query_any, key_ref, value_ref, query_ref, sems):
-    moves = ((key_any, key_ref), (value_any, value_ref), (query_any, query_ref))
+def near_kernel(key_any, value_any, query_any, key_ref, value_ref, sems):
+    moves = ((key_any, key_ref), (value_any, value_ref))
     copies = [pltpu.make_async_copy(source, target, sems.at[at]) for at, (source, target) in enumerate(moves)]
     for copy in copies:
         copy.start()
@@ -345,7 +345,7 @@
     raise ValueError(place)
 
 
-def state_grad_kernel(layout, groups, offsets, sums, width, facts_ref, query_ref, upstream_ref, gain_ref, *rest):
+def state_grad_kernel(layout, groups, offsets, sums, width, scaled_ref, upstream_ref, gain_ref, *rest):
     attended_refs, rest = rest[:len(groups)], rest[len(groups):]
     if sums:
         sum_refs, rest = rest[:sums], rest[sums:]
@@ -353,18 +353,16 @@
         norm_columns(sum_refs, width, inverse_ref, factor_ref)
     else:
         inverse_ref, factor_ref, *outs, whole = rest
-    rows, size = layout.rows, layout.size
     inverse = inverse_ref[...]
     factor = factor_ref[...]
 
     def left(place):
-        return query_ref[:, layout.span(place)]
+        return scaled_ref[:, layout.span(place)]
 
     def right(place):
         span = layout.span(place)
         scaled = upstream_ref[:, span].astype(f32) * gain_ref[:, span]
-        grad = inverse * scaled - factor * pick(layout, groups, attended_refs, place)
-        return (grad * query_scale(rows, size, facts_ref[place:place + 1, :])).astype(bf16)
+        return (inverse * scaled - factor * pick(layout, groups, attended_refs, place)).astype(bf16)
 
     write_states(layout, offsets, left, right, outs, whole)
 
@@ -428,26 +426,19 @@
         copy.wait()
 
 
-def finish_kernel(layout, groups, places, first, last, key_end_ref, value_end_ref, *rest):
+def finish_kernel(layout, groups, places, filled, key_end_ref, value_end_ref, *rest):
     key_locals, value_locals, rest = rest[:len(groups)], rest[len(groups):2 * len(groups)], rest[2 * len(groups):]
-    pieces, rest = rest[:layout.chips], rest[layout.chips + (0 if first else 2):]
-    key_full, value_full, *rest = rest
-    half = layout.rows // 2 if last else layout.rows
-    states = [layout.state(pieces, place).astype(bf16) for place in places]
+    pieces, rest = rest[:layout.chips], rest[layout.chips + filled:]
+    key_any, value_any, key_grad_ref, value_grad_ref, sems = rest
     copies = []
-    for begin in range(0, layout.rows, half):
-        part = slice(begin, begin + half)
-        for state_grad, place in zip(states, places):
-            span = layout.span(place)
-            key_part = nt(value_end_ref[part, span], state_grad)
-            value_part = nn(key_end_ref[part, span], state_grad)
-            key_full[part, span] = (pick(layout, groups, key_locals, place, part).astype(f32) + key_part).astype(bf16)
-            value_full[part, span] = (pick(layout, groups, value_locals, place, part).astype(f32) + value_part).astype(bf16)
-        if last:
-            key_any, value_any, sems = rest
-            for source, target in ((key_full, key_any), (value_full, value_any)):
-                copies.append(pltpu.make_async_copy(source.at[part, :], target.at[part, :], sems.at[len(copies)]))
-                copies[-1].start()
+    for place in places:
+        span, near = layout.span(place), layout.near(places, place)
+        state_grad = layout.state(pieces, place).astype(bf16)
+        key_part = nt(value_end_ref[:, span], state_grad)
+        value_part = nn(key_end_ref[:, span], state_grad)
+        key_grad_ref[:, near] = (pick(layout, groups, key_locals, place).astype(f32) + key_part).astype(bf16)
+        value_grad_ref[:, near] = (pick(layout, groups, value_locals, place).astype(f32) + value_part).astype(bf16)
+        send(layout, places, place, (key_grad_ref, value_grad_ref), (key_any, value_any), sems, copies)
     for copy in copies:
         copy.wait()
 
@@ -546,12 +537,12 @@
     def in_order(parts):
         return [dict(zip(sends[0] + sends[1], parts))[offset] for offset in offsets]
 
-    key_near, value_near, query_near = pl.pallas_call(
+    key_near, value_near = pl.pallas_call(
         near_kernel,
-        out_shape=[shape((rows, wide), bf16)] * 3,
+        out_shape=[shape((rows, wide), bf16)] * 2,
         in_specs=[ANY_SPEC] * 3,
-        out_specs=[VMEM_SPEC] * 3,
-        scratch_shapes=[pltpu.SemaphoreType.DMA((3,))],
+        out_specs=[VMEM_SPEC] * 2,
+        scratch_shapes=[pltpu.SemaphoreType.DMA((2,))],
         compiler_params=params(FIRST_LIMIT),
         name="bring_near",
     )(key_tokens, values, queries)
@@ -583,7 +574,7 @@
         compiler_params=params(),
         cost_estimate=pl.CostEstimate(flops=2 * rows * rows * wide, bytes_accessed=10 * rows * wide, transcendentals=rows * rows * heads),
         name="local_attention",
-    )(block_length, parent, decay_rate, query_near, key_near, value_near)
+    )(block_length, parent, decay_rate, queries, key_near, value_near)
 
     pairs = len(tile_pairs(layout.count))
     weighted, late_local, key_end, value_end = pl.pallas_call(
@@ -642,12 +633,12 @@
         parts = pl.pallas_call(
             functools.partial(state_grad_kernel, layout, groups, chosen, len(sum_parts) if first else 0, width),
             out_shape=[piece_shape] * len(chosen) + ([columns] * 2 if first else []),
-            in_specs=[VMEM_SPEC] * (4 + len(groups) + (len(sum_parts) if first else 2)),
+            in_specs=[VMEM_SPEC] * (3 + len(groups) + (len(sum_parts) if first else 2)),
             out_specs=[VMEM_SPEC] * (len(chosen) + (2 if first else 0)),
             scratch_shapes=[whole],
             compiler_params=params(),
             name="state_grad",
-        )(facts, masked, upstream, gain, *attended, *(sum_parts if first else norms))
+        )(scaled, upstream, gain, *attended, *(sum_parts if first else norms))
         state_grads += parts[:len(chosen)]
         norms = norms or parts[len(chosen):]
 
@@ -682,22 +673,21 @@
     state_sums = mix(in_order(state_grads), 1, token)
     attention_out, query_grad, key_last, value_last = backward(halves[1], halves[:1], [out_part, query_part], True)
 
-    fulls = []
-    for index, places in enumerate(groups):
-        first, last = index == 0, index == len(groups) - 1
+    grads = []
+    for places in groups:
         inputs = 6 + chips
-        fulls = pl.pallas_call(
-            functools.partial(finish_kernel, layout, halves, places, first, last),
-            out_shape=[shape((rows, wide), bf16)] * (4 if last else 2),
-            in_specs=[VMEM_SPEC] * (inputs + len(fulls)),
-            out_specs=[VMEM_SPEC] * 2 + [ANY_SPEC] * (2 if last else 0),
-            scratch_shapes=[pltpu.SemaphoreType.DMA((4,))] if last else [],
-            input_output_aliases={inputs + at: at for at in range(len(fulls))},
+        grads = pl.pallas_call(
+            functools.partial(finish_kernel, layout, halves, places, len(grads)),
+            out_shape=[shape((rows, wide), bf16)] * 2,
+            in_specs=[VMEM_SPEC] * inputs + [ANY_SPEC] * len(grads),
+            out_specs=[ANY_SPEC] * 2,
+            scratch_shapes=[near_scratch(places, bf16)] * 2 + [pltpu.SemaphoreType.DMA((2 * len(places),))],
+            input_output_aliases={inputs + at: at for at in range(len(grads))},
             compiler_params=params(),
             cost_estimate=pl.CostEstimate(flops=rows * rows * wide, bytes_accessed=10 * rows * wide, transcendentals=rows * wide),
             name="finish",
-        )(key_end, value_end, key_first, key_last, value_first, value_last, *shown(state_sums, places), *fulls)
-    return attention_out, query_grad, *fulls[2:]
+        )(key_end, value_end, key_first, key_last, value_first, value_last, *shown(state_sums, places), *grads)
+    return attention_out, query_grad, *grads
 
 
 def solution(mesh):

time: 56.5 us -> 55.4 us (0.981)
  waiting for transfers between devices: 11.9 us -> 9.9 us
  starting transfers between devices: 20.7 us -> 21.6 us
    ppermute x12, waiting for transfers between devices: 5.59 us -> 3.84 us  [exchange(): moved.append(lax.ppermute(pieces[slot], 'seg', pairs))]
    ppermute x8, starting transfers between devices: 1.26 us -> 2.16 us  [swap_cores(): return [lax.ppermute(piece, 'seg', pairs) for piece in pieces]]
  transfers between devices with their start and end apart: 22 -> 22, of which waited for: 13 -> 10; matrix products, arithmetic and copies ran while one was open for 0% -> 0% of each run, Pallas kernels for 28% -> 30%
where the time goes in v3:
time: 55.4 us; the launch traced here: 55.2 us
  Pallas kernels  22.7 us (41%)
  starting transfers between devices  21.6 us (39%)
  waiting for transfers between devices  9.9 us (18%)
  between operations  1.04 us (2%)
    ppermute x12, starting transfers between devices, exchange(): moved.append(lax.ppermute(pieces[slot], 'seg', pairs))  15.2 us
    pallas_call x2, Pallas kernels, backward(): pl.pallas_call(functools.partial(backward_kernel, layout, groups, places,...  7.23 us
    ppermute x2, starting transfers between devices, head_sums(): lax.ppermute(parts[0], 'head', [(at, at ^ step) for at in range(count)])  4.23 us
    ppermute x2, waiting for transfers between devices, head_sums(): lax.ppermute(parts[0], 'head', [(at, at ^ step) for at in range(count)])  3.94 us
    pallas_call x1, Pallas kernels, local(): pl.pallas_call(functools.partial(weighted_kernel, layout, late), out_shap...  3.93 us
    ppermute x12, waiting for transfers between devices, exchange(): moved.append(lax.ppermute(pieces[slot], 'seg', pairs))  3.84 us
    pallas_call x1, Pallas kernels, local(): pl.pallas_call(functools.partial(local_kernel, layout, early), out_shape=...  3.47 us
    pallas_call x2, Pallas kernels, local(): pl.pallas_call(functools.partial(finish_kernel, layout, halves, places, l...  2.58 us
  transfers between devices with their start and end apart: 22, of which 10 were waited for; matrix products, arithmetic and copies ran while one was open for 0% of the time, Pallas kernels for 30%

profile of v3, /device:TPU:0, one launch (start us, length us, event | category | flops | bytes accessed | tf_op | source)
XLA Modules:
  0.0 55.2 jit_solution(15700028299582023102)
XLA Ops:
  0.6 0.0 copy-start.1
  0.6 0.0 copy-start.3
  0.7 0.0 copy-start.4
  0.7 0.0 copy-start.5
  0.7 1.6 %bring_near.1 = (bf16[512,1024]{1,0:T(8,128)(2,1)S(1)}, bf16[512,1024]{1,0:T(8,128)(2,1)S(1)}) custom-call(bf16[512,1024]{1,0:T(8,128)(2,1)} %key_any.1, bf16[512,1024]{1,0:T(8,128)(2,1)} %value_any.1, bf16[512,1024]{1,0:T(8,128)(2,1)} %query_ref.1), custom_call_target="tpu_custom_call" | custom-call | tf_op jit(solution)/shard_map/bring_near/pallas_call | solution.py:540
  2.3 0.0 copy-done.3
  2.3 1.0 %block_state.1 = (f32[256,128]{1,0:T(8,128)S(1)}, f32[256,128]{1,0:T(8,128)S(1)}, f32[256,128]{1,0:T(8,128)S(1)}, f32[256,128]{1,0:T(8,128)S(1)}) custom-call(s32[1,8]{1,0:T(1,128)S(1)} %bitcast.8, f32[1,8]{1,0:T(1,128)S(1)} %bitcast.9, bf16[512,1024]{1,0:T(8,128)(2,1)S(1)} %get-tuple-element.51.key_ref, bf16[512,1024]{1,0:T(8,128)(2,1)S(1)} %get-tuple-element.52.value_ref), custom_call_target="tpu_custom_call" | custom-call | tf_op jit(solution)/shard_map/block_state/pallas_call | solution.py:552
  3.4 3.0 %collective-permute-start = (f32[256,128]{1,0:T(8,128)S(1)}, f32[256,128]{1,0:T(8,128)S(1)}, u32[]{:S(2)}, u32[]{:S(2)}) collective-permute-start(f32[256,128]{1,0:T(8,128)S(1)} %get-tuple-element.60), channel_id=1, source_target_pairs={{0,8},{4,12},{8,0},{12,4},{16,24},{20,28},{24,16},{28,20},{1,9},{5... | collective-permute-start | bytes 393224 | tf_op jit(solution)/shard_map/ppermute | solution.py:474
  6.4 1.5 %collective-permute-start.1 = (f32[256,128]{1,0:T(8,128)S(1)}, f32[256,128]{1,0:T(8,128)S(1)}, u32[]{:S(2)}, u32[]{:S(2)}) collective-permute-start(f32[256,128]{1,0:T(8,128)S(1)} %get-tuple-element.61), channel_id=1, source_target_pairs={{0,16},{4,20},{8,24},{12,28},{16,0},{20,4},{24,8},{28,12},{1,17},{... | collective-permute-start | bytes 393224 | tf_op jit(solution)/shard_map/ppermute | solution.py:474
  7.9 0.0 collective-permute-start.2
  7.9 0.0 collective-permute-start.3
  7.9 3.5 %local_attention.1 = (f32[512,512]{1,0:T(8,128)S(1)}, bf16[512,1024]{1,0:T(8,128)(2,1)S(1)}, bf16[512,1024]{1,0:T(8,128)(2,1)S(1)}, f32[64,8,128]{2,1,0:T(8,128)S(1)}, f32[9,128]{1,0:T(8,128)S(1)}) custom-call(s32[8]{0:T(128)S(1)} %copy-done.3, s32[8]{0:T(128)S(1)} %copy-done.5, f32[8]{0:T(128)S(1)} %copy-done.4, bf16[512,1024]{1,0:T(8,128)(2,1)S(1)} %copy-done.1, ...), custom_call_target="tpu_custom_call" | custom-call | flops 536870912 | bytes 5242880 | tf_op jit(solution)/shard_map/local_attention/pallas_call | solution.py:562
  11.4 0.0 collective-permute-done.piece_ref
  11.4 0.0 copy-start
  11.4 0.0 copy-start.2
  11.4 0.6 %collective-permute-start.4 = (f32[256,128]{1,0:T(8,128)S(1)}, f32[256,128]{1,0:T(8,128)S(1)}, u32[]{:S(2)}, u32[]{:S(2)}) collective-permute-start(f32[256,128]{1,0:T(8,128)S(1)} %after.6.rest_1_), channel_id=1, source_target_pairs={{0,4},{4,0},{8,12},{12,8},{16,20},{20,16},{24,28},{28,24},{1,5},{5... | collective-permute-start | bytes 393224 | tf_op jit(solution)/shard_map/ppermute | solution.py:487
  12.0 2.1 %collective-permute-done.1.piece_ref = f32[256,128]{1,0:T(8,128)S(1)} collective-permute-done((f32[256,128]{1,0:T(8,128)S(1)}, f32[256,128]{1,0:T(8,128)S(1)}, u32[]{:S(2)}, u32[]{:S(2)}) %collective-permute-start.1) | collective-permute-done | bytes 131104 | tf_op jit(solution)/shard_map/ppermute | solution.py:474
  14.2 0.0 collective-permute-start.5
  14.2 0.0 collective-permute-done.2.piece_ref
  14.2 0.5 collective-permute-start.6
  14.7 0.0 collective-permute-done.3.rest_4_
  14.7 0.0 collective-permute-done.4.rest_5_
  14.7 0.8 %collective-permute-done.5.rest_6_ = f32[256,128]{1,0:T(8,128)S(1)} collective-permute-done((f32[256,128]{1,0:T(8,128)S(1)}, f32[256,128]{1,0:T(8,128)S(1)}, u32[]{:S(2)}, u32[]{:S(2)}) %collective-permute-start.5) | collective-permute-done | bytes 131104 | tf_op jit(solution)/shard_map/ppermute | solution.py:487
  15.5 0.2 collective-permute-done.6.rest_7_
  15.7 0.3 mix_forward.1
  16.0 1.1 %collective-permute-start.7 = (f32[256,128]{1,0:T(8,128)S(1)}, f32[256,128]{1,0:T(8,128)S(1)}, u32[]{:S(2)}, u32[]{:S(2)}) collective-permute-start(f32[256,128]{1,0:T(8,128)S(1)} %get-tuple-element.64), channel_id=1, source_target_pairs={{0,8},{4,12},{8,0},{12,4},{16,24},{20,28},{24,16},{28,20},{1,9},{5... | collective-permute-start | bytes 393224 | tf_op jit(solution)/shard_map/ppermute | solution.py:474
  17.1 1.0 %collective-permute-start.8 = (f32[256,128]{1,0:T(8,128)S(1)}, f32[256,128]{1,0:T(8,128)S(1)}, u32[]{:S(2)}, u32[]{:S(2)}) collective-permute-start(f32[256,128]{1,0:T(8,128)S(1)} %get-tuple-element.67), channel_id=1, source_target_pairs={{0,16},{4,20},{8,24},{12,28},{16,0},{20,4},{24,8},{28,12},{1,17},{... | collective-permute-start | bytes 393224 | tf_op jit(solution)/shard_map/ppermute | solution.py:474
  18.1 1.4 %collective-permute-start.9 = (f32[256,128]{1,0:T(8,128)S(1)}, f32[256,128]{1,0:T(8,128)S(1)}, u32[]{:S(2)}, u32[]{:S(2)}) collective-permute-start(f32[256,128]{1,0:T(8,128)S(1)} %get-tuple-element.68), channel_id=1, source_target_pairs={{0,24},{4,28},{8,16},{12,20},{16,8},{20,12},{24,0},{28,4},{1,25},{... | collective-permute-start | bytes 393224 | tf_op jit(solution)/shard_map/ppermute | solution.py:474
  19.5 3.9 %weighted_scores.1 = (bf16[8,3,256,256]{3,2,1,0:T(8,128)(2,1)S(1)}, f32[512,512]{1,0:T(8,128)S(1)}, bf16[512,1024]{1,0:T(8,128)(2,1)S(1)}, bf16[512,1024]{1,0:T(8,128)(2,1)S(1)}) custom-call(f32[9,128]{1,0:T(8,128)S(1)} %get-tuple-element.53.facts_ref, bf16[512,1024]{1,0:T(8,128)(2,1)S(1)} %get-tuple-element.54.query_ref, ...), custom_call_target="tpu_custom_call" | custom-call | flops 1073741824 | bytes 5242880 | tf_op jit(solution)/shard_map/weighted_scores/pallas_call | solution.py:580
  23.5 0.0 collective-permute-done.7.rest_1_.rest_3_
  23.5 0.5 attend.2
  24.0 0.0 collective-permute-done.8.rest_2_.rest_4_
  24.0 1.5 %collective-permute-done.9.rest_3_.rest_5_ = f32[256,128]{1,0:T(8,128)S(1)} collective-permute-done((f32[256,128]{1,0:T(8,128)S(1)}, f32[256,128]{1,0:T(8,128)S(1)}, u32[]{:S(2)}, u32[]{:S(2)}) %collective-permute-start.9) | collective-permute-done | bytes 131104 | tf_op jit(solution)/shard_map/ppermute | solution.py:474
  25.5 0.6 %attend.3 = (f32[512,512]{1,0:T(8,128)S(1)}, f32[8,128]{1,0:T(8,128)S(1)}) custom-call(bf16[512,1024]{1,0:T(8,128)(2,1)S(1)} %get-tuple-element.56.scaled_ref, bf16[512,1024]{1,0:T(8,128)(2,1)S(1)} %copy-done, f32[1,1024]{1,0:T(1,128)S(1)} %bitcast.4, f32[512,512]{1,0:T(8,128)S(1)} %get-tuple-element.66.local_ref, ...), custom_call_target="tpu_custom_call" | custom-call | flops 268435456 | bytes 5242880 | tf_op jit(solution)/shard_map/attend/pallas_call | solution.py:618
  26.1 1.6 %collective-permute-start.10 = (f32[8,128]{1,0:T(8,128)S(1)}, f32[8,128]{1,0:T(8,128)S(1)}, u32[]{:S(2)}, u32[]{:S(2)}) collective-permute-start(f32[8,128]{1,0:T(8,128)S(1)} %get-tuple-element.72.left_ref), channel_id=1, source_target_pairs={{0,1},{1,0},{2,3},{3,2},{4,5},{5,4},{6,7},{7,6},{8,9},{9,8},{10,11... | collective-permute-start | bytes 12296 | tf_op jit(solution)/shard_map/ppermute | solution.py:509
  27.8 2.0 %collective-permute-done.10.right_ref = f32[8,128]{1,0:T(8,128)S(1)} collective-permute-done((f32[8,128]{1,0:T(8,128)S(1)}, f32[8,128]{1,0:T(8,128)S(1)}, u32[]{:S(2)}, u32[]{:S(2)}) %collective-permute-start.10) | collective-permute-done | bytes 4128 | tf_op jit(solution)/shard_map/ppermute | solution.py:509
  29.8 2.6 %collective-permute-start.11 = (f32[8,128]{1,0:T(8,128)S(1)}, f32[8,128]{1,0:T(8,128)S(1)}, u32[]{:S(2)}, u32[]{:S(2)}) collective-permute-start(f32[8,128]{1,0:T(8,128)S(1)} %add_sums.1.rest_2_), channel_id=1, source_target_pairs={{0,2},{1,3},{2,0},{3,1},{4,6},{5,7},{6,4},{7,5},{8,10},{9,11},{10,... | collective-permute-start | bytes 12296 | tf_op jit(solution)/shard_map/ppermute | solution.py:509
  32.4 1.9 %collective-permute-done.11.rest_3_ = f32[8,128]{1,0:T(8,128)S(1)} collective-permute-done((f32[8,128]{1,0:T(8,128)S(1)}, f32[8,128]{1,0:T(8,128)S(1)}, u32[]{:S(2)}, u32[]{:S(2)}) %collective-permute-start.11) | collective-permute-done | bytes 4128 | tf_op jit(solution)/shard_map/ppermute | solution.py:509
  34.3 1.1 %state_grad.1 = (f32[256,128]{1,0:T(8,128)S(1)}, f32[256,128]{1,0:T(8,128)S(1)}, f32[256,128]{1,0:T(8,128)S(1)}, f32[256,128]{1,0:T(8,128)S(1)}, f32[512,128]{1,0:T(8,128)S(1)}, /*index=5*/f32[512,128]{1,0:T(8,128)S(1)}) custom-call(bf16[512,1024]{1,0:T(8,128)(2,1)S(1)} %get-tuple-element.56.scaled_ref, bf16[512,1024]{1,0:T(8,128)(2,1)S(1)} %copy-done, ...), custom_call_target="tpu_custom_call" | custom-call | tf_op jit(solution)/shard_map/state_grad/pallas_call | solution.py:633
  35.5 1.8 %collective-permute-start.14 = (f32[256,128]{1,0:T(8,128)S(1)}, f32[256,128]{1,0:T(8,128)S(1)}, u32[]{:S(2)}, u32[]{:S(2)}) collective-permute-start(f32[256,128]{1,0:T(8,128)S(1)} %get-tuple-element.89), channel_id=1, source_target_pairs={{0,24},{4,28},{8,16},{12,20},{16,8},{20,12},{24,0},{28,4},{1,25},{... | collective-permute-start | bytes 393224 | tf_op jit(solution)/shard_map/ppermute | solution.py:474
  37.3 0.5 collective-permute-start.13
  37.8 1.2 %collective-permute-start.12 = (f32[256,128]{1,0:T(8,128)S(1)}, f32[256,128]{1,0:T(8,128)S(1)}, u32[]{:S(2)}, u32[]{:S(2)}) collective-permute-start(f32[256,128]{1,0:T(8,128)S(1)} %get-tuple-element.86), channel_id=1, source_target_pairs={{0,8},{4,12},{8,0},{12,4},{16,24},{20,28},{24,16},{28,20},{1,9},{5... | collective-permute-start | bytes 393224 | tf_op jit(solution)/shard_map/ppermute | solution.py:474
  39.0 0.0 collective-permute-start.15
  39.0 3.2 %local_backward.2 = (bf16[512,512]{1,0:T(8,128)(2,1)S(1)}, bf16[512,512]{1,0:T(8,128)(2,1)S(1)}, bf16[512,512]{1,0:T(8,128)(2,1)S(1)}, bf16[512,512]{1,0:T(8,128)(2,1)S(1)}, f32[8,128]{1,0:T(8,128)S(1)}) custom-call(f32[9,128]{1,0:T(8,128)S(1)} %get-tuple-element.53.facts_ref, bf16[512,1024]{1,0:T(8,128)(2,1)S(1)} %get-tuple-element.54.query_ref, ...), custom_call_target="tpu_custom_call" | custom-call | flops 1073741824 | bytes 4194304 | tf_op jit(solution)/shard_map/local_backward/pallas_call | solution.py:655
  42.2 0.0 collective-permute-done.14.piece_ref
  42.2 0.6 %collective-permute-start.18 = (f32[256,128]{1,0:T(8,128)S(1)}, f32[256,128]{1,0:T(8,128)S(1)}, u32[]{:S(2)}, u32[]{:S(2)}) collective-permute-start(f32[256,128]{1,0:T(8,128)S(1)} %after.11.rest_3_), channel_id=1, source_target_pairs={{0,4},{4,0},{8,12},{12,8},{16,20},{20,16},{24,28},{28,24},{1,5},{5... | collective-permute-start | bytes 393224 | tf_op jit(solution)/shard_map/ppermute | solution.py:487
  42.8 0.0 collective-permute-done.13.piece_ref
  42.8 0.1 collective-permute-start.17
  42.9 0.0 collective-permute-done.12.piece_ref
  42.9 0.4 collective-permute-start.16
  43.3 0.0 collective-permute-done.15.rest_4_
  43.3 0.5 collective-permute-done.18.rest_7_
  43.8 0.4 collective-permute-done.17.rest_6_
  44.2 0.3 collective-permute-done.16.rest_5_
  44.4 0.3 mix_backward.1
  44.7 1.0 %collective-permute-start.21 = (f32[256,128]{1,0:T(8,128)S(1)}, f32[256,128]{1,0:T(8,128)S(1)}, u32[]{:S(2)}, u32[]{:S(2)}) collective-permute-start(f32[256,128]{1,0:T(8,128)S(1)} %get-tuple-element.93), channel_id=1, source_target_pairs={{0,8},{4,12},{8,0},{12,4},{16,24},{20,28},{24,16},{28,20},{1,9},{5... | collective-permute-start | bytes 393224 | tf_op jit(solution)/shard_map/ppermute | solution.py:474
  45.7 1.4 %collective-permute-start.19 = (f32[256,128]{1,0:T(8,128)S(1)}, f32[256,128]{1,0:T(8,128)S(1)}, u32[]{:S(2)}, u32[]{:S(2)}) collective-permute-start(f32[256,128]{1,0:T(8,128)S(1)} %get-tuple-element.91), channel_id=1, source_target_pairs={{0,16},{4,20},{8,24},{12,28},{16,0},{20,4},{24,8},{28,12},{1,17},{... | collective-permute-start | bytes 393224 | tf_op jit(solution)/shard_map/ppermute | solution.py:474
  47.1 1.2 %collective-permute-start.20 = (f32[256,128]{1,0:T(8,128)S(1)}, f32[256,128]{1,0:T(8,128)S(1)}, u32[]{:S(2)}, u32[]{:S(2)}) collective-permute-start(f32[256,128]{1,0:T(8,128)S(1)} %get-tuple-element.92), channel_id=1, source_target_pairs={{0,24},{4,28},{8,16},{12,20},{16,8},{20,12},{24,0},{28,4},{1,25},{... | collective-permute-start | bytes 393224 | tf_op jit(solution)/shard_map/ppermute | solution.py:474
  48.3 4.0 %local_backward.3 = (bf16[512,1024]{1,0:T(8,128)(2,1)}, bf16[512,1024]{1,0:T(8,128)(2,1)}, bf16[512,512]{1,0:T(8,128)(2,1)S(1)}, bf16[512,512]{1,0:T(8,128)(2,1)S(1)}) custom-call(f32[9,128]{1,0:T(8,128)S(1)} %get-tuple-element.53.facts_ref, bf16[512,1024]{1,0:T(8,128)(2,1)S(1)} %get-tuple-element.54.query_ref, ...), custom_call_target="tpu_custom_call" | custom-call | flops 1073741824 | bytes 4194304 | tf_op jit(solution)/shard_map/local_backward/pallas_call | solution.py:655
  52.3 0.0 collective-permute-done.21.rest_5_
  52.3 1.3 %finish.2 = (bf16[512,1024]{1,0:T(8,128)(2,1)}, bf16[512,1024]{1,0:T(8,128)(2,1)}) custom-call(bf16[512,1024]{1,0:T(8,128)(2,1)S(1)} %get-tuple-element.79.key_end_ref, bf16[512,1024]{1,0:T(8,128)(2,1)S(1)} %get-tuple-element.80.value_end_ref, bf16[512,512]{1,0:T(8,128)(2,1)S(1)} %get-tuple-element.81.rest_0_, ...), custom_call_target="tpu_custom_call" | custom-call | flops 268435456 | bytes 5242880 | tf_op jit(solution)/shard_map/finish/pallas_call | solution.py:679
  53.6 0.0 collective-permute-done.19.rest_6_
  53.6 0.1 collective-permute-done.20.rest_7_
  53.8 1.3 %finish.3 = (bf16[512,1024]{1,0:T(8,128)(2,1)}, bf16[512,1024]{1,0:T(8,128)(2,1)}) custom-call(bf16[512,1024]{1,0:T(8,128)(2,1)S(1)} %get-tuple-element.79.key_end_ref, bf16[512,1024]{1,0:T(8,128)(2,1)S(1)} %get-tuple-element.80.value_end_ref, bf16[512,512]{1,0:T(8,128)(2,1)S(1)} %get-tuple-element.81.rest_0_, ...), custom_call_target="tpu_custom_call", output_to_operand_aliasing={{0}: (10, {}), {1}: (11, {})} | custom-call | flops 268435456 | bytes 5242880 | tf_op jit(solution)/shard_map/finish/pallas_call | solution.py:679
  (12 shorter events, 0.0 us)
Async XLA Ops:
  0.6 7.3 %copy-start.1 = (bf16[512,1024]{1,0:T(8,128)(2,1)S(1)}, bf16[512,1024]{1,0:T(8,128)(2,1)}, u32[]{:S(2)}) copy-start(bf16[512,1024]{1,0:T(8,128)(2,1)} %query_ref.1) | copy-start | bytes 3145732
  0.6 1.7 %copy-start.3 = (s32[8]{0:T(128)S(1)}, s32[8]{0:T(128)}, u32[]{:S(2)}) copy-start(s32[8]{0:T(128)} %length_ref.1) | copy-start | bytes 100
  0.7 1.7 %copy-start.4 = (f32[8]{0:T(128)S(1)}, f32[8]{0:T(128)}, u32[]{:S(2)}) copy-start(f32[8]{0:T(128)} %rate_ref.1) | copy-start | bytes 100
  0.7 7.3 %copy-start.5 = (s32[8]{0:T(128)S(1)}, s32[8]{0:T(128)}, u32[]{:S(2)}) copy-start(s32[8]{0:T(128)} %parent_ref.1) | copy-start | bytes 100
  3.4 8.0 %collective-permute-start = (f32[256,128]{1,0:T(8,128)S(1)}, f32[256,128]{1,0:T(8,128)S(1)}, u32[]{:S(2)}, u32[]{:S(2)}) collective-permute-start(f32[256,128]{1,0:T(8,128)S(1)} %get-tuple-element.60), channel_id=1, source_target_pairs={{0,8},{4,12},{8,0},{12,4},{16,24},{20,28},{24,16},{28,20},{1,9},{5... | collective-permute-start | bytes 393224 | tf_op jit(solution)/shard_map/ppermute | solution.py:474
  6.4 7.8 %collective-permute-start.1 = (f32[256,128]{1,0:T(8,128)S(1)}, f32[256,128]{1,0:T(8,128)S(1)}, u32[]{:S(2)}, u32[]{:S(2)}) collective-permute-start(f32[256,128]{1,0:T(8,128)S(1)} %get-tuple-element.61), channel_id=1, source_target_pairs={{0,16},{4,20},{8,24},{12,28},{16,0},{20,4},{24,8},{28,12},{1,17},{... | collective-permute-start | bytes 393224 | tf_op jit(solution)/shard_map/ppermute | solution.py:474
  7.9 6.3 %collective-permute-start.2 = (f32[256,128]{1,0:T(8,128)S(1)}, f32[256,128]{1,0:T(8,128)S(1)}, u32[]{:S(2)}, u32[]{:S(2)}) collective-permute-start(f32[256,128]{1,0:T(8,128)S(1)} %get-tuple-element.62), channel_id=1, source_target_pairs={{0,24},{4,28},{8,16},{12,20},{16,8},{20,12},{24,0},{28,4},{1,25},{... | collective-permute-start | bytes 393224 | tf_op jit(solution)/shard_map/ppermute | solution.py:474
  7.9 6.8 %collective-permute-start.3 = (f32[256,128]{1,0:T(8,128)S(1)}, f32[256,128]{1,0:T(8,128)S(1)}, u32[]{:S(2)}, u32[]{:S(2)}) collective-permute-start(f32[256,128]{1,0:T(8,128)S(1)} %get-tuple-element.59.rest_0_), channel_id=1, source_target_pairs={{0,4},{4,0},{8,12},{12,8},{16,20},{20,16},{24,28},{28,24},{1,5},{5... | collective-permute-start | bytes 393224 | tf_op jit(solution)/shard_map/ppermute | solution.py:487
  11.4 12.1 %copy-start = (bf16[512,1024]{1,0:T(8,128)(2,1)S(1)}, bf16[512,1024]{1,0:T(8,128)(2,1)}, u32[]{:S(2)}) copy-start(bf16[512,1024]{1,0:T(8,128)(2,1)} %upstream_ref.9) | copy-start | bytes 3145732
  11.4 12.1 %copy-start.2 = (f32[1024]{0:T(1024)S(1)}, f32[1024]{0:T(1024)}, u32[]{:S(2)}) copy-start(f32[1024]{0:T(1024)} %param.12) | copy-start | bytes 12292
  11.4 3.2 %collective-permute-start.4 = (f32[256,128]{1,0:T(8,128)S(1)}, f32[256,128]{1,0:T(8,128)S(1)}, u32[]{:S(2)}, u32[]{:S(2)}) collective-permute-start(f32[256,128]{1,0:T(8,128)S(1)} %after.6.rest_1_), channel_id=1, source_target_pairs={{0,4},{4,0},{8,12},{12,8},{16,20},{20,16},{24,28},{28,24},{1,5},{5... | collective-permute-start | bytes 393224 | tf_op jit(solution)/shard_map/ppermute | solution.py:487
  14.2 1.3 %collective-permute-start.5 = (f32[256,128]{1,0:T(8,128)S(1)}, f32[256,128]{1,0:T(8,128)S(1)}, u32[]{:S(2)}, u32[]{:S(2)}) collective-permute-start(f32[256,128]{1,0:T(8,128)S(1)} %after.7.rest_2_), channel_id=1, source_target_pairs={{0,4},{4,0},{8,12},{12,8},{16,20},{20,16},{24,28},{28,24},{1,5},{5... | collective-permute-start | bytes 393224 | tf_op jit(solution)/shard_map/ppermute | solution.py:487
  14.2 1.5 %collective-permute-start.6 = (f32[256,128]{1,0:T(8,128)S(1)}, f32[256,128]{1,0:T(8,128)S(1)}, u32[]{:S(2)}, u32[]{:S(2)}) collective-permute-start(f32[256,128]{1,0:T(8,128)S(1)} %after.8.rest_3_), channel_id=1, source_target_pairs={{0,4},{4,0},{8,12},{12,8},{16,20},{20,16},{24,28},{28,24},{1,5},{5... | collective-permute-start | bytes 393224 | tf_op jit(solution)/shard_map/ppermute | solution.py:487
  16.0 7.5 %collective-permute-start.7 = (f32[256,128]{1,0:T(8,128)S(1)}, f32[256,128]{1,0:T(8,128)S(1)}, u32[]{:S(2)}, u32[]{:S(2)}) collective-permute-start(f32[256,128]{1,0:T(8,128)S(1)} %get-tuple-element.64), channel_id=1, source_target_pairs={{0,8},{4,12},{8,0},{12,4},{16,24},{20,28},{24,16},{28,20},{1,9},{5... | collective-permute-start | bytes 393224 | tf_op jit(solution)/shard_map/ppermute | solution.py:474
  17.1 6.9 %collective-permute-start.8 = (f32[256,128]{1,0:T(8,128)S(1)}, f32[256,128]{1,0:T(8,128)S(1)}, u32[]{:S(2)}, u32[]{:S(2)}) collective-permute-start(f32[256,128]{1,0:T(8,128)S(1)} %get-tuple-element.67), channel_id=1, source_target_pairs={{0,16},{4,20},{8,24},{12,28},{16,0},{20,4},{24,8},{28,12},{1,17},{... | collective-permute-start | bytes 393224 | tf_op jit(solution)/shard_map/ppermute | solution.py:474
  18.1 7.4 %collective-permute-start.9 = (f32[256,128]{1,0:T(8,128)S(1)}, f32[256,128]{1,0:T(8,128)S(1)}, u32[]{:S(2)}, u32[]{:S(2)}) collective-permute-start(f32[256,128]{1,0:T(8,128)S(1)} %get-tuple-element.68), channel_id=1, source_target_pairs={{0,24},{4,28},{8,16},{12,20},{16,8},{20,12},{24,0},{28,4},{1,25},{... | collective-permute-start | bytes 393224 | tf_op jit(solution)/shard_map/ppermute | solution.py:474
  26.1 3.7 %collective-permute-start.10 = (f32[8,128]{1,0:T(8,128)S(1)}, f32[8,128]{1,0:T(8,128)S(1)}, u32[]{:S(2)}, u32[]{:S(2)}) collective-permute-start(f32[8,128]{1,0:T(8,128)S(1)} %get-tuple-element.72.left_ref), channel_id=1, source_target_pairs={{0,1},{1,0},{2,3},{3,2},{4,5},{5,4},{6,7},{7,6},{8,9},{9,8},{10,11... | collective-permute-start | bytes 12296 | tf_op jit(solution)/shard_map/ppermute | solution.py:509
  29.8 4.5 %collective-permute-start.11 = (f32[8,128]{1,0:T(8,128)S(1)}, f32[8,128]{1,0:T(8,128)S(1)}, u32[]{:S(2)}, u32[]{:S(2)}) collective-permute-start(f32[8,128]{1,0:T(8,128)S(1)} %add_sums.1.rest_2_), channel_id=1, source_target_pairs={{0,2},{1,3},{2,0},{3,1},{4,6},{5,7},{6,4},{7,5},{8,10},{9,11},{10,... | collective-permute-start | bytes 12296 | tf_op jit(solution)/shard_map/ppermute | solution.py:509
  35.5 6.8 %collective-permute-start.14 = (f32[256,128]{1,0:T(8,128)S(1)}, f32[256,128]{1,0:T(8,128)S(1)}, u32[]{:S(2)}, u32[]{:S(2)}) collective-permute-start(f32[256,128]{1,0:T(8,128)S(1)} %get-tuple-element.89), channel_id=1, source_target_pairs={{0,24},{4,28},{8,16},{12,20},{16,8},{20,12},{24,0},{28,4},{1,25},{... | collective-permute-start | bytes 393224 | tf_op jit(solution)/shard_map/ppermute | solution.py:474
  37.3 5.5 %collective-permute-start.13 = (f32[256,128]{1,0:T(8,128)S(1)}, f32[256,128]{1,0:T(8,128)S(1)}, u32[]{:S(2)}, u32[]{:S(2)}) collective-permute-start(f32[256,128]{1,0:T(8,128)S(1)} %get-tuple-element.88), channel_id=1, source_target_pairs={{0,16},{4,20},{8,24},{12,28},{16,0},{20,4},{24,8},{28,12},{1,17},{... | collective-permute-start | bytes 393224 | tf_op jit(solution)/shard_map/ppermute | solution.py:474
  37.8 5.1 %collective-permute-start.12 = (f32[256,128]{1,0:T(8,128)S(1)}, f32[256,128]{1,0:T(8,128)S(1)}, u32[]{:S(2)}, u32[]{:S(2)}) collective-permute-start(f32[256,128]{1,0:T(8,128)S(1)} %get-tuple-element.86), channel_id=1, source_target_pairs={{0,8},{4,12},{8,0},{12,4},{16,24},{20,28},{24,16},{28,20},{1,9},{5... | collective-permute-start | bytes 393224 | tf_op jit(solution)/shard_map/ppermute | solution.py:474
  39.0 4.3 %collective-permute-start.15 = (f32[256,128]{1,0:T(8,128)S(1)}, f32[256,128]{1,0:T(8,128)S(1)}, u32[]{:S(2)}, u32[]{:S(2)}) collective-permute-start(f32[256,128]{1,0:T(8,128)S(1)} %get-tuple-element.85.rest_0_), channel_id=1, source_target_pairs={{0,4},{4,0},{8,12},{12,8},{16,20},{20,16},{24,28},{28,24},{1,5},{5... | collective-permute-start | bytes 393224 | tf_op jit(solution)/shard_map/ppermute | solution.py:487
  42.2 1.6 %collective-permute-start.18 = (f32[256,128]{1,0:T(8,128)S(1)}, f32[256,128]{1,0:T(8,128)S(1)}, u32[]{:S(2)}, u32[]{:S(2)}) collective-permute-start(f32[256,128]{1,0:T(8,128)S(1)} %after.11.rest_3_), channel_id=1, source_target_pairs={{0,4},{4,0},{8,12},{12,8},{16,20},{20,16},{24,28},{28,24},{1,5},{5... | collective-permute-start | bytes 393224 | tf_op jit(solution)/shard_map/ppermute | solution.py:487
  42.8 1.3 %collective-permute-start.17 = (f32[256,128]{1,0:T(8,128)S(1)}, f32[256,128]{1,0:T(8,128)S(1)}, u32[]{:S(2)}, u32[]{:S(2)}) collective-permute-start(f32[256,128]{1,0:T(8,128)S(1)} %after.10.rest_2_), channel_id=1, source_target_pairs={{0,4},{4,0},{8,12},{12,8},{16,20},{20,16},{24,28},{28,24},{1,5},{5... | collective-permute-start | bytes 393224 | tf_op jit(solution)/shard_map/ppermute | solution.py:487
  42.9 1.5 %collective-permute-start.16 = (f32[256,128]{1,0:T(8,128)S(1)}, f32[256,128]{1,0:T(8,128)S(1)}, u32[]{:S(2)}, u32[]{:S(2)}) collective-permute-start(f32[256,128]{1,0:T(8,128)S(1)} %after.9.rest_1_), channel_id=1, source_target_pairs={{0,4},{4,0},{8,12},{12,8},{16,20},{20,16},{24,28},{28,24},{1,5},{5... | collective-permute-start | bytes 393224 | tf_op jit(solution)/shard_map/ppermute | solution.py:487
  44.7 7.6 %collective-permute-start.21 = (f32[256,128]{1,0:T(8,128)S(1)}, f32[256,128]{1,0:T(8,128)S(1)}, u32[]{:S(2)}, u32[]{:S(2)}) collective-permute-start(f32[256,128]{1,0:T(8,128)S(1)} %get-tuple-element.93), channel_id=1, source_target_pairs={{0,8},{4,12},{8,0},{12,4},{16,24},{20,28},{24,16},{28,20},{1,9},{5... | collective-permute-start | bytes 393224 | tf_op jit(solution)/shard_map/ppermute | solution.py:474
  45.7 7.9 %collective-permute-start.19 = (f32[256,128]{1,0:T(8,128)S(1)}, f32[256,128]{1,0:T(8,128)S(1)}, u32[]{:S(2)}, u32[]{:S(2)}) collective-permute-start(f32[256,128]{1,0:T(8,128)S(1)} %get-tuple-element.91), channel_id=1, source_target_pairs={{0,16},{4,20},{8,24},{12,28},{16,0},{20,4},{24,8},{28,12},{1,17},{... | collective-permute-start | bytes 393224 | tf_op jit(solution)/shard_map/ppermute | solution.py:474
  47.1 6.7 %collective-permute-start.20 = (f32[256,128]{1,0:T(8,128)S(1)}, f32[256,128]{1,0:T(8,128)S(1)}, u32[]{:S(2)}, u32[]{:S(2)}) collective-permute-start(f32[256,128]{1,0:T(8,128)S(1)} %get-tuple-element.92), channel_id=1, source_target_pairs={{0,24},{4,28},{8,16},{12,20},{16,8},{20,12},{24,0},{28,4},{1,25},{... | collective-permute-start | bytes 393224 | tf_op jit(solution)/shard_map/ppermute | solution.py:474

commit v4 on v3

--- a/solution.py
+++ b/solution.py
@@ -66,8 +66,8 @@
     totals[index] = part if totals[index] is None else totals[index] + part
 
 
-def core_offset(slot, core):
-    crossed = (slot & ~3) | ((slot & 1) << 1) | ((slot & 2) >> 1)
+def core_offset(slot, core, chips):
+    crossed = slot ^ ((slot & 1) << 1) if chips >= 4 else slot
     return slot + core * (crossed - slot)
 
 
@@ -82,8 +82,7 @@
 
     def chip(self, slot, sibling=0):
         own = lax.axis_index("seg")
-        crossing = False
-        return (own // 2) ^ (core_offset(slot, (own % 2) ^ sibling) if crossing else slot)
+        return (own // 2) ^ core_offset(slot, (own % 2) ^ sibling, self.chips)
 
     def head(self, place):
         if not self.each:
@@ -470,7 +469,7 @@
 def exchange(pieces, count):
     moved = [pieces[0]]
     for slot in range(1, len(pieces)):
-        pairs = [(at, at ^ (2 * (core_offset(slot, at % 2) if False else slot))) for at in range(count)]
+        pairs = [(at, at ^ (2 * core_offset(slot, at % 2, len(pieces)))) for at in range(count)]
         moved.append(lax.ppermute(pieces[slot], "seg", pairs))
     return moved
 
@@ -523,19 +522,18 @@
     whole = pltpu.VMEM((wide, size), f32)
     columns = shape((rows, size), f32)
     offsets = list(range(chips))
-    sends = [[slot for slot in offsets if 0 < slot < 3], [slot for slot in offsets if slot == 0 or slot >= 3]]
+    order = [slot for slot in offsets if 0 < slot < 3] + [slot for slot in offsets if slot == 0 or slot >= 3]
     groups = [group for group in (layout.places(offsets[:2]), layout.places(offsets[2:])) if group]
-    whole_sends = [sends[0] + sends[1]]
     early, late = groups if len(groups) == 2 else (groups[0], [])
+
+    def in_order(parts):
+        return [dict(zip(order, parts))[slot] for slot in offsets]
 
     def near_shape(places, dtype):
         return shape((rows, len(places) * size), dtype)
 
     def near_scratch(places, dtype):
         return pltpu.VMEM((rows, len(places) * size), dtype)
-
-    def in_order(parts):
-        return [dict(zip(sends[0] + sends[1], parts))[offset] for offset in offsets]
 
     key_near, value_near = pl.pallas_call(
         near_kernel,
@@ -548,7 +546,7 @@
     )(key_tokens, values, queries)
 
     states = []
-    for chosen in whole_sends:
+    for chosen in [order]:
         states += pl.pallas_call(
             functools.partial(state_kernel, layout, chosen),
             out_shape=[piece_shape] * len(chosen),
@@ -592,7 +590,7 @@
         mine = mine[:1] + [after(piece, before) for piece in mine[1:]]
         other = swap_cores(mine, seg_count)
         mixed = []
-        for chosen in whole_sends:
+        for chosen in [order]:
             mixed += pl.pallas_call(
                 functools.partial(mix_kernel, layout, backward, chosen),
                 out_shape=[piece_shape] * len(chosen),
@@ -628,7 +626,7 @@
     sum_parts = head_sums(before[0], head_count)
 
     state_grads, norms = [], []
-    for chosen in whole_sends:
+    for chosen in [order]:
         first = not norms
         parts = pl.pallas_call(
             functools.partial(state_grad_kernel, layout, groups, chosen, len(sum_parts) if first else 0, width),

time: 55.4 us -> 55.3 us (level)
    ppermute x8, starting transfers between devices: 2.16 us -> 1.42 us  [swap_cores(): return [lax.ppermute(piece, 'seg', pairs) for piece in pieces]]
    ppermute x8, waiting for transfers between devices: 2.11 us -> 2.68 us  [swap_cores(): return [lax.ppermute(piece, 'seg', pairs) for piece in pieces]]
  transfers between devices with their start and end apart: 22 -> 22, of which waited for: 10 -> 13; matrix products, arithmetic and copies ran while one was open for 0% -> 0% of each run, Pallas kernels for 30% -> 30%
where the time goes in v4:
time: 55.3 us; the launch traced here: 55.1 us
  Pallas kernels  22.7 us (41%)
  starting transfers between devices  21.4 us (39%)
  waiting for transfers between devices  10 us (18%)
  between operations  1.03 us (2%)
    ppermute x12, starting transfers between devices, exchange(): moved.append(lax.ppermute(pieces[slot], 'seg', pairs))  15.2 us
    pallas_call x2, Pallas kernels, backward(): pl.pallas_call(functools.partial(backward_kernel, layout, groups, places,...  7.22 us
    ppermute x2, starting transfers between devices, head_sums(): lax.ppermute(parts[0], 'head', [(at, at ^ step) for at in range(count)])  4.74 us
    pallas_call x1, Pallas kernels, local(): pl.pallas_call(functools.partial(weighted_kernel, layout, late), out_shap...  3.96 us
    ppermute x12, waiting for transfers between devices, exchange(): moved.append(lax.ppermute(pieces[slot], 'seg', pairs))  3.9 us
    pallas_call x1, Pallas kernels, local(): pl.pallas_call(functools.partial(local_kernel, layout, early), out_shape=...  3.48 us
    ppermute x2, waiting for transfers between devices, head_sums(): lax.ppermute(parts[0], 'head', [(at, at ^ step) for at in range(count)])  3.44 us
    ppermute x8, waiting for transfers between devices, swap_cores(): return [lax.ppermute(piece, 'seg', pairs) for piece in pieces]  2.68 us
  transfers between devices with their start and end apart: 22, of which 13 were waited for; matrix products, arithmetic and copies ran while one was open for 0% of the time, Pallas kernels for 30%

profile of v4, /device:TPU:0, one launch (start us, length us, event | category | flops | bytes accessed | tf_op | source)
XLA Modules:
  0.0 55.1 jit_solution(249210666831736651)
XLA Ops:
  0.6 0.0 copy-start.1
  0.6 0.0 copy-start.3
  0.7 1.6 %bring_near.1 = (bf16[512,1024]{1,0:T(8,128)(2,1)S(1)}, bf16[512,1024]{1,0:T(8,128)(2,1)S(1)}) custom-call(bf16[512,1024]{1,0:T(8,128)(2,1)} %key_any.1, bf16[512,1024]{1,0:T(8,128)(2,1)} %value_any.1, bf16[512,1024]{1,0:T(8,128)(2,1)} %query_ref.1), custom_call_target="tpu_custom_call" | custom-call | tf_op jit(solution)/shard_map/bring_near/pallas_call | solution.py:538
  2.3 1.0 %block_state.1 = (f32[256,128]{1,0:T(8,128)S(1)}, f32[256,128]{1,0:T(8,128)S(1)}, f32[256,128]{1,0:T(8,128)S(1)}, f32[256,128]{1,0:T(8,128)S(1)}) custom-call(s32[1,8]{1,0:T(1,128)S(1)} %bitcast.8, f32[1,8]{1,0:T(1,128)S(1)} %bitcast.9, bf16[512,1024]{1,0:T(8,128)(2,1)S(1)} %get-tuple-element.51.key_ref, bf16[512,1024]{1,0:T(8,128)(2,1)S(1)} %get-tuple-element.52.value_ref), custom_call_target="tpu_custom_call" | custom-call | tf_op jit(solution)/shard_map/block_state/pallas_call | solution.py:550
  3.4 3.0 %collective-permute-start = (f32[256,128]{1,0:T(8,128)S(1)}, f32[256,128]{1,0:T(8,128)S(1)}, u32[]{:S(2)}, u32[]{:S(2)}) collective-permute-start(f32[256,128]{1,0:T(8,128)S(1)} %get-tuple-element.60), channel_id=1, source_target_pairs={{0,8},{4,28},{8,0},{12,20},{16,24},{20,12},{24,16},{28,4},{1,9},{5... | collective-permute-start | bytes 393224 | tf_op jit(solution)/shard_map/ppermute | solution.py:473
  6.4 1.5 %collective-permute-start.1 = (f32[256,128]{1,0:T(8,128)S(1)}, f32[256,128]{1,0:T(8,128)S(1)}, u32[]{:S(2)}, u32[]{:S(2)}) collective-permute-start(f32[256,128]{1,0:T(8,128)S(1)} %get-tuple-element.61), channel_id=1, source_target_pairs={{0,16},{4,20},{8,24},{12,28},{16,0},{20,4},{24,8},{28,12},{1,17},{... | collective-permute-start | bytes 393224 | tf_op jit(solution)/shard_map/ppermute | solution.py:473
  7.9 0.0 collective-permute-start.2
  7.9 0.0 collective-permute-start.3
  7.9 0.0 copy-done.5
  7.9 3.5 %local_attention.1 = (f32[512,512]{1,0:T(8,128)S(1)}, bf16[512,1024]{1,0:T(8,128)(2,1)S(1)}, bf16[512,1024]{1,0:T(8,128)(2,1)S(1)}, f32[64,8,128]{2,1,0:T(8,128)S(1)}, f32[9,128]{1,0:T(8,128)S(1)}) custom-call(s32[8]{0:T(128)S(1)} %copy-done.3, s32[8]{0:T(128)S(1)} %copy-done.5, f32[8]{0:T(128)S(1)} %copy-done.4, bf16[512,1024]{1,0:T(8,128)(2,1)S(1)} %copy-done.1, ...), custom_call_target="tpu_custom_call" | custom-call | flops 536870912 | bytes 5242880 | tf_op jit(solution)/shard_map/local_attention/pallas_call | solution.py:560
  11.4 0.0 collective-permute-done.piece_ref
  11.4 0.0 copy-start
  11.4 0.0 copy-start.2
  11.5 0.6 %collective-permute-start.4 = (f32[256,128]{1,0:T(8,128)S(1)}, f32[256,128]{1,0:T(8,128)S(1)}, u32[]{:S(2)}, u32[]{:S(2)}) collective-permute-start(f32[256,128]{1,0:T(8,128)S(1)} %after.6.rest_1_), channel_id=1, source_target_pairs={{0,4},{4,0},{8,12},{12,8},{16,20},{20,16},{24,28},{28,24},{1,5},{5... | collective-permute-start | bytes 393224 | tf_op jit(solution)/shard_map/ppermute | solution.py:486
  12.0 1.0 %collective-permute-done.1.piece_ref = f32[256,128]{1,0:T(8,128)S(1)} collective-permute-done((f32[256,128]{1,0:T(8,128)S(1)}, f32[256,128]{1,0:T(8,128)S(1)}, u32[]{:S(2)}, u32[]{:S(2)}) %collective-permute-start.1) | collective-permute-done | bytes 131104 | tf_op jit(solution)/shard_map/ppermute | solution.py:473
  13.0 0.0 collective-permute-start.5
  13.0 0.7 %collective-permute-done.2.piece_ref = f32[256,128]{1,0:T(8,128)S(1)} collective-permute-done((f32[256,128]{1,0:T(8,128)S(1)}, f32[256,128]{1,0:T(8,128)S(1)}, u32[]{:S(2)}, u32[]{:S(2)}) %collective-permute-start.2) | collective-permute-done | bytes 131104 | tf_op jit(solution)/shard_map/ppermute | solution.py:473
  13.8 0.0 collective-permute-start.6
  13.8 0.0 collective-permute-done.3.rest_4_
  13.8 0.0 collective-permute-done.4.rest_5_
  13.8 0.6 %collective-permute-done.5.rest_6_ = f32[256,128]{1,0:T(8,128)S(1)} collective-permute-done((f32[256,128]{1,0:T(8,128)S(1)}, f32[256,128]{1,0:T(8,128)S(1)}, u32[]{:S(2)}, u32[]{:S(2)}) %collective-permute-start.5) | collective-permute-done | bytes 131104 | tf_op jit(solution)/shard_map/ppermute | solution.py:486
  14.4 0.7 %collective-permute-done.6.rest_7_ = f32[256,128]{1,0:T(8,128)S(1)} collective-permute-done((f32[256,128]{1,0:T(8,128)S(1)}, f32[256,128]{1,0:T(8,128)S(1)}, u32[]{:S(2)}, u32[]{:S(2)}) %collective-permute-start.6) | collective-permute-done | bytes 131104 | tf_op jit(solution)/shard_map/ppermute | solution.py:486
  15.1 0.3 mix_forward.1
  15.4 1.6 %collective-permute-start.7 = (f32[256,128]{1,0:T(8,128)S(1)}, f32[256,128]{1,0:T(8,128)S(1)}, u32[]{:S(2)}, u32[]{:S(2)}) collective-permute-start(f32[256,128]{1,0:T(8,128)S(1)} %get-tuple-element.64), channel_id=1, source_target_pairs={{0,8},{4,28},{8,0},{12,20},{16,24},{20,12},{24,16},{28,4},{1,9},{5... | collective-permute-start | bytes 393224 | tf_op jit(solution)/shard_map/ppermute | solution.py:473
  17.0 1.5 %collective-permute-start.8 = (f32[256,128]{1,0:T(8,128)S(1)}, f32[256,128]{1,0:T(8,128)S(1)}, u32[]{:S(2)}, u32[]{:S(2)}) collective-permute-start(f32[256,128]{1,0:T(8,128)S(1)} %get-tuple-element.67), channel_id=1, source_target_pairs={{0,16},{4,20},{8,24},{12,28},{16,0},{20,4},{24,8},{28,12},{1,17},{... | collective-permute-start | bytes 393224 | tf_op jit(solution)/shard_map/ppermute | solution.py:473
  18.5 0.4 collective-permute-start.9
  19.0 4.0 %weighted_scores.1 = (bf16[8,3,256,256]{3,2,1,0:T(8,128)(2,1)S(1)}, f32[512,512]{1,0:T(8,128)S(1)}, bf16[512,1024]{1,0:T(8,128)(2,1)S(1)}, bf16[512,1024]{1,0:T(8,128)(2,1)S(1)}) custom-call(f32[9,128]{1,0:T(8,128)S(1)} %get-tuple-element.53.facts_ref, bf16[512,1024]{1,0:T(8,128)(2,1)S(1)} %get-tuple-element.54.query_ref, ...), custom_call_target="tpu_custom_call" | custom-call | flops 1073741824 | bytes 5242880 | tf_op jit(solution)/shard_map/weighted_scores/pallas_call | solution.py:578
  22.9 0.0 collective-permute-done.7.rest_1_.rest_3_
  22.9 0.0 copy-done
  23.0 0.0 copy-done.2
  23.0 0.5 attend.2
  23.4 0.7 %collective-permute-done.8.rest_2_.rest_4_ = f32[256,128]{1,0:T(8,128)S(1)} collective-permute-done((f32[256,128]{1,0:T(8,128)S(1)}, f32[256,128]{1,0:T(8,128)S(1)}, u32[]{:S(2)}, u32[]{:S(2)}) %collective-permute-start.8) | collective-permute-done | bytes 131104 | tf_op jit(solution)/shard_map/ppermute | solution.py:473
  24.1 0.6 %collective-permute-done.9.rest_3_.rest_5_ = f32[256,128]{1,0:T(8,128)S(1)} collective-permute-done((f32[256,128]{1,0:T(8,128)S(1)}, f32[256,128]{1,0:T(8,128)S(1)}, u32[]{:S(2)}, u32[]{:S(2)}) %collective-permute-start.9) | collective-permute-done | bytes 131104 | tf_op jit(solution)/shard_map/ppermute | solution.py:473
  24.8 0.6 %attend.3 = (f32[512,512]{1,0:T(8,128)S(1)}, f32[8,128]{1,0:T(8,128)S(1)}) custom-call(bf16[512,1024]{1,0:T(8,128)(2,1)S(1)} %get-tuple-element.56.scaled_ref, bf16[512,1024]{1,0:T(8,128)(2,1)S(1)} %copy-done, f32[1,1024]{1,0:T(1,128)S(1)} %bitcast.4, f32[512,512]{1,0:T(8,128)S(1)} %get-tuple-element.66.local_ref, ...), custom_call_target="tpu_custom_call" | custom-call | flops 268435456 | bytes 5242880 | tf_op jit(solution)/shard_map/attend/pallas_call | solution.py:616
  25.4 1.9 %collective-permute-start.10 = (f32[8,128]{1,0:T(8,128)S(1)}, f32[8,128]{1,0:T(8,128)S(1)}, u32[]{:S(2)}, u32[]{:S(2)}) collective-permute-start(f32[8,128]{1,0:T(8,128)S(1)} %get-tuple-element.72.left_ref), channel_id=1, source_target_pairs={{0,1},{1,0},{2,3},{3,2},{4,5},{5,4},{6,7},{7,6},{8,9},{9,8},{10,11... | collective-permute-start | bytes 12296 | tf_op jit(solution)/shard_map/ppermute | solution.py:508
  27.3 1.8 %collective-permute-done.10.right_ref = f32[8,128]{1,0:T(8,128)S(1)} collective-permute-done((f32[8,128]{1,0:T(8,128)S(1)}, f32[8,128]{1,0:T(8,128)S(1)}, u32[]{:S(2)}, u32[]{:S(2)}) %collective-permute-start.10) | collective-permute-done | bytes 4128 | tf_op jit(solution)/shard_map/ppermute | solution.py:508
  29.0 2.8 %collective-permute-start.11 = (f32[8,128]{1,0:T(8,128)S(1)}, f32[8,128]{1,0:T(8,128)S(1)}, u32[]{:S(2)}, u32[]{:S(2)}) collective-permute-start(f32[8,128]{1,0:T(8,128)S(1)} %add_sums.1.rest_2_), channel_id=1, source_target_pairs={{0,2},{1,3},{2,0},{3,1},{4,6},{5,7},{6,4},{7,5},{8,10},{9,11},{10,... | collective-permute-start | bytes 12296 | tf_op jit(solution)/shard_map/ppermute | solution.py:508
  31.9 1.7 %collective-permute-done.11.rest_3_ = f32[8,128]{1,0:T(8,128)S(1)} collective-permute-done((f32[8,128]{1,0:T(8,128)S(1)}, f32[8,128]{1,0:T(8,128)S(1)}, u32[]{:S(2)}, u32[]{:S(2)}) %collective-permute-start.11) | collective-permute-done | bytes 4128 | tf_op jit(solution)/shard_map/ppermute | solution.py:508
  33.5 1.1 %state_grad.1 = (f32[256,128]{1,0:T(8,128)S(1)}, f32[256,128]{1,0:T(8,128)S(1)}, f32[256,128]{1,0:T(8,128)S(1)}, f32[256,128]{1,0:T(8,128)S(1)}, f32[512,128]{1,0:T(8,128)S(1)}, /*index=5*/f32[512,128]{1,0:T(8,128)S(1)}) custom-call(bf16[512,1024]{1,0:T(8,128)(2,1)S(1)} %get-tuple-element.56.scaled_ref, bf16[512,1024]{1,0:T(8,128)(2,1)S(1)} %copy-done, ...), custom_call_target="tpu_custom_call" | custom-call | tf_op jit(solution)/shard_map/state_grad/pallas_call | solution.py:631
  34.7 2.3 %collective-permute-start.14 = (f32[256,128]{1,0:T(8,128)S(1)}, f32[256,128]{1,0:T(8,128)S(1)}, u32[]{:S(2)}, u32[]{:S(2)}) collective-permute-start(f32[256,128]{1,0:T(8,128)S(1)} %get-tuple-element.89), channel_id=1, source_target_pairs={{0,24},{4,12},{8,16},{12,4},{16,8},{20,28},{24,0},{28,20},{1,25},{... | collective-permute-start | bytes 393224 | tf_op jit(solution)/shard_map/ppermute | solution.py:473
  37.0 0.8 %collective-permute-start.13 = (f32[256,128]{1,0:T(8,128)S(1)}, f32[256,128]{1,0:T(8,128)S(1)}, u32[]{:S(2)}, u32[]{:S(2)}) collective-permute-start(f32[256,128]{1,0:T(8,128)S(1)} %get-tuple-element.88), channel_id=1, source_target_pairs={{0,16},{4,20},{8,24},{12,28},{16,0},{20,4},{24,8},{28,12},{1,17},{... | collective-permute-start | bytes 393224 | tf_op jit(solution)/shard_map/ppermute | solution.py:473
  37.8 0.5 collective-permute-start.12
  38.2 0.0 collective-permute-start.15
  38.2 3.2 %local_backward.2 = (bf16[512,512]{1,0:T(8,128)(2,1)S(1)}, bf16[512,512]{1,0:T(8,128)(2,1)S(1)}, bf16[512,512]{1,0:T(8,128)(2,1)S(1)}, bf16[512,512]{1,0:T(8,128)(2,1)S(1)}, f32[8,128]{1,0:T(8,128)S(1)}) custom-call(f32[9,128]{1,0:T(8,128)S(1)} %get-tuple-element.53.facts_ref, bf16[512,1024]{1,0:T(8,128)(2,1)S(1)} %get-tuple-element.54.query_ref, ...), custom_call_target="tpu_custom_call" | custom-call | flops 1073741824 | bytes 4194304 | tf_op jit(solution)/shard_map/local_backward/pallas_call | solution.py:653
  41.4 0.0 collective-permute-done.14.piece_ref
  41.4 0.6 %collective-permute-start.18 = (f32[256,128]{1,0:T(8,128)S(1)}, f32[256,128]{1,0:T(8,128)S(1)}, u32[]{:S(2)}, u32[]{:S(2)}) collective-permute-start(f32[256,128]{1,0:T(8,128)S(1)} %after.11.rest_3_), channel_id=1, source_target_pairs={{0,4},{4,0},{8,12},{12,8},{16,20},{20,16},{24,28},{28,24},{1,5},{5... | collective-permute-start | bytes 393224 | tf_op jit(solution)/shard_map/ppermute | solution.py:486
  42.0 0.0 collective-permute-done.13.piece_ref
  42.0 0.3 collective-permute-start.17
  42.3 0.4 collective-permute-done.12.piece_ref
  42.7 0.0 collective-permute-start.16
  42.7 0.0 collective-permute-done.15.rest_4_
  42.7 0.3 collective-permute-done.18.rest_7_
  43.0 0.4 collective-permute-done.17.rest_6_
  43.4 0.7 %collective-permute-done.16.rest_5_ = f32[256,128]{1,0:T(8,128)S(1)} collective-permute-done((f32[256,128]{1,0:T(8,128)S(1)}, f32[256,128]{1,0:T(8,128)S(1)}, u32[]{:S(2)}, u32[]{:S(2)}) %collective-permute-start.16) | collective-permute-done | bytes 131104 | tf_op jit(solution)/shard_map/ppermute | solution.py:486
  44.1 0.3 mix_backward.1
  44.4 1.2 %collective-permute-start.21 = (f32[256,128]{1,0:T(8,128)S(1)}, f32[256,128]{1,0:T(8,128)S(1)}, u32[]{:S(2)}, u32[]{:S(2)}) collective-permute-start(f32[256,128]{1,0:T(8,128)S(1)} %get-tuple-element.93), channel_id=1, source_target_pairs={{0,8},{4,28},{8,0},{12,20},{16,24},{20,12},{24,16},{28,4},{1,9},{5... | collective-permute-start | bytes 393224 | tf_op jit(solution)/shard_map/ppermute | solution.py:473
  45.6 1.2 %collective-permute-start.19 = (f32[256,128]{1,0:T(8,128)S(1)}, f32[256,128]{1,0:T(8,128)S(1)}, u32[]{:S(2)}, u32[]{:S(2)}) collective-permute-start(f32[256,128]{1,0:T(8,128)S(1)} %get-tuple-element.91), channel_id=1, source_target_pairs={{0,16},{4,20},{8,24},{12,28},{16,0},{20,4},{24,8},{28,12},{1,17},{... | collective-permute-start | bytes 393224 | tf_op jit(solution)/shard_map/ppermute | solution.py:473
  46.8 1.1 %collective-permute-start.20 = (f32[256,128]{1,0:T(8,128)S(1)}, f32[256,128]{1,0:T(8,128)S(1)}, u32[]{:S(2)}, u32[]{:S(2)}) collective-permute-start(f32[256,128]{1,0:T(8,128)S(1)} %get-tuple-element.92), channel_id=1, source_target_pairs={{0,24},{4,12},{8,16},{12,4},{16,8},{20,28},{24,0},{28,20},{1,25},{... | collective-permute-start | bytes 393224 | tf_op jit(solution)/shard_map/ppermute | solution.py:473
  47.9 4.0 %local_backward.3 = (bf16[512,1024]{1,0:T(8,128)(2,1)}, bf16[512,1024]{1,0:T(8,128)(2,1)}, bf16[512,512]{1,0:T(8,128)(2,1)S(1)}, bf16[512,512]{1,0:T(8,128)(2,1)S(1)}) custom-call(f32[9,128]{1,0:T(8,128)S(1)} %get-tuple-element.53.facts_ref, bf16[512,1024]{1,0:T(8,128)(2,1)S(1)} %get-tuple-element.54.query_ref, ...), custom_call_target="tpu_custom_call" | custom-call | flops 1073741824 | bytes 4194304 | tf_op jit(solution)/shard_map/local_backward/pallas_call | solution.py:653
  52.0 0.0 collective-permute-done.21.rest_5_
  52.0 1.3 %finish.2 = (bf16[512,1024]{1,0:T(8,128)(2,1)}, bf16[512,1024]{1,0:T(8,128)(2,1)}) custom-call(bf16[512,1024]{1,0:T(8,128)(2,1)S(1)} %get-tuple-element.79.key_end_ref, bf16[512,1024]{1,0:T(8,128)(2,1)S(1)} %get-tuple-element.80.value_end_ref, bf16[512,512]{1,0:T(8,128)(2,1)S(1)} %get-tuple-element.81.rest_0_, ...), custom_call_target="tpu_custom_call" | custom-call | flops 268435456 | bytes 5242880 | tf_op jit(solution)/shard_map/finish/pallas_call | solution.py:677
  53.3 0.0 collective-permute-done.19.rest_6_
  53.3 0.4 collective-permute-done.20.rest_7_
  53.7 1.3 %finish.3 = (bf16[512,1024]{1,0:T(8,128)(2,1)}, bf16[512,1024]{1,0:T(8,128)(2,1)}) custom-call(bf16[512,1024]{1,0:T(8,128)(2,1)S(1)} %get-tuple-element.79.key_end_ref, bf16[512,1024]{1,0:T(8,128)(2,1)S(1)} %get-tuple-element.80.value_end_ref, bf16[512,512]{1,0:T(8,128)(2,1)S(1)} %get-tuple-element.81.rest_0_, ...), custom_call_target="tpu_custom_call", output_to_operand_aliasing={{0}: (10, {}), {1}: (11, {})} | custom-call | flops 268435456 | bytes 5242880 | tf_op jit(solution)/shard_map/finish/pallas_call | solution.py:677
  (12 shorter events, 0.0 us)
Async XLA Ops:
  0.6 7.3 %copy-start.1 = (bf16[512,1024]{1,0:T(8,128)(2,1)S(1)}, bf16[512,1024]{1,0:T(8,128)(2,1)}, u32[]{:S(2)}) copy-start(bf16[512,1024]{1,0:T(8,128)(2,1)} %query_ref.1) | copy-start | bytes 3145732
  0.6 1.7 %copy-start.3 = (s32[8]{0:T(128)S(1)}, s32[8]{0:T(128)}, u32[]{:S(2)}) copy-start(s32[8]{0:T(128)} %length_ref.1) | copy-start | bytes 100
  0.7 1.7 %copy-start.4 = (f32[8]{0:T(128)S(1)}, f32[8]{0:T(128)}, u32[]{:S(2)}) copy-start(f32[8]{0:T(128)} %rate_ref.1) | copy-start | bytes 100
  0.7 7.3 %copy-start.5 = (s32[8]{0:T(128)S(1)}, s32[8]{0:T(128)}, u32[]{:S(2)}) copy-start(s32[8]{0:T(128)} %parent_ref.1) | copy-start | bytes 100
  3.4 8.0 %collective-permute-start = (f32[256,128]{1,0:T(8,128)S(1)}, f32[256,128]{1,0:T(8,128)S(1)}, u32[]{:S(2)}, u32[]{:S(2)}) collective-permute-start(f32[256,128]{1,0:T(8,128)S(1)} %get-tuple-element.60), channel_id=1, source_target_pairs={{0,8},{4,28},{8,0},{12,20},{16,24},{20,12},{24,16},{28,4},{1,9},{5... | collective-permute-start | bytes 393224 | tf_op jit(solution)/shard_map/ppermute | solution.py:473
  6.4 6.6 %collective-permute-start.1 = (f32[256,128]{1,0:T(8,128)S(1)}, f32[256,128]{1,0:T(8,128)S(1)}, u32[]{:S(2)}, u32[]{:S(2)}) collective-permute-start(f32[256,128]{1,0:T(8,128)S(1)} %get-tuple-element.61), channel_id=1, source_target_pairs={{0,16},{4,20},{8,24},{12,28},{16,0},{20,4},{24,8},{28,12},{1,17},{... | collective-permute-start | bytes 393224 | tf_op jit(solution)/shard_map/ppermute | solution.py:473
  7.9 5.9 %collective-permute-start.2 = (f32[256,128]{1,0:T(8,128)S(1)}, f32[256,128]{1,0:T(8,128)S(1)}, u32[]{:S(2)}, u32[]{:S(2)}) collective-permute-start(f32[256,128]{1,0:T(8,128)S(1)} %get-tuple-element.62), channel_id=1, source_target_pairs={{0,24},{4,12},{8,16},{12,4},{16,8},{20,28},{24,0},{28,20},{1,25},{... | collective-permute-start | bytes 393224 | tf_op jit(solution)/shard_map/ppermute | solution.py:473
  7.9 5.9 %collective-permute-start.3 = (f32[256,128]{1,0:T(8,128)S(1)}, f32[256,128]{1,0:T(8,128)S(1)}, u32[]{:S(2)}, u32[]{:S(2)}) collective-permute-start(f32[256,128]{1,0:T(8,128)S(1)} %get-tuple-element.59.rest_0_), channel_id=1, source_target_pairs={{0,4},{4,0},{8,12},{12,8},{16,20},{20,16},{24,28},{28,24},{1,5},{5... | collective-permute-start | bytes 393224 | tf_op jit(solution)/shard_map/ppermute | solution.py:486
  11.4 11.5 %copy-start = (bf16[512,1024]{1,0:T(8,128)(2,1)S(1)}, bf16[512,1024]{1,0:T(8,128)(2,1)}, u32[]{:S(2)}) copy-start(bf16[512,1024]{1,0:T(8,128)(2,1)} %upstream_ref.9) | copy-start | bytes 3145732
  11.4 11.5 %copy-start.2 = (f32[1024]{0:T(1024)S(1)}, f32[1024]{0:T(1024)}, u32[]{:S(2)}) copy-start(f32[1024]{0:T(1024)} %param.12) | copy-start | bytes 12292
  11.5 2.3 %collective-permute-start.4 = (f32[256,128]{1,0:T(8,128)S(1)}, f32[256,128]{1,0:T(8,128)S(1)}, u32[]{:S(2)}, u32[]{:S(2)}) collective-permute-start(f32[256,128]{1,0:T(8,128)S(1)} %after.6.rest_1_), channel_id=1, source_target_pairs={{0,4},{4,0},{8,12},{12,8},{16,20},{20,16},{24,28},{28,24},{1,5},{5... | collective-permute-start | bytes 393224 | tf_op jit(solution)/shard_map/ppermute | solution.py:486
  13.0 1.3 %collective-permute-start.5 = (f32[256,128]{1,0:T(8,128)S(1)}, f32[256,128]{1,0:T(8,128)S(1)}, u32[]{:S(2)}, u32[]{:S(2)}) collective-permute-start(f32[256,128]{1,0:T(8,128)S(1)} %after.7.rest_2_), channel_id=1, source_target_pairs={{0,4},{4,0},{8,12},{12,8},{16,20},{20,16},{24,28},{28,24},{1,5},{5... | collective-permute-start | bytes 393224 | tf_op jit(solution)/shard_map/ppermute | solution.py:486
  13.8 1.3 %collective-permute-start.6 = (f32[256,128]{1,0:T(8,128)S(1)}, f32[256,128]{1,0:T(8,128)S(1)}, u32[]{:S(2)}, u32[]{:S(2)}) collective-permute-start(f32[256,128]{1,0:T(8,128)S(1)} %after.8.rest_3_), channel_id=1, source_target_pairs={{0,4},{4,0},{8,12},{12,8},{16,20},{20,16},{24,28},{28,24},{1,5},{5... | collective-permute-start | bytes 393224 | tf_op jit(solution)/shard_map/ppermute | solution.py:486
  15.4 7.5 %collective-permute-start.7 = (f32[256,128]{1,0:T(8,128)S(1)}, f32[256,128]{1,0:T(8,128)S(1)}, u32[]{:S(2)}, u32[]{:S(2)}) collective-permute-start(f32[256,128]{1,0:T(8,128)S(1)} %get-tuple-element.64), channel_id=1, source_target_pairs={{0,8},{4,28},{8,0},{12,20},{16,24},{20,12},{24,16},{28,4},{1,9},{5... | collective-permute-start | bytes 393224 | tf_op jit(solution)/shard_map/ppermute | solution.py:473
  17.0 7.1 %collective-permute-start.8 = (f32[256,128]{1,0:T(8,128)S(1)}, f32[256,128]{1,0:T(8,128)S(1)}, u32[]{:S(2)}, u32[]{:S(2)}) collective-permute-start(f32[256,128]{1,0:T(8,128)S(1)} %get-tuple-element.67), channel_id=1, source_target_pairs={{0,16},{4,20},{8,24},{12,28},{16,0},{20,4},{24,8},{28,12},{1,17},{... | collective-permute-start | bytes 393224 | tf_op jit(solution)/shard_map/ppermute | solution.py:473
  18.5 6.2 %collective-permute-start.9 = (f32[256,128]{1,0:T(8,128)S(1)}, f32[256,128]{1,0:T(8,128)S(1)}, u32[]{:S(2)}, u32[]{:S(2)}) collective-permute-start(f32[256,128]{1,0:T(8,128)S(1)} %get-tuple-element.68), channel_id=1, source_target_pairs={{0,24},{4,12},{8,16},{12,4},{16,8},{20,28},{24,0},{28,20},{1,25},{... | collective-permute-start | bytes 393224 | tf_op jit(solution)/shard_map/ppermute | solution.py:473
  25.4 3.7 %collective-permute-start.10 = (f32[8,128]{1,0:T(8,128)S(1)}, f32[8,128]{1,0:T(8,128)S(1)}, u32[]{:S(2)}, u32[]{:S(2)}) collective-permute-start(f32[8,128]{1,0:T(8,128)S(1)} %get-tuple-element.72.left_ref), channel_id=1, source_target_pairs={{0,1},{1,0},{2,3},{3,2},{4,5},{5,4},{6,7},{7,6},{8,9},{9,8},{10,11... | collective-permute-start | bytes 12296 | tf_op jit(solution)/shard_map/ppermute | solution.py:508
  29.0 4.5 %collective-permute-start.11 = (f32[8,128]{1,0:T(8,128)S(1)}, f32[8,128]{1,0:T(8,128)S(1)}, u32[]{:S(2)}, u32[]{:S(2)}) collective-permute-start(f32[8,128]{1,0:T(8,128)S(1)} %add_sums.1.rest_2_), channel_id=1, source_target_pairs={{0,2},{1,3},{2,0},{3,1},{4,6},{5,7},{6,4},{7,5},{8,10},{9,11},{10,... | collective-permute-start | bytes 12296 | tf_op jit(solution)/shard_map/ppermute | solution.py:508
  34.7 6.8 %collective-permute-start.14 = (f32[256,128]{1,0:T(8,128)S(1)}, f32[256,128]{1,0:T(8,128)S(1)}, u32[]{:S(2)}, u32[]{:S(2)}) collective-permute-start(f32[256,128]{1,0:T(8,128)S(1)} %get-tuple-element.89), channel_id=1, source_target_pairs={{0,24},{4,12},{8,16},{12,4},{16,8},{20,28},{24,0},{28,20},{1,25},{... | collective-permute-start | bytes 393224 | tf_op jit(solution)/shard_map/ppermute | solution.py:473
  37.0 5.1 %collective-permute-start.13 = (f32[256,128]{1,0:T(8,128)S(1)}, f32[256,128]{1,0:T(8,128)S(1)}, u32[]{:S(2)}, u32[]{:S(2)}) collective-permute-start(f32[256,128]{1,0:T(8,128)S(1)} %get-tuple-element.88), channel_id=1, source_target_pairs={{0,16},{4,20},{8,24},{12,28},{16,0},{20,4},{24,8},{28,12},{1,17},{... | collective-permute-start | bytes 393224 | tf_op jit(solution)/shard_map/ppermute | solution.py:473
  37.8 5.0 %collective-permute-start.12 = (f32[256,128]{1,0:T(8,128)S(1)}, f32[256,128]{1,0:T(8,128)S(1)}, u32[]{:S(2)}, u32[]{:S(2)}) collective-permute-start(f32[256,128]{1,0:T(8,128)S(1)} %get-tuple-element.86), channel_id=1, source_target_pairs={{0,8},{4,28},{8,0},{12,20},{16,24},{20,12},{24,16},{28,4},{1,9},{5... | collective-permute-start | bytes 393224 | tf_op jit(solution)/shard_map/ppermute | solution.py:473
  38.2 4.5 %collective-permute-start.15 = (f32[256,128]{1,0:T(8,128)S(1)}, f32[256,128]{1,0:T(8,128)S(1)}, u32[]{:S(2)}, u32[]{:S(2)}) collective-permute-start(f32[256,128]{1,0:T(8,128)S(1)} %get-tuple-element.85.rest_0_), channel_id=1, source_target_pairs={{0,4},{4,0},{8,12},{12,8},{16,20},{20,16},{24,28},{28,24},{1,5},{5... | collective-permute-start | bytes 393224 | tf_op jit(solution)/shard_map/ppermute | solution.py:486
  41.4 1.6 %collective-permute-start.18 = (f32[256,128]{1,0:T(8,128)S(1)}, f32[256,128]{1,0:T(8,128)S(1)}, u32[]{:S(2)}, u32[]{:S(2)}) collective-permute-start(f32[256,128]{1,0:T(8,128)S(1)} %after.11.rest_3_), channel_id=1, source_target_pairs={{0,4},{4,0},{8,12},{12,8},{16,20},{20,16},{24,28},{28,24},{1,5},{5... | collective-permute-start | bytes 393224 | tf_op jit(solution)/shard_map/ppermute | solution.py:486
  42.0 1.3 %collective-permute-start.17 = (f32[256,128]{1,0:T(8,128)S(1)}, f32[256,128]{1,0:T(8,128)S(1)}, u32[]{:S(2)}, u32[]{:S(2)}) collective-permute-start(f32[256,128]{1,0:T(8,128)S(1)} %after.10.rest_2_), channel_id=1, source_target_pairs={{0,4},{4,0},{8,12},{12,8},{16,20},{20,16},{24,28},{28,24},{1,5},{5... | collective-permute-start | bytes 393224 | tf_op jit(solution)/shard_map/ppermute | solution.py:486
  42.7 1.3 %collective-permute-start.16 = (f32[256,128]{1,0:T(8,128)S(1)}, f32[256,128]{1,0:T(8,128)S(1)}, u32[]{:S(2)}, u32[]{:S(2)}) collective-permute-start(f32[256,128]{1,0:T(8,128)S(1)} %after.9.rest_1_), channel_id=1, source_target_pairs={{0,4},{4,0},{8,12},{12,8},{16,20},{20,16},{24,28},{28,24},{1,5},{5... | collective-permute-start | bytes 393224 | tf_op jit(solution)/shard_map/ppermute | solution.py:486
  44.4 7.6 %collective-permute-start.21 = (f32[256,128]{1,0:T(8,128)S(1)}, f32[256,128]{1,0:T(8,128)S(1)}, u32[]{:S(2)}, u32[]{:S(2)}) collective-permute-start(f32[256,128]{1,0:T(8,128)S(1)} %get-tuple-element.93), channel_id=1, source_target_pairs={{0,8},{4,28},{8,0},{12,20},{16,24},{20,12},{24,16},{28,4},{1,9},{5... | collective-permute-start | bytes 393224 | tf_op jit(solution)/shard_map/ppermute | solution.py:473
  45.6 7.7 %collective-permute-start.19 = (f32[256,128]{1,0:T(8,128)S(1)}, f32[256,128]{1,0:T(8,128)S(1)}, u32[]{:S(2)}, u32[]{:S(2)}) collective-permute-start(f32[256,128]{1,0:T(8,128)S(1)} %get-tuple-element.91), channel_id=1, source_target_pairs={{0,16},{4,20},{8,24},{12,28},{16,0},{20,4},{24,8},{28,12},{1,17},{... | collective-permute-start | bytes 393224 | tf_op jit(solution)/shard_map/ppermute | solution.py:473
  46.8 6.9 %collective-permute-start.20 = (f32[256,128]{1,0:T(8,128)S(1)}, f32[256,128]{1,0:T(8,128)S(1)}, u32[]{:S(2)}, u32[]{:S(2)}) collective-permute-start(f32[256,128]{1,0:T(8,128)S(1)} %get-tuple-element.92), channel_id=1, source_target_pairs={{0,24},{4,12},{8,16},{12,4},{16,8},{20,28},{24,0},{28,20},{1,25},{... | collective-permute-start | bytes 393224 | tf_op jit(solution)/shard_map/ppermute | solution.py:473

commit v5 on v3

--- a/solution.py
+++ b/solution.py
@@ -492,9 +492,9 @@
 
 
 def head_sums(sums, count):
-    step = 1
+    step = count // 2
     parts = [sums]
-    while step < count:
+    while step:
         if len(parts) == 2:
             parts = [
                 pl.pallas_call(
@@ -507,7 +507,7 @@
                 )(*parts)
             ]
         parts.append(lax.ppermute(parts[0], "head", [(at, at ^ step) for at in range(count)]))
-        step *= 2
+        step //= 2
     return parts
 
 

time: 55.4 us -> 55.4 us (level)
  no operation moved by 1% of the time
where the time goes in v5:
time: 55.4 us; the launch traced here: 55.2 us
  Pallas kernels  22.7 us (41%)
  starting transfers between devices  21.6 us (39%)
  waiting for transfers between devices  9.9 us (18%)
  between operations  1.04 us (2%)
    ppermute x12, starting transfers between devices, exchange(): moved.append(lax.ppermute(pieces[slot], 'seg', pairs))  15.2 us
    pallas_call x2, Pallas kernels, backward(): pl.pallas_call(functools.partial(backward_kernel, layout, groups, places,...  7.23 us
    ppermute x2, starting transfers between devices, head_sums(): lax.ppermute(parts[0], 'head', [(at, at ^ step) for at in range(count)])  4.23 us
    ppermute x2, waiting for transfers between devices, head_sums(): lax.ppermute(parts[0], 'head', [(at, at ^ step) for at in range(count)])  3.94 us
    pallas_call x1, Pallas kernels, local(): pl.pallas_call(functools.partial(weighted_kernel, layout, late), out_shap...  3.93 us
    ppermute x12, waiting for transfers between devices, exchange(): moved.append(lax.ppermute(pieces[slot], 'seg', pairs))  3.84 us
    pallas_call x1, Pallas kernels, local(): pl.pallas_call(functools.partial(local_kernel, layout, early), out_shape=...  3.47 us
    pallas_call x2, Pallas kernels, local(): pl.pallas_call(functools.partial(finish_kernel, layout, halves, places, l...  2.58 us
  transfers between devices with their start and end apart: 22, of which 10 were waited for; matrix products, arithmetic and copies ran while one was open for 0% of the time, Pallas kernels for 30%

profile of v5, /device:TPU:0, one launch (start us, length us, event | category | flops | bytes accessed | tf_op | source)
XLA Modules:
  0.0 55.2 jit_solution(7542289973267776585)
XLA Ops:
  0.6 0.0 copy-start.1
  0.6 0.0 copy-start.3
  0.7 0.0 copy-start.4
  0.7 0.0 copy-start.5
  0.7 1.6 %bring_near.1 = (bf16[512,1024]{1,0:T(8,128)(2,1)S(1)}, bf16[512,1024]{1,0:T(8,128)(2,1)S(1)}) custom-call(bf16[512,1024]{1,0:T(8,128)(2,1)} %key_any.1, bf16[512,1024]{1,0:T(8,128)(2,1)} %value_any.1, bf16[512,1024]{1,0:T(8,128)(2,1)} %query_ref.1), custom_call_target="tpu_custom_call" | custom-call | tf_op jit(solution)/shard_map/bring_near/pallas_call | solution.py:540
  2.3 0.0 copy-done.3
  2.3 1.0 %block_state.1 = (f32[256,128]{1,0:T(8,128)S(1)}, f32[256,128]{1,0:T(8,128)S(1)}, f32[256,128]{1,0:T(8,128)S(1)}, f32[256,128]{1,0:T(8,128)S(1)}) custom-call(s32[1,8]{1,0:T(1,128)S(1)} %bitcast.8, f32[1,8]{1,0:T(1,128)S(1)} %bitcast.9, bf16[512,1024]{1,0:T(8,128)(2,1)S(1)} %get-tuple-element.51.key_ref, bf16[512,1024]{1,0:T(8,128)(2,1)S(1)} %get-tuple-element.52.value_ref), custom_call_target="tpu_custom_call" | custom-call | tf_op jit(solution)/shard_map/block_state/pallas_call | solution.py:552
  3.4 3.0 %collective-permute-start = (f32[256,128]{1,0:T(8,128)S(1)}, f32[256,128]{1,0:T(8,128)S(1)}, u32[]{:S(2)}, u32[]{:S(2)}) collective-permute-start(f32[256,128]{1,0:T(8,128)S(1)} %get-tuple-element.60), channel_id=1, source_target_pairs={{0,8},{4,12},{8,0},{12,4},{16,24},{20,28},{24,16},{28,20},{1,9},{5... | collective-permute-start | bytes 393224 | tf_op jit(solution)/shard_map/ppermute | solution.py:474
  6.4 1.5 %collective-permute-start.1 = (f32[256,128]{1,0:T(8,128)S(1)}, f32[256,128]{1,0:T(8,128)S(1)}, u32[]{:S(2)}, u32[]{:S(2)}) collective-permute-start(f32[256,128]{1,0:T(8,128)S(1)} %get-tuple-element.61), channel_id=1, source_target_pairs={{0,16},{4,20},{8,24},{12,28},{16,0},{20,4},{24,8},{28,12},{1,17},{... | collective-permute-start | bytes 393224 | tf_op jit(solution)/shard_map/ppermute | solution.py:474
  7.9 0.0 collective-permute-start.2
  7.9 0.0 collective-permute-start.3
  7.9 3.5 %local_attention.1 = (f32[512,512]{1,0:T(8,128)S(1)}, bf16[512,1024]{1,0:T(8,128)(2,1)S(1)}, bf16[512,1024]{1,0:T(8,128)(2,1)S(1)}, f32[64,8,128]{2,1,0:T(8,128)S(1)}, f32[9,128]{1,0:T(8,128)S(1)}) custom-call(s32[8]{0:T(128)S(1)} %copy-done.3, s32[8]{0:T(128)S(1)} %copy-done.5, f32[8]{0:T(128)S(1)} %copy-done.4, bf16[512,1024]{1,0:T(8,128)(2,1)S(1)} %copy-done.1, ...), custom_call_target="tpu_custom_call" | custom-call | flops 536870912 | bytes 5242880 | tf_op jit(solution)/shard_map/local_attention/pallas_call | solution.py:562
  11.4 0.0 collective-permute-done.piece_ref
  11.4 0.0 copy-start
  11.4 0.0 copy-start.2
  11.4 0.6 %collective-permute-start.4 = (f32[256,128]{1,0:T(8,128)S(1)}, f32[256,128]{1,0:T(8,128)S(1)}, u32[]{:S(2)}, u32[]{:S(2)}) collective-permute-start(f32[256,128]{1,0:T(8,128)S(1)} %after.6.rest_1_), channel_id=1, source_target_pairs={{0,4},{4,0},{8,12},{12,8},{16,20},{20,16},{24,28},{28,24},{1,5},{5... | collective-permute-start | bytes 393224 | tf_op jit(solution)/shard_map/ppermute | solution.py:487
  12.0 2.1 %collective-permute-done.1.piece_ref = f32[256,128]{1,0:T(8,128)S(1)} collective-permute-done((f32[256,128]{1,0:T(8,128)S(1)}, f32[256,128]{1,0:T(8,128)S(1)}, u32[]{:S(2)}, u32[]{:S(2)}) %collective-permute-start.1) | collective-permute-done | bytes 131104 | tf_op jit(solution)/shard_map/ppermute | solution.py:474
  14.2 0.0 collective-permute-start.5
  14.2 0.0 collective-permute-done.2.piece_ref
  14.2 0.5 collective-permute-start.6
  14.7 0.0 collective-permute-done.3.rest_4_
  14.7 0.0 collective-permute-done.4.rest_5_
  14.7 0.8 %collective-permute-done.5.rest_6_ = f32[256,128]{1,0:T(8,128)S(1)} collective-permute-done((f32[256,128]{1,0:T(8,128)S(1)}, f32[256,128]{1,0:T(8,128)S(1)}, u32[]{:S(2)}, u32[]{:S(2)}) %collective-permute-start.5) | collective-permute-done | bytes 131104 | tf_op jit(solution)/shard_map/ppermute | solution.py:487
  15.5 0.2 collective-permute-done.6.rest_7_
  15.7 0.3 mix_forward.1
  16.0 1.1 %collective-permute-start.7 = (f32[256,128]{1,0:T(8,128)S(1)}, f32[256,128]{1,0:T(8,128)S(1)}, u32[]{:S(2)}, u32[]{:S(2)}) collective-permute-start(f32[256,128]{1,0:T(8,128)S(1)} %get-tuple-element.64), channel_id=1, source_target_pairs={{0,8},{4,12},{8,0},{12,4},{16,24},{20,28},{24,16},{28,20},{1,9},{5... | collective-permute-start | bytes 393224 | tf_op jit(solution)/shard_map/ppermute | solution.py:474
  17.1 1.0 %collective-permute-start.8 = (f32[256,128]{1,0:T(8,128)S(1)}, f32[256,128]{1,0:T(8,128)S(1)}, u32[]{:S(2)}, u32[]{:S(2)}) collective-permute-start(f32[256,128]{1,0:T(8,128)S(1)} %get-tuple-element.67), channel_id=1, source_target_pairs={{0,16},{4,20},{8,24},{12,28},{16,0},{20,4},{24,8},{28,12},{1,17},{... | collective-permute-start | bytes 393224 | tf_op jit(solution)/shard_map/ppermute | solution.py:474
  18.1 1.4 %collective-permute-start.9 = (f32[256,128]{1,0:T(8,128)S(1)}, f32[256,128]{1,0:T(8,128)S(1)}, u32[]{:S(2)}, u32[]{:S(2)}) collective-permute-start(f32[256,128]{1,0:T(8,128)S(1)} %get-tuple-element.68), channel_id=1, source_target_pairs={{0,24},{4,28},{8,16},{12,20},{16,8},{20,12},{24,0},{28,4},{1,25},{... | collective-permute-start | bytes 393224 | tf_op jit(solution)/shard_map/ppermute | solution.py:474
  19.5 3.9 %weighted_scores.1 = (bf16[8,3,256,256]{3,2,1,0:T(8,128)(2,1)S(1)}, f32[512,512]{1,0:T(8,128)S(1)}, bf16[512,1024]{1,0:T(8,128)(2,1)S(1)}, bf16[512,1024]{1,0:T(8,128)(2,1)S(1)}) custom-call(f32[9,128]{1,0:T(8,128)S(1)} %get-tuple-element.53.facts_ref, bf16[512,1024]{1,0:T(8,128)(2,1)S(1)} %get-tuple-element.54.query_ref, ...), custom_call_target="tpu_custom_call" | custom-call | flops 1073741824 | bytes 5242880 | tf_op jit(solution)/shard_map/weighted_scores/pallas_call | solution.py:580
  23.5 0.0 collective-permute-done.7.rest_1_.rest_3_
  23.5 0.5 attend.2
  24.0 0.0 collective-permute-done.8.rest_2_.rest_4_
  24.0 1.5 %collective-permute-done.9.rest_3_.rest_5_ = f32[256,128]{1,0:T(8,128)S(1)} collective-permute-done((f32[256,128]{1,0:T(8,128)S(1)}, f32[256,128]{1,0:T(8,128)S(1)}, u32[]{:S(2)}, u32[]{:S(2)}) %collective-permute-start.9) | collective-permute-done | bytes 131104 | tf_op jit(solution)/shard_map/ppermute | solution.py:474
  25.5 0.6 %attend.3 = (f32[512,512]{1,0:T(8,128)S(1)}, f32[8,128]{1,0:T(8,128)S(1)}) custom-call(bf16[512,1024]{1,0:T(8,128)(2,1)S(1)} %get-tuple-element.56.scaled_ref, bf16[512,1024]{1,0:T(8,128)(2,1)S(1)} %copy-done, f32[1,1024]{1,0:T(1,128)S(1)} %bitcast.4, f32[512,512]{1,0:T(8,128)S(1)} %get-tuple-element.66.local_ref, ...), custom_call_target="tpu_custom_call" | custom-call | flops 268435456 | bytes 5242880 | tf_op jit(solution)/shard_map/attend/pallas_call | solution.py:618
  26.1 2.7 %collective-permute-start.10 = (f32[8,128]{1,0:T(8,128)S(1)}, f32[8,128]{1,0:T(8,128)S(1)}, u32[]{:S(2)}, u32[]{:S(2)}) collective-permute-start(f32[8,128]{1,0:T(8,128)S(1)} %get-tuple-element.72.left_ref), channel_id=1, source_target_pairs={{0,2},{1,3},{2,0},{3,1},{4,6},{5,7},{6,4},{7,5},{8,10},{9,11},{10,... | collective-permute-start | bytes 12296 | tf_op jit(solution)/shard_map/ppermute | solution.py:509
  28.8 1.9 %collective-permute-done.10.right_ref = f32[8,128]{1,0:T(8,128)S(1)} collective-permute-done((f32[8,128]{1,0:T(8,128)S(1)}, f32[8,128]{1,0:T(8,128)S(1)}, u32[]{:S(2)}, u32[]{:S(2)}) %collective-permute-start.10) | collective-permute-done | bytes 4128 | tf_op jit(solution)/shard_map/ppermute | solution.py:509
  30.7 1.6 %collective-permute-start.11 = (f32[8,128]{1,0:T(8,128)S(1)}, f32[8,128]{1,0:T(8,128)S(1)}, u32[]{:S(2)}, u32[]{:S(2)}) collective-permute-start(f32[8,128]{1,0:T(8,128)S(1)} %add_sums.1.rest_2_), channel_id=1, source_target_pairs={{0,1},{1,0},{2,3},{3,2},{4,5},{5,4},{6,7},{7,6},{8,9},{9,8},{10,11... | collective-permute-start | bytes 12296 | tf_op jit(solution)/shard_map/ppermute | solution.py:509
  32.3 2.0 %collective-permute-done.11.rest_3_ = f32[8,128]{1,0:T(8,128)S(1)} collective-permute-done((f32[8,128]{1,0:T(8,128)S(1)}, f32[8,128]{1,0:T(8,128)S(1)}, u32[]{:S(2)}, u32[]{:S(2)}) %collective-permute-start.11) | collective-permute-done | bytes 4128 | tf_op jit(solution)/shard_map/ppermute | solution.py:509
  34.3 1.1 %state_grad.1 = (f32[256,128]{1,0:T(8,128)S(1)}, f32[256,128]{1,0:T(8,128)S(1)}, f32[256,128]{1,0:T(8,128)S(1)}, f32[256,128]{1,0:T(8,128)S(1)}, f32[512,128]{1,0:T(8,128)S(1)}, /*index=5*/f32[512,128]{1,0:T(8,128)S(1)}) custom-call(bf16[512,1024]{1,0:T(8,128)(2,1)S(1)} %get-tuple-element.56.scaled_ref, bf16[512,1024]{1,0:T(8,128)(2,1)S(1)} %copy-done, ...), custom_call_target="tpu_custom_call" | custom-call | tf_op jit(solution)/shard_map/state_grad/pallas_call | solution.py:633
  35.5 1.8 %collective-permute-start.14 = (f32[256,128]{1,0:T(8,128)S(1)}, f32[256,128]{1,0:T(8,128)S(1)}, u32[]{:S(2)}, u32[]{:S(2)}) collective-permute-start(f32[256,128]{1,0:T(8,128)S(1)} %get-tuple-element.89), channel_id=1, source_target_pairs={{0,24},{4,28},{8,16},{12,20},{16,8},{20,12},{24,0},{28,4},{1,25},{... | collective-permute-start | bytes 393224 | tf_op jit(solution)/shard_map/ppermute | solution.py:474
  37.3 0.5 collective-permute-start.13
  37.8 1.2 %collective-permute-start.12 = (f32[256,128]{1,0:T(8,128)S(1)}, f32[256,128]{1,0:T(8,128)S(1)}, u32[]{:S(2)}, u32[]{:S(2)}) collective-permute-start(f32[256,128]{1,0:T(8,128)S(1)} %get-tuple-element.86), channel_id=1, source_target_pairs={{0,8},{4,12},{8,0},{12,4},{16,24},{20,28},{24,16},{28,20},{1,9},{5... | collective-permute-start | bytes 393224 | tf_op jit(solution)/shard_map/ppermute | solution.py:474
  39.0 0.0 collective-permute-start.15
  39.0 3.2 %local_backward.2 = (bf16[512,512]{1,0:T(8,128)(2,1)S(1)}, bf16[512,512]{1,0:T(8,128)(2,1)S(1)}, bf16[512,512]{1,0:T(8,128)(2,1)S(1)}, bf16[512,512]{1,0:T(8,128)(2,1)S(1)}, f32[8,128]{1,0:T(8,128)S(1)}) custom-call(f32[9,128]{1,0:T(8,128)S(1)} %get-tuple-element.53.facts_ref, bf16[512,1024]{1,0:T(8,128)(2,1)S(1)} %get-tuple-element.54.query_ref, ...), custom_call_target="tpu_custom_call" | custom-call | flops 1073741824 | bytes 4194304 | tf_op jit(solution)/shard_map/local_backward/pallas_call | solution.py:655
  42.2 0.0 collective-permute-done.14.piece_ref
  42.2 0.6 %collective-permute-start.18 = (f32[256,128]{1,0:T(8,128)S(1)}, f32[256,128]{1,0:T(8,128)S(1)}, u32[]{:S(2)}, u32[]{:S(2)}) collective-permute-start(f32[256,128]{1,0:T(8,128)S(1)} %after.11.rest_3_), channel_id=1, source_target_pairs={{0,4},{4,0},{8,12},{12,8},{16,20},{20,16},{24,28},{28,24},{1,5},{5... | collective-permute-start | bytes 393224 | tf_op jit(solution)/shard_map/ppermute | solution.py:487
  42.8 0.0 collective-permute-done.13.piece_ref
  42.8 0.1 collective-permute-start.17
  42.9 0.0 collective-permute-done.12.piece_ref
  42.9 0.4 collective-permute-start.16
  43.3 0.0 collective-permute-done.15.rest_4_
  43.3 0.5 collective-permute-done.18.rest_7_
  43.8 0.4 collective-permute-done.17.rest_6_
  44.2 0.3 collective-permute-done.16.rest_5_
  44.4 0.3 mix_backward.1
  44.7 1.0 %collective-permute-start.21 = (f32[256,128]{1,0:T(8,128)S(1)}, f32[256,128]{1,0:T(8,128)S(1)}, u32[]{:S(2)}, u32[]{:S(2)}) collective-permute-start(f32[256,128]{1,0:T(8,128)S(1)} %get-tuple-element.93), channel_id=1, source_target_pairs={{0,8},{4,12},{8,0},{12,4},{16,24},{20,28},{24,16},{28,20},{1,9},{5... | collective-permute-start | bytes 393224 | tf_op jit(solution)/shard_map/ppermute | solution.py:474
  45.7 1.4 %collective-permute-start.19 = (f32[256,128]{1,0:T(8,128)S(1)}, f32[256,128]{1,0:T(8,128)S(1)}, u32[]{:S(2)}, u32[]{:S(2)}) collective-permute-start(f32[256,128]{1,0:T(8,128)S(1)} %get-tuple-element.91), channel_id=1, source_target_pairs={{0,16},{4,20},{8,24},{12,28},{16,0},{20,4},{24,8},{28,12},{1,17},{... | collective-permute-start | bytes 393224 | tf_op jit(solution)/shard_map/ppermute | solution.py:474
  47.1 1.2 %collective-permute-start.20 = (f32[256,128]{1,0:T(8,128)S(1)}, f32[256,128]{1,0:T(8,128)S(1)}, u32[]{:S(2)}, u32[]{:S(2)}) collective-permute-start(f32[256,128]{1,0:T(8,128)S(1)} %get-tuple-element.92), channel_id=1, source_target_pairs={{0,24},{4,28},{8,16},{12,20},{16,8},{20,12},{24,0},{28,4},{1,25},{... | collective-permute-start | bytes 393224 | tf_op jit(solution)/shard_map/ppermute | solution.py:474
  48.3 4.0 %local_backward.3 = (bf16[512,1024]{1,0:T(8,128)(2,1)}, bf16[512,1024]{1,0:T(8,128)(2,1)}, bf16[512,512]{1,0:T(8,128)(2,1)S(1)}, bf16[512,512]{1,0:T(8,128)(2,1)S(1)}) custom-call(f32[9,128]{1,0:T(8,128)S(1)} %get-tuple-element.53.facts_ref, bf16[512,1024]{1,0:T(8,128)(2,1)S(1)} %get-tuple-element.54.query_ref, ...), custom_call_target="tpu_custom_call" | custom-call | flops 1073741824 | bytes 4194304 | tf_op jit(solution)/shard_map/local_backward/pallas_call | solution.py:655
  52.3 0.0 collective-permute-done.21.rest_5_
  52.3 1.3 %finish.2 = (bf16[512,1024]{1,0:T(8,128)(2,1)}, bf16[512,1024]{1,0:T(8,128)(2,1)}) custom-call(bf16[512,1024]{1,0:T(8,128)(2,1)S(1)} %get-tuple-element.79.key_end_ref, bf16[512,1024]{1,0:T(8,128)(2,1)S(1)} %get-tuple-element.80.value_end_ref, bf16[512,512]{1,0:T(8,128)(2,1)S(1)} %get-tuple-element.81.rest_0_, ...), custom_call_target="tpu_custom_call" | custom-call | flops 268435456 | bytes 5242880 | tf_op jit(solution)/shard_map/finish/pallas_call | solution.py:679
  53.6 0.0 collective-permute-done.19.rest_6_
  53.6 0.1 collective-permute-done.20.rest_7_
  53.8 1.3 %finish.3 = (bf16[512,1024]{1,0:T(8,128)(2,1)}, bf16[512,1024]{1,0:T(8,128)(2,1)}) custom-call(bf16[512,1024]{1,0:T(8,128)(2,1)S(1)} %get-tuple-element.79.key_end_ref, bf16[512,1024]{1,0:T(8,128)(2,1)S(1)} %get-tuple-element.80.value_end_ref, bf16[512,512]{1,0:T(8,128)(2,1)S(1)} %get-tuple-element.81.rest_0_, ...), custom_call_target="tpu_custom_call", output_to_operand_aliasing={{0}: (10, {}), {1}: (11, {})} | custom-call | flops 268435456 | bytes 5242880 | tf_op jit(solution)/shard_map/finish/pallas_call | solution.py:679
  (12 shorter events, 0.0 us)
Async XLA Ops:
  0.6 7.3 %copy-start.1 = (bf16[512,1024]{1,0:T(8,128)(2,1)S(1)}, bf16[512,1024]{1,0:T(8,128)(2,1)}, u32[]{:S(2)}) copy-start(bf16[512,1024]{1,0:T(8,128)(2,1)} %query_ref.1) | copy-start | bytes 3145732
  0.6 1.7 %copy-start.3 = (s32[8]{0:T(128)S(1)}, s32[8]{0:T(128)}, u32[]{:S(2)}) copy-start(s32[8]{0:T(128)} %length_ref.1) | copy-start | bytes 100
  0.7 1.7 %copy-start.4 = (f32[8]{0:T(128)S(1)}, f32[8]{0:T(128)}, u32[]{:S(2)}) copy-start(f32[8]{0:T(128)} %rate_ref.1) | copy-start | bytes 100
  0.7 7.3 %copy-start.5 = (s32[8]{0:T(128)S(1)}, s32[8]{0:T(128)}, u32[]{:S(2)}) copy-start(s32[8]{0:T(128)} %parent_ref.1) | copy-start | bytes 100
  3.4 8.0 %collective-permute-start = (f32[256,128]{1,0:T(8,128)S(1)}, f32[256,128]{1,0:T(8,128)S(1)}, u32[]{:S(2)}, u32[]{:S(2)}) collective-permute-start(f32[256,128]{1,0:T(8,128)S(1)} %get-tuple-element.60), channel_id=1, source_target_pairs={{0,8},{4,12},{8,0},{12,4},{16,24},{20,28},{24,16},{28,20},{1,9},{5... | collective-permute-start | bytes 393224 | tf_op jit(solution)/shard_map/ppermute | solution.py:474
  6.4 7.8 %collective-permute-start.1 = (f32[256,128]{1,0:T(8,128)S(1)}, f32[256,128]{1,0:T(8,128)S(1)}, u32[]{:S(2)}, u32[]{:S(2)}) collective-permute-start(f32[256,128]{1,0:T(8,128)S(1)} %get-tuple-element.61), channel_id=1, source_target_pairs={{0,16},{4,20},{8,24},{12,28},{16,0},{20,4},{24,8},{28,12},{1,17},{... | collective-permute-start | bytes 393224 | tf_op jit(solution)/shard_map/ppermute | solution.py:474
  7.9 6.3 %collective-permute-start.2 = (f32[256,128]{1,0:T(8,128)S(1)}, f32[256,128]{1,0:T(8,128)S(1)}, u32[]{:S(2)}, u32[]{:S(2)}) collective-permute-start(f32[256,128]{1,0:T(8,128)S(1)} %get-tuple-element.62), channel_id=1, source_target_pairs={{0,24},{4,28},{8,16},{12,20},{16,8},{20,12},{24,0},{28,4},{1,25},{... | collective-permute-start | bytes 393224 | tf_op jit(solution)/shard_map/ppermute | solution.py:474
  7.9 6.8 %collective-permute-start.3 = (f32[256,128]{1,0:T(8,128)S(1)}, f32[256,128]{1,0:T(8,128)S(1)}, u32[]{:S(2)}, u32[]{:S(2)}) collective-permute-start(f32[256,128]{1,0:T(8,128)S(1)} %get-tuple-element.59.rest_0_), channel_id=1, source_target_pairs={{0,4},{4,0},{8,12},{12,8},{16,20},{20,16},{24,28},{28,24},{1,5},{5... | collective-permute-start | bytes 393224 | tf_op jit(solution)/shard_map/ppermute | solution.py:487
  11.4 12.1 %copy-start = (bf16[512,1024]{1,0:T(8,128)(2,1)S(1)}, bf16[512,1024]{1,0:T(8,128)(2,1)}, u32[]{:S(2)}) copy-start(bf16[512,1024]{1,0:T(8,128)(2,1)} %upstream_ref.9) | copy-start | bytes 3145732
  11.4 12.1 %copy-start.2 = (f32[1024]{0:T(1024)S(1)}, f32[1024]{0:T(1024)}, u32[]{:S(2)}) copy-start(f32[1024]{0:T(1024)} %param.12) | copy-start | bytes 12292
  11.4 3.2 %collective-permute-start.4 = (f32[256,128]{1,0:T(8,128)S(1)}, f32[256,128]{1,0:T(8,128)S(1)}, u32[]{:S(2)}, u32[]{:S(2)}) collective-permute-start(f32[256,128]{1,0:T(8,128)S(1)} %after.6.rest_1_), channel_id=1, source_target_pairs={{0,4},{4,0},{8,12},{12,8},{16,20},{20,16},{24,28},{28,24},{1,5},{5... | collective-permute-start | bytes 393224 | tf_op jit(solution)/shard_map/ppermute | solution.py:487
  14.2 1.3 %collective-permute-start.5 = (f32[256,128]{1,0:T(8,128)S(1)}, f32[256,128]{1,0:T(8,128)S(1)}, u32[]{:S(2)}, u32[]{:S(2)}) collective-permute-start(f32[256,128]{1,0:T(8,128)S(1)} %after.7.rest_2_), channel_id=1, source_target_pairs={{0,4},{4,0},{8,12},{12,8},{16,20},{20,16},{24,28},{28,24},{1,5},{5... | collective-permute-start | bytes 393224 | tf_op jit(solution)/shard_map/ppermute | solution.py:487
  14.2 1.5 %collective-permute-start.6 = (f32[256,128]{1,0:T(8,128)S(1)}, f32[256,128]{1,0:T(8,128)S(1)}, u32[]{:S(2)}, u32[]{:S(2)}) collective-permute-start(f32[256,128]{1,0:T(8,128)S(1)} %after.8.rest_3_), channel_id=1, source_target_pairs={{0,4},{4,0},{8,12},{12,8},{16,20},{20,16},{24,28},{28,24},{1,5},{5... | collective-permute-start | bytes 393224 | tf_op jit(solution)/shard_map/ppermute | solution.py:487
  16.0 7.5 %collective-permute-start.7 = (f32[256,128]{1,0:T(8,128)S(1)}, f32[256,128]{1,0:T(8,128)S(1)}, u32[]{:S(2)}, u32[]{:S(2)}) collective-permute-start(f32[256,128]{1,0:T(8,128)S(1)} %get-tuple-element.64), channel_id=1, source_target_pairs={{0,8},{4,12},{8,0},{12,4},{16,24},{20,28},{24,16},{28,20},{1,9},{5... | collective-permute-start | bytes 393224 | tf_op jit(solution)/shard_map/ppermute | solution.py:474
  17.1 6.9 %collective-permute-start.8 = (f32[256,128]{1,0:T(8,128)S(1)}, f32[256,128]{1,0:T(8,128)S(1)}, u32[]{:S(2)}, u32[]{:S(2)}) collective-permute-start(f32[256,128]{1,0:T(8,128)S(1)} %get-tuple-element.67), channel_id=1, source_target_pairs={{0,16},{4,20},{8,24},{12,28},{16,0},{20,4},{24,8},{28,12},{1,17},{... | collective-permute-start | bytes 393224 | tf_op jit(solution)/shard_map/ppermute | solution.py:474
  18.1 7.4 %collective-permute-start.9 = (f32[256,128]{1,0:T(8,128)S(1)}, f32[256,128]{1,0:T(8,128)S(1)}, u32[]{:S(2)}, u32[]{:S(2)}) collective-permute-start(f32[256,128]{1,0:T(8,128)S(1)} %get-tuple-element.68), channel_id=1, source_target_pairs={{0,24},{4,28},{8,16},{12,20},{16,8},{20,12},{24,0},{28,4},{1,25},{... | collective-permute-start | bytes 393224 | tf_op jit(solution)/shard_map/ppermute | solution.py:474
  26.1 4.6 %collective-permute-start.10 = (f32[8,128]{1,0:T(8,128)S(1)}, f32[8,128]{1,0:T(8,128)S(1)}, u32[]{:S(2)}, u32[]{:S(2)}) collective-permute-start(f32[8,128]{1,0:T(8,128)S(1)} %get-tuple-element.72.left_ref), channel_id=1, source_target_pairs={{0,2},{1,3},{2,0},{3,1},{4,6},{5,7},{6,4},{7,5},{8,10},{9,11},{10,... | collective-permute-start | bytes 12296 | tf_op jit(solution)/shard_map/ppermute | solution.py:509
  30.7 3.6 %collective-permute-start.11 = (f32[8,128]{1,0:T(8,128)S(1)}, f32[8,128]{1,0:T(8,128)S(1)}, u32[]{:S(2)}, u32[]{:S(2)}) collective-permute-start(f32[8,128]{1,0:T(8,128)S(1)} %add_sums.1.rest_2_), channel_id=1, source_target_pairs={{0,1},{1,0},{2,3},{3,2},{4,5},{5,4},{6,7},{7,6},{8,9},{9,8},{10,11... | collective-permute-start | bytes 12296 | tf_op jit(solution)/shard_map/ppermute | solution.py:509
  35.5 6.8 %collective-permute-start.14 = (f32[256,128]{1,0:T(8,128)S(1)}, f32[256,128]{1,0:T(8,128)S(1)}, u32[]{:S(2)}, u32[]{:S(2)}) collective-permute-start(f32[256,128]{1,0:T(8,128)S(1)} %get-tuple-element.89), channel_id=1, source_target_pairs={{0,24},{4,28},{8,16},{12,20},{16,8},{20,12},{24,0},{28,4},{1,25},{... | collective-permute-start | bytes 393224 | tf_op jit(solution)/shard_map/ppermute | solution.py:474
  37.3 5.5 %collective-permute-start.13 = (f32[256,128]{1,0:T(8,128)S(1)}, f32[256,128]{1,0:T(8,128)S(1)}, u32[]{:S(2)}, u32[]{:S(2)}) collective-permute-start(f32[256,128]{1,0:T(8,128)S(1)} %get-tuple-element.88), channel_id=1, source_target_pairs={{0,16},{4,20},{8,24},{12,28},{16,0},{20,4},{24,8},{28,12},{1,17},{... | collective-permute-start | bytes 393224 | tf_op jit(solution)/shard_map/ppermute | solution.py:474
  37.8 5.1 %collective-permute-start.12 = (f32[256,128]{1,0:T(8,128)S(1)}, f32[256,128]{1,0:T(8,128)S(1)}, u32[]{:S(2)}, u32[]{:S(2)}) collective-permute-start(f32[256,128]{1,0:T(8,128)S(1)} %get-tuple-element.86), channel_id=1, source_target_pairs={{0,8},{4,12},{8,0},{12,4},{16,24},{20,28},{24,16},{28,20},{1,9},{5... | collective-permute-start | bytes 393224 | tf_op jit(solution)/shard_map/ppermute | solution.py:474
  39.0 4.3 %collective-permute-start.15 = (f32[256,128]{1,0:T(8,128)S(1)}, f32[256,128]{1,0:T(8,128)S(1)}, u32[]{:S(2)}, u32[]{:S(2)}) collective-permute-start(f32[256,128]{1,0:T(8,128)S(1)} %get-tuple-element.85.rest_0_), channel_id=1, source_target_pairs={{0,4},{4,0},{8,12},{12,8},{16,20},{20,16},{24,28},{28,24},{1,5},{5... | collective-permute-start | bytes 393224 | tf_op jit(solution)/shard_map/ppermute | solution.py:487
  42.2 1.6 %collective-permute-start.18 = (f32[256,128]{1,0:T(8,128)S(1)}, f32[256,128]{1,0:T(8,128)S(1)}, u32[]{:S(2)}, u32[]{:S(2)}) collective-permute-start(f32[256,128]{1,0:T(8,128)S(1)} %after.11.rest_3_), channel_id=1, source_target_pairs={{0,4},{4,0},{8,12},{12,8},{16,20},{20,16},{24,28},{28,24},{1,5},{5... | collective-permute-start | bytes 393224 | tf_op jit(solution)/shard_map/ppermute | solution.py:487
  42.8 1.3 %collective-permute-start.17 = (f32[256,128]{1,0:T(8,128)S(1)}, f32[256,128]{1,0:T(8,128)S(1)}, u32[]{:S(2)}, u32[]{:S(2)}) collective-permute-start(f32[256,128]{1,0:T(8,128)S(1)} %after.10.rest_2_), channel_id=1, source_target_pairs={{0,4},{4,0},{8,12},{12,8},{16,20},{20,16},{24,28},{28,24},{1,5},{5... | collective-permute-start | bytes 393224 | tf_op jit(solution)/shard_map/ppermute | solution.py:487
  42.9 1.5 %collective-permute-start.16 = (f32[256,128]{1,0:T(8,128)S(1)}, f32[256,128]{1,0:T(8,128)S(1)}, u32[]{:S(2)}, u32[]{:S(2)}) collective-permute-start(f32[256,128]{1,0:T(8,128)S(1)} %after.9.rest_1_), channel_id=1, source_target_pairs={{0,4},{4,0},{8,12},{12,8},{16,20},{20,16},{24,28},{28,24},{1,5},{5... | collective-permute-start | bytes 393224 | tf_op jit(solution)/shard_map/ppermute | solution.py:487
  44.7 7.6 %collective-permute-start.21 = (f32[256,128]{1,0:T(8,128)S(1)}, f32[256,128]{1,0:T(8,128)S(1)}, u32[]{:S(2)}, u32[]{:S(2)}) collective-permute-start(f32[256,128]{1,0:T(8,128)S(1)} %get-tuple-element.93), channel_id=1, source_target_pairs={{0,8},{4,12},{8,0},{12,4},{16,24},{20,28},{24,16},{28,20},{1,9},{5... | collective-permute-start | bytes 393224 | tf_op jit(solution)/shard_map/ppermute | solution.py:474
  45.7 7.9 %collective-permute-start.19 = (f32[256,128]{1,0:T(8,128)S(1)}, f32[256,128]{1,0:T(8,128)S(1)}, u32[]{:S(2)}, u32[]{:S(2)}) collective-permute-start(f32[256,128]{1,0:T(8,128)S(1)} %get-tuple-element.91), channel_id=1, source_target_pairs={{0,16},{4,20},{8,24},{12,28},{16,0},{20,4},{24,8},{28,12},{1,17},{... | collective-permute-start | bytes 393224 | tf_op jit(solution)/shard_map/ppermute | solution.py:474
  47.1 6.7 %collective-permute-start.20 = (f32[256,128]{1,0:T(8,128)S(1)}, f32[256,128]{1,0:T(8,128)S(1)}, u32[]{:S(2)}, u32[]{:S(2)}) collective-permute-start(f32[256,128]{1,0:T(8,128)S(1)} %get-tuple-element.92), channel_id=1, source_target_pairs={{0,24},{4,28},{8,16},{12,20},{16,8},{20,12},{24,0},{28,4},{1,25},{... | collective-permute-start | bytes 393224 | tf_op jit(solution)/shard_map/ppermute | solution.py:474

commit v6 on v4

--- a/solution.py
+++ b/solution.py
@@ -491,9 +491,9 @@
 
 
 def head_sums(sums, count):
-    step = 1
+    step = count // 2
     parts = [sums]
-    while step < count:
+    while step:
         if len(parts) == 2:
             parts = [
                 pl.pallas_call(
@@ -506,7 +506,7 @@
                 )(*parts)
             ]
         parts.append(lax.ppermute(parts[0], "head", [(at, at ^ step) for at in range(count)]))
-        step *= 2
+        step //= 2
     return parts
 
 

time: 55.3 us -> 55.3 us (level)
  no operation moved by 1% of the time
where the time goes in v6:
time: 55.3 us; the launch traced here: 55.1 us
  Pallas kernels  22.7 us (41%)
  starting transfers between devices  21.4 us (39%)
  waiting for transfers between devices  10 us (18%)
  between operations  1.03 us (2%)
    ppermute x12, starting transfers between devices, exchange(): moved.append(lax.ppermute(pieces[slot], 'seg', pairs))  15.2 us
    pallas_call x2, Pallas kernels, backward(): pl.pallas_call(functools.partial(backward_kernel, layout, groups, places,...  7.22 us
    ppermute x2, starting transfers between devices, head_sums(): lax.ppermute(parts[0], 'head', [(at, at ^ step) for at in range(count)])  4.74 us
    pallas_call x1, Pallas kernels, local(): pl.pallas_call(functools.partial(weighted_kernel, layout, late), out_shap...  3.96 us
    ppermute x12, waiting for transfers between devices, exchange(): moved.append(lax.ppermute(pieces[slot], 'seg', pairs))  3.9 us
    pallas_call x1, Pallas kernels, local(): pl.pallas_call(functools.partial(local_kernel, layout, early), out_shape=...  3.48 us
    ppermute x2, waiting for transfers between devices, head_sums(): lax.ppermute(parts[0], 'head', [(at, at ^ step) for at in range(count)])  3.44 us
    ppermute x8, waiting for transfers between devices, swap_cores(): return [lax.ppermute(piece, 'seg', pairs) for piece in pieces]  2.68 us
  transfers between devices with their start and end apart: 22, of which 13 were waited for; matrix products, arithmetic and copies ran while one was open for 0% of the time, Pallas kernels for 30%

profile of v6, /device:TPU:0, one launch (start us, length us, event | category | flops | bytes accessed | tf_op | source)
XLA Modules:
  0.0 55.1 jit_solution(7443900763279141283)
XLA Ops:
  0.6 0.0 copy-start.1
  0.6 0.0 copy-start.3
  0.7 1.6 %bring_near.1 = (bf16[512,1024]{1,0:T(8,128)(2,1)S(1)}, bf16[512,1024]{1,0:T(8,128)(2,1)S(1)}) custom-call(bf16[512,1024]{1,0:T(8,128)(2,1)} %key_any.1, bf16[512,1024]{1,0:T(8,128)(2,1)} %value_any.1, bf16[512,1024]{1,0:T(8,128)(2,1)} %query_ref.1), custom_call_target="tpu_custom_call" | custom-call | tf_op jit(solution)/shard_map/bring_near/pallas_call | solution.py:538
  2.3 1.0 %block_state.1 = (f32[256,128]{1,0:T(8,128)S(1)}, f32[256,128]{1,0:T(8,128)S(1)}, f32[256,128]{1,0:T(8,128)S(1)}, f32[256,128]{1,0:T(8,128)S(1)}) custom-call(s32[1,8]{1,0:T(1,128)S(1)} %bitcast.8, f32[1,8]{1,0:T(1,128)S(1)} %bitcast.9, bf16[512,1024]{1,0:T(8,128)(2,1)S(1)} %get-tuple-element.51.key_ref, bf16[512,1024]{1,0:T(8,128)(2,1)S(1)} %get-tuple-element.52.value_ref), custom_call_target="tpu_custom_call" | custom-call | tf_op jit(solution)/shard_map/block_state/pallas_call | solution.py:550
  3.4 3.0 %collective-permute-start = (f32[256,128]{1,0:T(8,128)S(1)}, f32[256,128]{1,0:T(8,128)S(1)}, u32[]{:S(2)}, u32[]{:S(2)}) collective-permute-start(f32[256,128]{1,0:T(8,128)S(1)} %get-tuple-element.60), channel_id=1, source_target_pairs={{0,8},{4,28},{8,0},{12,20},{16,24},{20,12},{24,16},{28,4},{1,9},{5... | collective-permute-start | bytes 393224 | tf_op jit(solution)/shard_map/ppermute | solution.py:473
  6.4 1.5 %collective-permute-start.1 = (f32[256,128]{1,0:T(8,128)S(1)}, f32[256,128]{1,0:T(8,128)S(1)}, u32[]{:S(2)}, u32[]{:S(2)}) collective-permute-start(f32[256,128]{1,0:T(8,128)S(1)} %get-tuple-element.61), channel_id=1, source_target_pairs={{0,16},{4,20},{8,24},{12,28},{16,0},{20,4},{24,8},{28,12},{1,17},{... | collective-permute-start | bytes 393224 | tf_op jit(solution)/shard_map/ppermute | solution.py:473
  7.9 0.0 collective-permute-start.2
  7.9 0.0 collective-permute-start.3
  7.9 0.0 copy-done.5
  7.9 3.5 %local_attention.1 = (f32[512,512]{1,0:T(8,128)S(1)}, bf16[512,1024]{1,0:T(8,128)(2,1)S(1)}, bf16[512,1024]{1,0:T(8,128)(2,1)S(1)}, f32[64,8,128]{2,1,0:T(8,128)S(1)}, f32[9,128]{1,0:T(8,128)S(1)}) custom-call(s32[8]{0:T(128)S(1)} %copy-done.3, s32[8]{0:T(128)S(1)} %copy-done.5, f32[8]{0:T(128)S(1)} %copy-done.4, bf16[512,1024]{1,0:T(8,128)(2,1)S(1)} %copy-done.1, ...), custom_call_target="tpu_custom_call" | custom-call | flops 536870912 | bytes 5242880 | tf_op jit(solution)/shard_map/local_attention/pallas_call | solution.py:560
  11.4 0.0 collective-permute-done.piece_ref
  11.4 0.0 copy-start
  11.4 0.0 copy-start.2
  11.5 0.6 %collective-permute-start.4 = (f32[256,128]{1,0:T(8,128)S(1)}, f32[256,128]{1,0:T(8,128)S(1)}, u32[]{:S(2)}, u32[]{:S(2)}) collective-permute-start(f32[256,128]{1,0:T(8,128)S(1)} %after.6.rest_1_), channel_id=1, source_target_pairs={{0,4},{4,0},{8,12},{12,8},{16,20},{20,16},{24,28},{28,24},{1,5},{5... | collective-permute-start | bytes 393224 | tf_op jit(solution)/shard_map/ppermute | solution.py:486
  12.0 1.0 %collective-permute-done.1.piece_ref = f32[256,128]{1,0:T(8,128)S(1)} collective-permute-done((f32[256,128]{1,0:T(8,128)S(1)}, f32[256,128]{1,0:T(8,128)S(1)}, u32[]{:S(2)}, u32[]{:S(2)}) %collective-permute-start.1) | collective-permute-done | bytes 131104 | tf_op jit(solution)/shard_map/ppermute | solution.py:473
  13.0 0.0 collective-permute-start.5
  13.0 0.7 %collective-permute-done.2.piece_ref = f32[256,128]{1,0:T(8,128)S(1)} collective-permute-done((f32[256,128]{1,0:T(8,128)S(1)}, f32[256,128]{1,0:T(8,128)S(1)}, u32[]{:S(2)}, u32[]{:S(2)}) %collective-permute-start.2) | collective-permute-done | bytes 131104 | tf_op jit(solution)/shard_map/ppermute | solution.py:473
  13.8 0.0 collective-permute-start.6
  13.8 0.0 collective-permute-done.3.rest_4_
  13.8 0.0 collective-permute-done.4.rest_5_
  13.8 0.6 %collective-permute-done.5.rest_6_ = f32[256,128]{1,0:T(8,128)S(1)} collective-permute-done((f32[256,128]{1,0:T(8,128)S(1)}, f32[256,128]{1,0:T(8,128)S(1)}, u32[]{:S(2)}, u32[]{:S(2)}) %collective-permute-start.5) | collective-permute-done | bytes 131104 | tf_op jit(solution)/shard_map/ppermute | solution.py:486
  14.4 0.7 %collective-permute-done.6.rest_7_ = f32[256,128]{1,0:T(8,128)S(1)} collective-permute-done((f32[256,128]{1,0:T(8,128)S(1)}, f32[256,128]{1,0:T(8,128)S(1)}, u32[]{:S(2)}, u32[]{:S(2)}) %collective-permute-start.6) | collective-permute-done | bytes 131104 | tf_op jit(solution)/shard_map/ppermute | solution.py:486
  15.1 0.3 mix_forward.1
  15.4 1.6 %collective-permute-start.7 = (f32[256,128]{1,0:T(8,128)S(1)}, f32[256,128]{1,0:T(8,128)S(1)}, u32[]{:S(2)}, u32[]{:S(2)}) collective-permute-start(f32[256,128]{1,0:T(8,128)S(1)} %get-tuple-element.64), channel_id=1, source_target_pairs={{0,8},{4,28},{8,0},{12,20},{16,24},{20,12},{24,16},{28,4},{1,9},{5... | collective-permute-start | bytes 393224 | tf_op jit(solution)/shard_map/ppermute | solution.py:473
  17.0 1.5 %collective-permute-start.8 = (f32[256,128]{1,0:T(8,128)S(1)}, f32[256,128]{1,0:T(8,128)S(1)}, u32[]{:S(2)}, u32[]{:S(2)}) collective-permute-start(f32[256,128]{1,0:T(8,128)S(1)} %get-tuple-element.67), channel_id=1, source_target_pairs={{0,16},{4,20},{8,24},{12,28},{16,0},{20,4},{24,8},{28,12},{1,17},{... | collective-permute-start | bytes 393224 | tf_op jit(solution)/shard_map/ppermute | solution.py:473
  18.5 0.4 collective-permute-start.9
  19.0 4.0 %weighted_scores.1 = (bf16[8,3,256,256]{3,2,1,0:T(8,128)(2,1)S(1)}, f32[512,512]{1,0:T(8,128)S(1)}, bf16[512,1024]{1,0:T(8,128)(2,1)S(1)}, bf16[512,1024]{1,0:T(8,128)(2,1)S(1)}) custom-call(f32[9,128]{1,0:T(8,128)S(1)} %get-tuple-element.53.facts_ref, bf16[512,1024]{1,0:T(8,128)(2,1)S(1)} %get-tuple-element.54.query_ref, ...), custom_call_target="tpu_custom_call" | custom-call | flops 1073741824 | bytes 5242880 | tf_op jit(solution)/shard_map/weighted_scores/pallas_call | solution.py:578
  22.9 0.0 collective-permute-done.7.rest_1_.rest_3_
  22.9 0.0 copy-done
  23.0 0.0 copy-done.2
  23.0 0.5 attend.2
  23.4 0.7 %collective-permute-done.8.rest_2_.rest_4_ = f32[256,128]{1,0:T(8,128)S(1)} collective-permute-done((f32[256,128]{1,0:T(8,128)S(1)}, f32[256,128]{1,0:T(8,128)S(1)}, u32[]{:S(2)}, u32[]{:S(2)}) %collective-permute-start.8) | collective-permute-done | bytes 131104 | tf_op jit(solution)/shard_map/ppermute | solution.py:473
  24.1 0.6 %collective-permute-done.9.rest_3_.rest_5_ = f32[256,128]{1,0:T(8,128)S(1)} collective-permute-done((f32[256,128]{1,0:T(8,128)S(1)}, f32[256,128]{1,0:T(8,128)S(1)}, u32[]{:S(2)}, u32[]{:S(2)}) %collective-permute-start.9) | collective-permute-done | bytes 131104 | tf_op jit(solution)/shard_map/ppermute | solution.py:473
  24.8 0.6 %attend.3 = (f32[512,512]{1,0:T(8,128)S(1)}, f32[8,128]{1,0:T(8,128)S(1)}) custom-call(bf16[512,1024]{1,0:T(8,128)(2,1)S(1)} %get-tuple-element.56.scaled_ref, bf16[512,1024]{1,0:T(8,128)(2,1)S(1)} %copy-done, f32[1,1024]{1,0:T(1,128)S(1)} %bitcast.4, f32[512,512]{1,0:T(8,128)S(1)} %get-tuple-element.66.local_ref, ...), custom_call_target="tpu_custom_call" | custom-call | flops 268435456 | bytes 5242880 | tf_op jit(solution)/shard_map/attend/pallas_call | solution.py:616
  25.4 2.9 %collective-permute-start.10 = (f32[8,128]{1,0:T(8,128)S(1)}, f32[8,128]{1,0:T(8,128)S(1)}, u32[]{:S(2)}, u32[]{:S(2)}) collective-permute-start(f32[8,128]{1,0:T(8,128)S(1)} %get-tuple-element.72.left_ref), channel_id=1, source_target_pairs={{0,2},{1,3},{2,0},{3,1},{4,6},{5,7},{6,4},{7,5},{8,10},{9,11},{10,... | collective-permute-start | bytes 12296 | tf_op jit(solution)/shard_map/ppermute | solution.py:508
  28.3 1.7 %collective-permute-done.10.right_ref = f32[8,128]{1,0:T(8,128)S(1)} collective-permute-done((f32[8,128]{1,0:T(8,128)S(1)}, f32[8,128]{1,0:T(8,128)S(1)}, u32[]{:S(2)}, u32[]{:S(2)}) %collective-permute-start.10) | collective-permute-done | bytes 4128 | tf_op jit(solution)/shard_map/ppermute | solution.py:508
  29.9 1.8 %collective-permute-start.11 = (f32[8,128]{1,0:T(8,128)S(1)}, f32[8,128]{1,0:T(8,128)S(1)}, u32[]{:S(2)}, u32[]{:S(2)}) collective-permute-start(f32[8,128]{1,0:T(8,128)S(1)} %add_sums.1.rest_2_), channel_id=1, source_target_pairs={{0,1},{1,0},{2,3},{3,2},{4,5},{5,4},{6,7},{7,6},{8,9},{9,8},{10,11... | collective-permute-start | bytes 12296 | tf_op jit(solution)/shard_map/ppermute | solution.py:508
  31.8 1.8 %collective-permute-done.11.rest_3_ = f32[8,128]{1,0:T(8,128)S(1)} collective-permute-done((f32[8,128]{1,0:T(8,128)S(1)}, f32[8,128]{1,0:T(8,128)S(1)}, u32[]{:S(2)}, u32[]{:S(2)}) %collective-permute-start.11) | collective-permute-done | bytes 4128 | tf_op jit(solution)/shard_map/ppermute | solution.py:508
  33.5 1.1 %state_grad.1 = (f32[256,128]{1,0:T(8,128)S(1)}, f32[256,128]{1,0:T(8,128)S(1)}, f32[256,128]{1,0:T(8,128)S(1)}, f32[256,128]{1,0:T(8,128)S(1)}, f32[512,128]{1,0:T(8,128)S(1)}, /*index=5*/f32[512,128]{1,0:T(8,128)S(1)}) custom-call(bf16[512,1024]{1,0:T(8,128)(2,1)S(1)} %get-tuple-element.56.scaled_ref, bf16[512,1024]{1,0:T(8,128)(2,1)S(1)} %copy-done, ...), custom_call_target="tpu_custom_call" | custom-call | tf_op jit(solution)/shard_map/state_grad/pallas_call | solution.py:631
  34.7 2.3 %collective-permute-start.14 = (f32[256,128]{1,0:T(8,128)S(1)}, f32[256,128]{1,0:T(8,128)S(1)}, u32[]{:S(2)}, u32[]{:S(2)}) collective-permute-start(f32[256,128]{1,0:T(8,128)S(1)} %get-tuple-element.89), channel_id=1, source_target_pairs={{0,24},{4,12},{8,16},{12,4},{16,8},{20,28},{24,0},{28,20},{1,25},{... | collective-permute-start | bytes 393224 | tf_op jit(solution)/shard_map/ppermute | solution.py:473
  37.0 0.8 %collective-permute-start.13 = (f32[256,128]{1,0:T(8,128)S(1)}, f32[256,128]{1,0:T(8,128)S(1)}, u32[]{:S(2)}, u32[]{:S(2)}) collective-permute-start(f32[256,128]{1,0:T(8,128)S(1)} %get-tuple-element.88), channel_id=1, source_target_pairs={{0,16},{4,20},{8,24},{12,28},{16,0},{20,4},{24,8},{28,12},{1,17},{... | collective-permute-start | bytes 393224 | tf_op jit(solution)/shard_map/ppermute | solution.py:473
  37.8 0.5 collective-permute-start.12
  38.2 0.0 collective-permute-start.15
  38.2 3.2 %local_backward.2 = (bf16[512,512]{1,0:T(8,128)(2,1)S(1)}, bf16[512,512]{1,0:T(8,128)(2,1)S(1)}, bf16[512,512]{1,0:T(8,128)(2,1)S(1)}, bf16[512,512]{1,0:T(8,128)(2,1)S(1)}, f32[8,128]{1,0:T(8,128)S(1)}) custom-call(f32[9,128]{1,0:T(8,128)S(1)} %get-tuple-element.53.facts_ref, bf16[512,1024]{1,0:T(8,128)(2,1)S(1)} %get-tuple-element.54.query_ref, ...), custom_call_target="tpu_custom_call" | custom-call | flops 1073741824 | bytes 4194304 | tf_op jit(solution)/shard_map/local_backward/pallas_call | solution.py:653
  41.4 0.0 collective-permute-done.14.piece_ref
  41.4 0.6 %collective-permute-start.18 = (f32[256,128]{1,0:T(8,128)S(1)}, f32[256,128]{1,0:T(8,128)S(1)}, u32[]{:S(2)}, u32[]{:S(2)}) collective-permute-start(f32[256,128]{1,0:T(8,128)S(1)} %after.11.rest_3_), channel_id=1, source_target_pairs={{0,4},{4,0},{8,12},{12,8},{16,20},{20,16},{24,28},{28,24},{1,5},{5... | collective-permute-start | bytes 393224 | tf_op jit(solution)/shard_map/ppermute | solution.py:486
  42.0 0.0 collective-permute-done.13.piece_ref
  42.0 0.3 collective-permute-start.17
  42.3 0.4 collective-permute-done.12.piece_ref
  42.7 0.0 collective-permute-start.16
  42.7 0.0 collective-permute-done.15.rest_4_
  42.7 0.3 collective-permute-done.18.rest_7_
  43.0 0.4 collective-permute-done.17.rest_6_
  43.4 0.7 %collective-permute-done.16.rest_5_ = f32[256,128]{1,0:T(8,128)S(1)} collective-permute-done((f32[256,128]{1,0:T(8,128)S(1)}, f32[256,128]{1,0:T(8,128)S(1)}, u32[]{:S(2)}, u32[]{:S(2)}) %collective-permute-start.16) | collective-permute-done | bytes 131104 | tf_op jit(solution)/shard_map/ppermute | solution.py:486
  44.1 0.3 mix_backward.1
  44.4 1.2 %collective-permute-start.21 = (f32[256,128]{1,0:T(8,128)S(1)}, f32[256,128]{1,0:T(8,128)S(1)}, u32[]{:S(2)}, u32[]{:S(2)}) collective-permute-start(f32[256,128]{1,0:T(8,128)S(1)} %get-tuple-element.93), channel_id=1, source_target_pairs={{0,8},{4,28},{8,0},{12,20},{16,24},{20,12},{24,16},{28,4},{1,9},{5... | collective-permute-start | bytes 393224 | tf_op jit(solution)/shard_map/ppermute | solution.py:473
  45.6 1.2 %collective-permute-start.19 = (f32[256,128]{1,0:T(8,128)S(1)}, f32[256,128]{1,0:T(8,128)S(1)}, u32[]{:S(2)}, u32[]{:S(2)}) collective-permute-start(f32[256,128]{1,0:T(8,128)S(1)} %get-tuple-element.91), channel_id=1, source_target_pairs={{0,16},{4,20},{8,24},{12,28},{16,0},{20,4},{24,8},{28,12},{1,17},{... | collective-permute-start | bytes 393224 | tf_op jit(solution)/shard_map/ppermute | solution.py:473
  46.8 1.1 %collective-permute-start.20 = (f32[256,128]{1,0:T(8,128)S(1)}, f32[256,128]{1,0:T(8,128)S(1)}, u32[]{:S(2)}, u32[]{:S(2)}) collective-permute-start(f32[256,128]{1,0:T(8,128)S(1)} %get-tuple-element.92), channel_id=1, source_target_pairs={{0,24},{4,12},{8,16},{12,4},{16,8},{20,28},{24,0},{28,20},{1,25},{... | collective-permute-start | bytes 393224 | tf_op jit(solution)/shard_map/ppermute | solution.py:473
  47.9 4.0 %local_backward.3 = (bf16[512,1024]{1,0:T(8,128)(2,1)}, bf16[512,1024]{1,0:T(8,128)(2,1)}, bf16[512,512]{1,0:T(8,128)(2,1)S(1)}, bf16[512,512]{1,0:T(8,128)(2,1)S(1)}) custom-call(f32[9,128]{1,0:T(8,128)S(1)} %get-tuple-element.53.facts_ref, bf16[512,1024]{1,0:T(8,128)(2,1)S(1)} %get-tuple-element.54.query_ref, ...), custom_call_target="tpu_custom_call" | custom-call | flops 1073741824 | bytes 4194304 | tf_op jit(solution)/shard_map/local_backward/pallas_call | solution.py:653
  52.0 0.0 collective-permute-done.21.rest_5_
  52.0 1.3 %finish.2 = (bf16[512,1024]{1,0:T(8,128)(2,1)}, bf16[512,1024]{1,0:T(8,128)(2,1)}) custom-call(bf16[512,1024]{1,0:T(8,128)(2,1)S(1)} %get-tuple-element.79.key_end_ref, bf16[512,1024]{1,0:T(8,128)(2,1)S(1)} %get-tuple-element.80.value_end_ref, bf16[512,512]{1,0:T(8,128)(2,1)S(1)} %get-tuple-element.81.rest_0_, ...), custom_call_target="tpu_custom_call" | custom-call | flops 268435456 | bytes 5242880 | tf_op jit(solution)/shard_map/finish/pallas_call | solution.py:677
  53.3 0.0 collective-permute-done.19.rest_6_
  53.3 0.4 collective-permute-done.20.rest_7_
  53.7 1.3 %finish.3 = (bf16[512,1024]{1,0:T(8,128)(2,1)}, bf16[512,1024]{1,0:T(8,128)(2,1)}) custom-call(bf16[512,1024]{1,0:T(8,128)(2,1)S(1)} %get-tuple-element.79.key_end_ref, bf16[512,1024]{1,0:T(8,128)(2,1)S(1)} %get-tuple-element.80.value_end_ref, bf16[512,512]{1,0:T(8,128)(2,1)S(1)} %get-tuple-element.81.rest_0_, ...), custom_call_target="tpu_custom_call", output_to_operand_aliasing={{0}: (10, {}), {1}: (11, {})} | custom-call | flops 268435456 | bytes 5242880 | tf_op jit(solution)/shard_map/finish/pallas_call | solution.py:677
  (12 shorter events, 0.0 us)
Async XLA Ops:
  0.6 7.3 %copy-start.1 = (bf16[512,1024]{1,0:T(8,128)(2,1)S(1)}, bf16[512,1024]{1,0:T(8,128)(2,1)}, u32[]{:S(2)}) copy-start(bf16[512,1024]{1,0:T(8,128)(2,1)} %query_ref.1) | copy-start | bytes 3145732
  0.6 1.7 %copy-start.3 = (s32[8]{0:T(128)S(1)}, s32[8]{0:T(128)}, u32[]{:S(2)}) copy-start(s32[8]{0:T(128)} %length_ref.1) | copy-start | bytes 100
  0.7 1.7 %copy-start.4 = (f32[8]{0:T(128)S(1)}, f32[8]{0:T(128)}, u32[]{:S(2)}) copy-start(f32[8]{0:T(128)} %rate_ref.1) | copy-start | bytes 100
  0.7 7.3 %copy-start.5 = (s32[8]{0:T(128)S(1)}, s32[8]{0:T(128)}, u32[]{:S(2)}) copy-start(s32[8]{0:T(128)} %parent_ref.1) | copy-start | bytes 100
  3.4 8.0 %collective-permute-start = (f32[256,128]{1,0:T(8,128)S(1)}, f32[256,128]{1,0:T(8,128)S(1)}, u32[]{:S(2)}, u32[]{:S(2)}) collective-permute-start(f32[256,128]{1,0:T(8,128)S(1)} %get-tuple-element.60), channel_id=1, source_target_pairs={{0,8},{4,28},{8,0},{12,20},{16,24},{20,12},{24,16},{28,4},{1,9},{5... | collective-permute-start | bytes 393224 | tf_op jit(solution)/shard_map/ppermute | solution.py:473
  6.4 6.6 %collective-permute-start.1 = (f32[256,128]{1,0:T(8,128)S(1)}, f32[256,128]{1,0:T(8,128)S(1)}, u32[]{:S(2)}, u32[]{:S(2)}) collective-permute-start(f32[256,128]{1,0:T(8,128)S(1)} %get-tuple-element.61), channel_id=1, source_target_pairs={{0,16},{4,20},{8,24},{12,28},{16,0},{20,4},{24,8},{28,12},{1,17},{... | collective-permute-start | bytes 393224 | tf_op jit(solution)/shard_map/ppermute | solution.py:473
  7.9 5.9 %collective-permute-start.2 = (f32[256,128]{1,0:T(8,128)S(1)}, f32[256,128]{1,0:T(8,128)S(1)}, u32[]{:S(2)}, u32[]{:S(2)}) collective-permute-start(f32[256,128]{1,0:T(8,128)S(1)} %get-tuple-element.62), channel_id=1, source_target_pairs={{0,24},{4,12},{8,16},{12,4},{16,8},{20,28},{24,0},{28,20},{1,25},{... | collective-permute-start | bytes 393224 | tf_op jit(solution)/shard_map/ppermute | solution.py:473
  7.9 5.9 %collective-permute-start.3 = (f32[256,128]{1,0:T(8,128)S(1)}, f32[256,128]{1,0:T(8,128)S(1)}, u32[]{:S(2)}, u32[]{:S(2)}) collective-permute-start(f32[256,128]{1,0:T(8,128)S(1)} %get-tuple-element.59.rest_0_), channel_id=1, source_target_pairs={{0,4},{4,0},{8,12},{12,8},{16,20},{20,16},{24,28},{28,24},{1,5},{5... | collective-permute-start | bytes 393224 | tf_op jit(solution)/shard_map/ppermute | solution.py:486
  11.4 11.5 %copy-start = (bf16[512,1024]{1,0:T(8,128)(2,1)S(1)}, bf16[512,1024]{1,0:T(8,128)(2,1)}, u32[]{:S(2)}) copy-start(bf16[512,1024]{1,0:T(8,128)(2,1)} %upstream_ref.9) | copy-start | bytes 3145732
  11.4 11.5 %copy-start.2 = (f32[1024]{0:T(1024)S(1)}, f32[1024]{0:T(1024)}, u32[]{:S(2)}) copy-start(f32[1024]{0:T(1024)} %param.12) | copy-start | bytes 12292
  11.5 2.3 %collective-permute-start.4 = (f32[256,128]{1,0:T(8,128)S(1)}, f32[256,128]{1,0:T(8,128)S(1)}, u32[]{:S(2)}, u32[]{:S(2)}) collective-permute-start(f32[256,128]{1,0:T(8,128)S(1)} %after.6.rest_1_), channel_id=1, source_target_pairs={{0,4},{4,0},{8,12},{12,8},{16,20},{20,16},{24,28},{28,24},{1,5},{5... | collective-permute-start | bytes 393224 | tf_op jit(solution)/shard_map/ppermute | solution.py:486
  13.0 1.3 %collective-permute-start.5 = (f32[256,128]{1,0:T(8,128)S(1)}, f32[256,128]{1,0:T(8,128)S(1)}, u32[]{:S(2)}, u32[]{:S(2)}) collective-permute-start(f32[256,128]{1,0:T(8,128)S(1)} %after.7.rest_2_), channel_id=1, source_target_pairs={{0,4},{4,0},{8,12},{12,8},{16,20},{20,16},{24,28},{28,24},{1,5},{5... | collective-permute-start | bytes 393224 | tf_op jit(solution)/shard_map/ppermute | solution.py:486
  13.8 1.3 %collective-permute-start.6 = (f32[256,128]{1,0:T(8,128)S(1)}, f32[256,128]{1,0:T(8,128)S(1)}, u32[]{:S(2)}, u32[]{:S(2)}) collective-permute-start(f32[256,128]{1,0:T(8,128)S(1)} %after.8.rest_3_), channel_id=1, source_target_pairs={{0,4},{4,0},{8,12},{12,8},{16,20},{20,16},{24,28},{28,24},{1,5},{5... | collective-permute-start | bytes 393224 | tf_op jit(solution)/shard_map/ppermute | solution.py:486
  15.4 7.5 %collective-permute-start.7 = (f32[256,128]{1,0:T(8,128)S(1)}, f32[256,128]{1,0:T(8,128)S(1)}, u32[]{:S(2)}, u32[]{:S(2)}) collective-permute-start(f32[256,128]{1,0:T(8,128)S(1)} %get-tuple-element.64), channel_id=1, source_target_pairs={{0,8},{4,28},{8,0},{12,20},{16,24},{20,12},{24,16},{28,4},{1,9},{5... | collective-permute-start | bytes 393224 | tf_op jit(solution)/shard_map/ppermute | solution.py:473
  17.0 7.1 %collective-permute-start.8 = (f32[256,128]{1,0:T(8,128)S(1)}, f32[256,128]{1,0:T(8,128)S(1)}, u32[]{:S(2)}, u32[]{:S(2)}) collective-permute-start(f32[256,128]{1,0:T(8,128)S(1)} %get-tuple-element.67), channel_id=1, source_target_pairs={{0,16},{4,20},{8,24},{12,28},{16,0},{20,4},{24,8},{28,12},{1,17},{... | collective-permute-start | bytes 393224 | tf_op jit(solution)/shard_map/ppermute | solution.py:473
  18.5 6.2 %collective-permute-start.9 = (f32[256,128]{1,0:T(8,128)S(1)}, f32[256,128]{1,0:T(8,128)S(1)}, u32[]{:S(2)}, u32[]{:S(2)}) collective-permute-start(f32[256,128]{1,0:T(8,128)S(1)} %get-tuple-element.68), channel_id=1, source_target_pairs={{0,24},{4,12},{8,16},{12,4},{16,8},{20,28},{24,0},{28,20},{1,25},{... | collective-permute-start | bytes 393224 | tf_op jit(solution)/shard_map/ppermute | solution.py:473
  25.4 4.6 %collective-permute-start.10 = (f32[8,128]{1,0:T(8,128)S(1)}, f32[8,128]{1,0:T(8,128)S(1)}, u32[]{:S(2)}, u32[]{:S(2)}) collective-permute-start(f32[8,128]{1,0:T(8,128)S(1)} %get-tuple-element.72.left_ref), channel_id=1, source_target_pairs={{0,2},{1,3},{2,0},{3,1},{4,6},{5,7},{6,4},{7,5},{8,10},{9,11},{10,... | collective-permute-start | bytes 12296 | tf_op jit(solution)/shard_map/ppermute | solution.py:508
  29.9 3.6 %collective-permute-start.11 = (f32[8,128]{1,0:T(8,128)S(1)}, f32[8,128]{1,0:T(8,128)S(1)}, u32[]{:S(2)}, u32[]{:S(2)}) collective-permute-start(f32[8,128]{1,0:T(8,128)S(1)} %add_sums.1.rest_2_), channel_id=1, source_target_pairs={{0,1},{1,0},{2,3},{3,2},{4,5},{5,4},{6,7},{7,6},{8,9},{9,8},{10,11... | collective-permute-start | bytes 12296 | tf_op jit(solution)/shard_map/ppermute | solution.py:508
  34.7 6.8 %collective-permute-start.14 = (f32[256,128]{1,0:T(8,128)S(1)}, f32[256,128]{1,0:T(8,128)S(1)}, u32[]{:S(2)}, u32[]{:S(2)}) collective-permute-start(f32[256,128]{1,0:T(8,128)S(1)} %get-tuple-element.89), channel_id=1, source_target_pairs={{0,24},{4,12},{8,16},{12,4},{16,8},{20,28},{24,0},{28,20},{1,25},{... | collective-permute-start | bytes 393224 | tf_op jit(solution)/shard_map/ppermute | solution.py:473
  37.0 5.1 %collective-permute-start.13 = (f32[256,128]{1,0:T(8,128)S(1)}, f32[256,128]{1,0:T(8,128)S(1)}, u32[]{:S(2)}, u32[]{:S(2)}) collective-permute-start(f32[256,128]{1,0:T(8,128)S(1)} %get-tuple-element.88), channel_id=1, source_target_pairs={{0,16},{4,20},{8,24},{12,28},{16,0},{20,4},{24,8},{28,12},{1,17},{... | collective-permute-start | bytes 393224 | tf_op jit(solution)/shard_map/ppermute | solution.py:473
  37.8 5.0 %collective-permute-start.12 = (f32[256,128]{1,0:T(8,128)S(1)}, f32[256,128]{1,0:T(8,128)S(1)}, u32[]{:S(2)}, u32[]{:S(2)}) collective-permute-start(f32[256,128]{1,0:T(8,128)S(1)} %get-tuple-element.86), channel_id=1, source_target_pairs={{0,8},{4,28},{8,0},{12,20},{16,24},{20,12},{24,16},{28,4},{1,9},{5... | collective-permute-start | bytes 393224 | tf_op jit(solution)/shard_map/ppermute | solution.py:473
  38.2 4.5 %collective-permute-start.15 = (f32[256,128]{1,0:T(8,128)S(1)}, f32[256,128]{1,0:T(8,128)S(1)}, u32[]{:S(2)}, u32[]{:S(2)}) collective-permute-start(f32[256,128]{1,0:T(8,128)S(1)} %get-tuple-element.85.rest_0_), channel_id=1, source_target_pairs={{0,4},{4,0},{8,12},{12,8},{16,20},{20,16},{24,28},{28,24},{1,5},{5... | collective-permute-start | bytes 393224 | tf_op jit(solution)/shard_map/ppermute | solution.py:486
  41.4 1.6 %collective-permute-start.18 = (f32[256,128]{1,0:T(8,128)S(1)}, f32[256,128]{1,0:T(8,128)S(1)}, u32[]{:S(2)}, u32[]{:S(2)}) collective-permute-start(f32[256,128]{1,0:T(8,128)S(1)} %after.11.rest_3_), channel_id=1, source_target_pairs={{0,4},{4,0},{8,12},{12,8},{16,20},{20,16},{24,28},{28,24},{1,5},{5... | collective-permute-start | bytes 393224 | tf_op jit(solution)/shard_map/ppermute | solution.py:486
  42.0 1.3 %collective-permute-start.17 = (f32[256,128]{1,0:T(8,128)S(1)}, f32[256,128]{1,0:T(8,128)S(1)}, u32[]{:S(2)}, u32[]{:S(2)}) collective-permute-start(f32[256,128]{1,0:T(8,128)S(1)} %after.10.rest_2_), channel_id=1, source_target_pairs={{0,4},{4,0},{8,12},{12,8},{16,20},{20,16},{24,28},{28,24},{1,5},{5... | collective-permute-start | bytes 393224 | tf_op jit(solution)/shard_map/ppermute | solution.py:486
  42.7 1.3 %collective-permute-start.16 = (f32[256,128]{1,0:T(8,128)S(1)}, f32[256,128]{1,0:T(8,128)S(1)}, u32[]{:S(2)}, u32[]{:S(2)}) collective-permute-start(f32[256,128]{1,0:T(8,128)S(1)} %after.9.rest_1_), channel_id=1, source_target_pairs={{0,4},{4,0},{8,12},{12,8},{16,20},{20,16},{24,28},{28,24},{1,5},{5... | collective-permute-start | bytes 393224 | tf_op jit(solution)/shard_map/ppermute | solution.py:486
  44.4 7.6 %collective-permute-start.21 = (f32[256,128]{1,0:T(8,128)S(1)}, f32[256,128]{1,0:T(8,128)S(1)}, u32[]{:S(2)}, u32[]{:S(2)}) collective-permute-start(f32[256,128]{1,0:T(8,128)S(1)} %get-tuple-element.93), channel_id=1, source_target_pairs={{0,8},{4,28},{8,0},{12,20},{16,24},{20,12},{24,16},{28,4},{1,9},{5... | collective-permute-start | bytes 393224 | tf_op jit(solution)/shard_map/ppermute | solution.py:473
  45.6 7.7 %collective-permute-start.19 = (f32[256,128]{1,0:T(8,128)S(1)}, f32[256,128]{1,0:T(8,128)S(1)}, u32[]{:S(2)}, u32[]{:S(2)}) collective-permute-start(f32[256,128]{1,0:T(8,128)S(1)} %get-tuple-element.91), channel_id=1, source_target_pairs={{0,16},{4,20},{8,24},{12,28},{16,0},{20,4},{24,8},{28,12},{1,17},{... | collective-permute-start | bytes 393224 | tf_op jit(solution)/shard_map/ppermute | solution.py:473
  46.8 6.9 %collective-permute-start.20 = (f32[256,128]{1,0:T(8,128)S(1)}, f32[256,128]{1,0:T(8,128)S(1)}, u32[]{:S(2)}, u32[]{:S(2)}) collective-permute-start(f32[256,128]{1,0:T(8,128)S(1)} %get-tuple-element.92), channel_id=1, source_target_pairs={{0,24},{4,12},{8,16},{12,4},{16,8},{20,28},{24,0},{28,20},{1,25},{... | collective-permute-start | bytes 393224 | tf_op jit(solution)/shard_map/ppermute | solution.py:473
